TPU v7x, 256 devices: a whole 4x4x8 slice. The times are simulated.
256 devices in a mesh: grp: 8 (over x, core), shard: 32 (over z, y).
Axes of the slice: x: 4, y: 4, z: 8, core: 2. Of those that a mesh axis runs over, the one named last changes fastest.
Arguments:
- queries: bfloat16 [32768, 768], P(('grp', 'shard')), may hold values from -6 to 6
- positives: bfloat16 [32768, 768], P(('grp', 'shard')), may hold values from -6 to 6
- negative_ids: int32 [32768, 16], P(('grp', 'shard')), may hold values from 0 to 131071, as said below
- passage_table: bfloat16 [131072, 768], P('shard'), may hold values from -6 to 6
- inner_weight: bfloat16 [768, 2048], P('shard'), may hold values from -0.21875 to 0.21875
- outer_weight: bfloat16 [2048, 768], P('shard'), may hold values from -0.125 to 0.125
Outputs:
- loss_values: float32 [32768], P(('grp', 'shard'))
- inner_grad: float32 [768, 2048], P('shard')
- outer_grad: float32 [2048, 768], P('shard')
Inputs may be any that keep to these rules, and one draw needn't show every extreme that they name: `negative_ids`: the owner of a row id is id // 4096. The 2048 ids of one block of 128 consecutive queries name at most 128 rows of one owner; one owner gets exactly 128 from every block. Owners 2 j and 2 j + 1 form a pair, and each block names exactly 128 rows of each pair. Rows may repeat.
All inputs are finite; a program needn't handle non-finite values.
Results may differ from a plain program's by a relative error of at most 0.025.
Values may be sent and summed in bfloat16 or wider, within the bound.
No kernel may reach another device: no remote copies, remote signals or barrier semaphores. Data moves between devices by JAX's collectives and lax.ppermute only.
A program may use at most 128 MiB of HBM per device.

v0:
```python
import functools

import jax
import jax.numpy as jnp
from jax import lax
from jax.experimental import pallas as pl
from jax.experimental.pallas import tpu as pltpu
from jax.sharding import Mesh, PartitionSpec as P

X, CORE, Z, Y = 4, 2, 8, 4
GRP, SHARD = X * CORE, Z * Y
PAIRS = SHARD // 2
CHUNKS = 4
VMEM = 50 * 1024 * 1024


def gelu_value(pre_act):
    return pre_act * 0.5 * (1.0 + lax.erf(pre_act * 0.7071067811865476))


def gelu_slope(pre_act):
    return (
        0.5 * (1.0 + lax.erf(pre_act * 0.7071067811865476))
        + pre_act * jnp.exp(-0.5 * pre_act * pre_act) * 0.3989422804014327
    )


def contract_first(left, right):
    return lax.dot_general(
        left, right, (((0,), (0,)), ((), ())), preferred_element_type=jnp.float32
    )


def contract_last(left, right):
    return lax.dot_general(
        left, right, (((1,), (1,)), ((), ())), preferred_element_type=jnp.float32
    )


def exchange(value, axes):
    return lax.all_to_all(value, axes, split_axis=0, concat_axis=0, tiled=True)


def spread(value, axes, count):
    return exchange(jnp.broadcast_to(value[None], (count, *value.shape)), axes)


def swap(value, axis, by):
    return lax.ppermute(value, axis, [(i, i ^ by) for i in range(lax.axis_size(axis))])


def after(value, *done):
    return lax.optimization_barrier((value, *done))[0]


def request_kernel(shift, ids_ref, code_ref, query_ref):
    ids = ids_ref[...]
    q_dev, neg = ids.shape
    lane = lax.broadcasted_iota(jnp.int32, (q_dev, q_dev), 1)
    query = lax.broadcasted_iota(jnp.int32, (q_dev, q_dev), 0)
    before = (lane < query).astype(jnp.float32).astype(jnp.bfloat16)
    kind, pair_lane = lane // PAIRS, lane % PAIRS
    seen = jnp.zeros((1, q_dev), jnp.float32)
    placed = jnp.zeros((q_dev, q_dev), jnp.float32)
    for k in range(neg):
        id_k = ids[:, k : k + 1]
        owner = id_k >> shift
        odd = owner & 1
        member = owner == lane
        ones = member.astype(jnp.float32)
        counts = seen + jnp.dot(before, ones.astype(jnp.bfloat16), preferred_element_type=jnp.float32)
        rank = jnp.sum(jnp.where(member, counts, 0.0), axis=1, keepdims=True).astype(jnp.int32)
        seen = seen + jnp.sum(ones, axis=0, keepdims=True)
        slot = jnp.where(odd == 1, q_dev - 1 - rank, rank)
        at_slot = (slot == lane).astype(jnp.float32).astype(jnp.bfloat16)
        code = (odd << shift) + (id_k - (owner << shift))
        item = jnp.where(
            kind == 0, code >> 6, jnp.where(kind == 1, code & 63, jnp.where(kind == 2, query, 0))
        )
        item = jnp.where((owner >> 1) == pair_lane, item, 0)
        placed = placed + contract_first(item.astype(jnp.float32).astype(jnp.bfloat16), at_slot)
    code_ref[...] = (placed[:PAIRS] * 64.0 + placed[PAIRS : 2 * PAIRS]).astype(jnp.int32)
    query_ref[...] = placed[2 * PAIRS : 3 * PAIRS].astype(jnp.int32)


def score_kernel(scale, place_ref, embedded_ref, positives_ref, hidden_ref, query_ref, *refs):
    row_refs, (loss_ref, grad_ref, keep_ref, send_ref) = refs[:CHUNKS], refs[CHUNKS:]
    embedded = embedded_ref[...]
    positives = positives_ref[...].astype(jnp.float32)
    q_dev, width = embedded.shape
    pos_scores = (
        jnp.sum(embedded.astype(jnp.float32) * positives, axis=1, keepdims=True) * scale
    )
    total = jnp.exp(pos_scores)
    per = row_refs[0].shape[0]
    query = lax.broadcasted_iota(jnp.int32, (q_dev, per), 0)
    scores, members = [], []
    for c in range(CHUNKS):
        score = contract_last(embedded, row_refs[c][...]) * scale
        member = query_ref[:, c * per : (c + 1) * per] == query
        total = total + jnp.sum(jnp.where(member, jnp.exp(score), 0.0), axis=1, keepdims=True)
        scores.append(score)
        members.append(member)
    log_total = jnp.log(total)
    loss_ref[...] = log_total - pos_scores
    grad = (jnp.exp(pos_scores - log_total) - 1.0) * positives
    for c in range(CHUNKS):
        weight = jnp.where(members[c], jnp.exp(scores[c] - log_total), 0.0)
        high = weight.astype(jnp.bfloat16)
        low = (weight - high.astype(jnp.float32)).astype(jnp.bfloat16)
        rows = row_refs[c][...]
        grad = grad + jnp.dot(high, rows, preferred_element_type=jnp.float32)
        grad = grad + jnp.dot(low, rows, preferred_element_type=jnp.float32)
    query_grad = (grad * scale).astype(jnp.bfloat16)
    grad_ref[...] = query_grad
    my_core = place_ref[1]
    hid = hidden_ref.shape[1]
    deep, part, half = hid // SHARD // X, hid // Z, width // CORE
    for z in range(Z):
        outer = contract_first(hidden_ref[:, z * part : (z + 1) * part], query_grad)
        left, right = outer[:, :half], outer[:, half:]
        keep = jnp.where(my_core == 0, left, right).astype(jnp.bfloat16)
        send = jnp.where(my_core == 0, right, left).astype(jnp.bfloat16)
        for y in range(Y):
            for x in range(X):
                rows = slice((y * X + x) * deep, (y * X + x + 1) * deep)
                keep_ref[y, x, z * deep : (z + 1) * deep, :] = keep[rows]
                send_ref[y, x, z * deep : (z + 1) * deep, :] = send[rows]


def inner_kernel(place_ref, queries_ref, grad_ref, slope_ref, weight_ref, keep_ref, send_ref):
    queries, query_grad = queries_ref[...], grad_ref[...]
    part = weight_ref.shape[0] // GRP
    for by_core, out_ref in ((1, send_ref), (0, keep_ref)):
        for by_x in range(X):
            group = (place_ref[0] ^ by_x) * CORE + (place_ref[1] ^ by_core)
            at = pl.ds(pl.multiple_of(group * part, part), part)
            hidden_grad = contract_last(query_grad, weight_ref[at, :])
            pre_grad = (hidden_grad * slope_ref[:, at]).astype(jnp.bfloat16)
            out_ref[by_x] = contract_first(queries, pre_grad).astype(jnp.bfloat16)


def total_of(parts):
    return sum(part.astype(jnp.float32) for part in parts)


def columns_to_rows(value, wide):
    return jnp.concatenate(
        [value[..., i : i + wide] for i in range(0, value.shape[-1], wide)], axis=-2
    )


def rows_to_columns(value, deep):
    return jnp.concatenate(
        [value[..., i : i + deep, :] for i in range(0, value.shape[-2], deep)], axis=-1
    )


def shards(queries, positives, negative_ids, passage_table, inner_weight, outer_weight):
    q_dev, width = queries.shape
    rows_dev = passage_table.shape[0]
    shift = rows_dev.bit_length() - 1
    hid = inner_weight.shape[1]
    inner_rows, outer_rows = inner_weight.shape[0], outer_weight.shape[0]
    scale = float(width) ** (-0.5)
    limits = {"compiler_params": pltpu.CompilerParams(vmem_limit_bytes=VMEM)}
    my_x, my_core, my_y = (lax.axis_index(axis) for axis in ("x", "core", "y"))
    group = my_x * CORE + my_core
    place = jnp.stack([my_x, my_core]).astype(jnp.int32)
    in_smem = pl.BlockSpec(memory_space=pltpu.SMEM)
    in_vmem = pl.BlockSpec(memory_space=pltpu.VMEM)

    slots = jax.ShapeDtypeStruct((PAIRS, q_dev), jnp.int32)
    code, slot_query = pl.pallas_call(
        functools.partial(request_kernel, shift), out_shape=[slots] * 2, **limits
    )(negative_ids)
    code = exchange(
        jnp.broadcast_to(code[:, None], (PAIRS, 2, q_dev)).reshape(SHARD, q_dev), ("z", "y")
    ).reshape(Z, Y, q_dev)
    code = jnp.stack([lax.dynamic_index_in_dim(code, my_y ^ by, 1, False) for by in range(Y)])
    own = (code >> shift) == my_y % 2
    wanted = code & (rows_dev - 1)
    wanted = lax.optimization_barrier((wanted[:, :, : q_dev // 2], wanted[:, :, q_dev // 2 :]))
    per = q_dev // 2
    cuts = slice(0, per), slice(per, q_dev)

    def find(picks, *done):
        ids = jnp.stack([wanted[part][by] for by, part in picks])
        ids = after(ids.reshape(-1), *done)
        found = passage_table.at[ids].get(mode="promise_in_bounds").reshape(-1, Z * per, width)
        return [
            jnp.where(own[by, :, cuts[part]].reshape(-1, 1), found[i], jnp.zeros((), found.dtype))
            for i, (by, part) in enumerate(picks)
        ]

    wide, deep = hid // GRP, outer_rows // GRP
    inner_piece = lax.dynamic_slice(inner_weight, (0, group * wide), (inner_rows, wide))
    outer_piece = lax.dynamic_slice(outer_weight, (group * deep, 0), (deep, width))
    piece = jnp.concatenate([rows_to_columns(inner_piece, deep), outer_piece], axis=0)

    (found_10,) = find([(1, 0)])
    near_10 = swap(found_10, "y", 1)
    gathered = spread(after(piece, found_10), ("z", "y"), SHARD)
    found_00, found_11 = find([(0, 0), (1, 1)], found_10)
    near_11 = swap(found_11, "y", 1)
    own_0 = after(found_00 + near_10, gathered)
    rows_0 = exchange(own_0, "z")
    gathered = after(gathered, own_0)
    parts = [gathered] + [swap(gathered, "x", by) for by in range(1, X)]
    found_30, found_01, found_20 = find([(3, 0), (0, 1), (2, 0)], own_0)
    near_30, near_20 = swap(found_30, "y", 3), swap(found_20, "y", 2)
    found_31, found_21 = find([(3, 1), (2, 1)], found_30)
    near_31, near_21 = swap(found_31, "y", 3), swap(found_21, "y", 2)
    rows_1 = exchange(after(found_01 + near_11, rows_0, near_30, found_31, parts[1], parts[3]), "z")
    other_0 = near_20 + near_30
    rows_2 = exchange(after(other_0, rows_1, near_31), "z")
    other_1 = near_21 + near_31
    rows_3 = exchange(after(other_1, rows_2), "z")
    chunks = [rows_0, rows_1, rows_2, rows_3]
    parts = after(tuple(parts), rows_1, other_0, near_31)
    gathered = jnp.zeros((X, *gathered.shape), gathered.dtype)
    for by in range(X):
        gathered = lax.dynamic_update_index_in_dim(gathered, parts[by], my_x ^ by, 0)
    twin = swap(gathered, "core", 1)
    gathered, twin = after((gathered, twin), other_1)
    slot_query = slot_query.reshape(Z, 2, q_dev)
    slot_query = jnp.where(my_y // 2 == 0, slot_query, slot_query[:, ::-1])
    slot_query = jnp.concatenate(
        [slot_query[:, pair, cut].reshape(1, -1) for pair in range(2) for cut in cuts], axis=1
    )

    halves = jnp.stack(
        [jnp.where(my_core == 0, gathered, twin), jnp.where(my_core == 0, twin, gathered)], axis=1
    )
    inner_full = [
        columns_to_rows(halves[g // CORE, g % CORE, :, :deep], wide).reshape(width, wide)
        for g in range(GRP)
    ]
    outer_full = halves[:, :, :, deep:].transpose(2, 0, 1, 3, 4).reshape(hid, width)

    pre_act = jnp.concatenate(
        [jnp.dot(queries, part, preferred_element_type=jnp.float32) for part in inner_full], axis=1
    )
    hidden = gelu_value(pre_act).astype(jnp.bfloat16)
    slope = gelu_slope(pre_act)
    projected = jnp.dot(hidden, outer_full, preferred_element_type=jnp.float32)
    embedded = (queries.astype(jnp.float32) + projected).astype(jnp.bfloat16)

    half = width // CORE
    outer_cut = jax.ShapeDtypeStruct((Y, X, hid // Y // X, half), jnp.bfloat16)
    losses, query_grad, outer, outer_sent = pl.pallas_call(
        functools.partial(score_kernel, scale),
        out_shape=[
            jax.ShapeDtypeStruct((q_dev, 1), jnp.float32),
            jax.ShapeDtypeStruct((q_dev, width), jnp.bfloat16),
            outer_cut,
            outer_cut,
        ],
        in_specs=[in_smem] + [in_vmem] * (4 + CHUNKS),
        **limits,
    )(place, embedded, positives, hidden, slot_query, *chunks)
    outer_sent = swap(outer_sent, "core", 1)
    inner, inner_sent = pl.pallas_call(
        inner_kernel,
        out_shape=[jax.ShapeDtypeStruct((X, width, wide), jnp.bfloat16)] * 2,
        in_specs=[in_smem] + [in_vmem] * 4,
        **limits,
    )(place, queries, query_grad, slope, outer_full)
    inner_sent = swap(inner_sent, "core", 1)

    narrow = lambda value: value.astype(jnp.bfloat16)
    outer = exchange(narrow(total_of([outer, outer_sent])), "y")
    inner = [narrow(total_of([inner[by], inner_sent[by]])) for by in range(X)]
    inner = inner[:1] + [swap(inner[by], "x", by) for by in range(1, X)]
    outer = narrow(total_of(list(outer)))
    inner = after(tuple(inner), outer)
    outer = exchange(outer, "x")
    inner = narrow(total_of(inner)).reshape(Z, Y, inner_rows, wide)
    inner = [lax.dynamic_index_in_dim(inner, my_y ^ by, 1, False) for by in range(Y)]
    inner = inner[:1] + [swap(inner[by], "y", by) for by in range(1, Y)]
    lanes = 128
    both = jnp.concatenate(
        [
            columns_to_rows(total_of(inner), lanes),
            columns_to_rows(total_of(list(outer)).reshape(Z, -1, half), lanes),
        ],
        axis=1,
    )
    both = total_of(list(exchange(narrow(both), "z")))
    both = spread(both, ("x", "core"), GRP)
    inner_deep = inner_rows * wide // lanes
    inner = rows_to_columns(both[:, :inner_deep], inner_rows)
    outer = rows_to_columns(both[:, inner_deep:], outer_rows // X)
    inner = jnp.concatenate(list(inner), axis=1)
    outer = jnp.concatenate(
        [jnp.concatenate([outer[x * CORE + c] for c in range(CORE)], axis=1) for x in range(X)],
        axis=0,
    )
    return (losses.reshape(-1), inner, outer)


def solution(mesh):
    fine = Mesh(mesh.devices.reshape(X, CORE, Z, Y), ("x", "core", "z", "y"))
    blocks, rows = ("x", "core", "z", "y"), ("z", "y")
    return jax.shard_map(
        shards,
        mesh=fine,
        in_specs=(
            P(blocks, None),
            P(blocks, None),
            P(blocks, None),
            P(rows, None),
            P(rows, None),
            P(rows, None),
        ),
        out_specs=(P(blocks), P(rows, None), P(rows, None)),
        check_vma=False,
    )
```

profile of v0, /device:TPU:1, one launch (start us, length us, event | category | flops | bytes accessed | tf_op | source)
XLA Modules:
  0.0 296.4 jit_solution(16984636609511661650)
XLA Ops:
  1.5 5.8 %shard_map.85 = (s32[16,128]{1,0:T(8,128)S(1)}, s32[16,128]{1,0:T(8,128)S(1)}) custom-call(s32[128,16]{1,0:T(8,128)S(1)} %copy.39.ids_ref), custom_call_target="tpu_custom_call" | custom-call | tf_op jit(solution)/shard_map/pallas_call | solution.py:174
  7.9 12.0 %all-to-all-start = ((s32[32,1,128]{2,1,0:T(1,128)}), s32[32,1,128]{2,1,0:T(1,128)S(1)}, u32[]{:S(2)}, u32[]{:S(2)}) async-start(s32[32,1,128]{2,1,0:T(1,128)} %bitcast.2), calls=%async_computation | async-start | bytes 32768 | tf_op jit(solution)/shard_map/all_to_all | solution.py:41
  20.8 7.7 %all-to-all-done = s32[32,1,128]{2,1,0:T(1,128)S(1)} async-done(((s32[32,1,128]{2,1,0:T(1,128)}), s32[32,1,128]{2,1,0:T(1,128)S(1)}, u32[]{:S(2)}, u32[]{:S(2)}) %all-to-all-start) | async-done | bytes 16416 | tf_op jit(solution)/shard_map/all_to_all | solution.py:41
  28.9 6.0 %gather_fusion = bf16[512,768]{1,0:T(8,128)(2,1)S(1)} fusion(bf16[4096,768]{1,0:T(8,128)(2,1)} %param.9, s32[1024]{0:T(1024)S(1)} %pad_clamp_fusion.1), kind=kCustom, calls=%fused_computation | custom fusion | bytes 1574912 | tf_op jit(solution)/shard_map/gather | solution.py:190
  36.4 3.9 %all-to-all-start.1 = ((bf16[32,16,768]{2,1,0:T(8,128)(2,1)}), bf16[32,16,768]{2,1,0:T(8,128)(2,1)S(1)}, u32[]{:S(2)}, u32[]{:S(2)}) async-start(bf16[32,16,768]{2,1,0:T(8,128)(2,1)} %broadcast_in_dim.124), calls=%async_computation.1 | async-start | bytes 1572864 | tf_op jit(solution)/shard_map/all_to_all | solution.py:41
  40.6 8.1 %gather_fusion.1 = bf16[1024,768]{1,0:T(8,128)(2,1)S(1)} fusion(bf16[4096,768]{1,0:T(8,128)(2,1)} %param.9, s32[1024]{0:T(1024)S(1)} %fusion.41), kind=kCustom, calls=%fused_computation.1 | custom fusion | bytes 3149824 | tf_op jit(solution)/shard_map/gather | solution.py:190
  48.6 9.4 %collective-permute-done = bf16[512,768]{1,0:T(8,128)(2,1)} collective-permute-done((bf16[512,768]{1,0:T(8,128)(2,1)S(1)}, bf16[512,768]{1,0:T(8,128)(2,1)}, u32[]{:S(2)}, u32[]{:S(2)}) %collective-permute-start) | collective-permute-done | bytes 786464 | tf_op jit(solution)/shard_map/ppermute | solution.py:49
  58.1 2.5 slice_select_fusion.4
  61.1 2.5 collective-permute-start.3
  63.6 3.7 %all-to-all-start.2 = ((bf16[8,64,768]{2,1,0:T(8,128)(2,1)}), bf16[8,64,768]{2,1,0:T(8,128)(2,1)S(1)}, u32[]{:S(2)}, u32[]{:S(2)}) async-start(bf16[8,64,768]{2,1,0:T(8,128)(2,1)} %bitcast.8), calls=%async_computation.2 | async-start | bytes 1572864 | tf_op jit(solution)/shard_map/all_to_all | solution.py:41
  67.4 10.3 %gather_fusion.2 = bf16[1536,768]{1,0:T(8,128)(2,1)} fusion(bf16[4096,768]{1,0:T(8,128)(2,1)} %param.9, s32[2048]{0:T(1024)S(1)} %pad_clamp_fusion), kind=kCustom, calls=%fused_computation.2 | custom fusion | bytes 4724736 | tf_op jit(solution)/shard_map/gather | solution.py:190
  77.7 2.8 slice_select_fusion.1
  80.5 1.5 collective-permute-start.5
  82.2 9.1 %gather_fusion.3 = bf16[1024,768]{1,0:T(8,128)(2,1)} fusion(bf16[4096,768]{1,0:T(8,128)(2,1)} %param.9, s32[1024]{0:T(1024)S(1)} %fusion.42), kind=kCustom, calls=%fused_computation.3 | custom fusion | bytes 3149824 | tf_op jit(solution)/shard_map/gather | solution.py:190
  91.4 2.7 slice_select_fusion
  95.9 6.1 %all-to-all-start.3 = ((bf16[8,64,768]{2,1,0:T(8,128)(2,1)}), bf16[8,64,768]{2,1,0:T(8,128)(2,1)S(1)}, u32[]{:S(2)}, u32[]{:S(2)}) async-start(bf16[8,64,768]{2,1,0:T(8,128)(2,1)} %bitcast.10), calls=%async_computation.3 | async-start | bytes 1572864 | tf_op jit(solution)/shard_map/all_to_all | solution.py:41
  103.2 1.3 collective-permute-start.2
  104.5 1.5 collective-permute-start.7
  106.0 9.3 %collective-permute-done.6 = bf16[512,768]{1,0:T(8,128)(2,1)} collective-permute-done((bf16[512,768]{1,0:T(8,128)(2,1)S(1)}, bf16[512,768]{1,0:T(8,128)(2,1)}, u32[]{:S(2)}, u32[]{:S(2)}) %collective-permute-start.6) | collective-permute-done | bytes 786464 | tf_op jit(solution)/shard_map/ppermute | solution.py:49
  115.3 2.5 add.197
  117.8 22.1 %collective-permute-done.7 = bf16[512,768]{1,0:T(8,128)(2,1)} collective-permute-done((bf16[512,768]{1,0:T(8,128)(2,1)}, bf16[512,768]{1,0:T(8,128)(2,1)}, u32[]{:S(2)}, u32[]{:S(2)}) %collective-permute-start.7) | collective-permute-done | bytes 786464 | tf_op jit(solution)/shard_map/ppermute | solution.py:49
  139.9 2.0 broadcast_in_dim.118
  142.9 2.2 bitcast_dynamic-update-slice_fusion.1
  145.1 2.2 bitcast_dynamic-update-slice_fusion
  147.3 2.1 bitcast_dynamic-update-slice_fusion.3
  149.9 6.6 %all-to-all-start.4 = ((bf16[8,64,768]{2,1,0:T(8,128)(2,1)}), bf16[8,64,768]{2,1,0:T(8,128)(2,1)S(1)}, u32[]{:S(2)}, u32[]{:S(2)}) async-start(bf16[8,64,768]{2,1,0:T(8,128)(2,1)} %bitcast.49), calls=%async_computation.4 | async-start | bytes 1572864 | tf_op jit(solution)/shard_map/all_to_all | solution.py:41
  156.5 1.3 collective-permute-start.9
  158.3 18.8 %collective-permute-done.9 = bf16[512,768]{1,0:T(8,128)(2,1)} collective-permute-done((bf16[512,768]{1,0:T(8,128)(2,1)S(1)}, bf16[512,768]{1,0:T(8,128)(2,1)}, u32[]{:S(2)}, u32[]{:S(2)}) %collective-permute-start.9) | collective-permute-done | bytes 786464 | tf_op jit(solution)/shard_map/ppermute | solution.py:49
  177.1 2.4 add.202
  180.2 5.6 %all-to-all-start.5 = ((bf16[8,64,768]{2,1,0:T(8,128)(2,1)}), bf16[8,64,768]{2,1,0:T(8,128)(2,1)}, u32[]{:S(2)}, u32[]{:S(2)}) async-start(bf16[8,64,768]{2,1,0:T(8,128)(2,1)} %bitcast.51), calls=%async_computation.5 | async-start | bytes 1572864 | tf_op jit(solution)/shard_map/all_to_all | solution.py:41
  185.8 3.2 %fusion = (bf16[4,1,32,16,768]{4,3,1,0,2:T(8,128)(2,1)S(1)}, bf16[4,1,32,16,768]{4,3,1,0,2:T(8,128)(2,1)S(1)}, bf16[4,1,32,16,768]{4,3,0,2,1:T(8,128)(2,1)S(1)}) fusion(bf16[4,32,16,768]{3,2,0,1:T(8,128)(2,1)} %bitcast_dynamic-update-slice_fusion.3, bf16[4,32,16,768]{3,2,0,1:T(8,128)(2,1)} %collective-permute-done.8, pred[]{:T(512)S(6)} %eq.15), kind=kLoop, calls=%fused_computation.10 | loop fusion | flops 3145728 | bytes 15728641 | tf_op jit(solution)/shard_map/stack | solution.py:232
  193.7 14.6 %all-to-all-done.5 = bf16[8,64,768]{2,1,0:T(8,128)(2,1)} async-done(((bf16[8,64,768]{2,1,0:T(8,128)(2,1)}), bf16[8,64,768]{2,1,0:T(8,128)(2,1)}, u32[]{:S(2)}, u32[]{:S(2)}) %all-to-all-start.5) | async-done | bytes 786464 | tf_op jit(solution)/shard_map/all_to_all | solution.py:41
  210.4 6.7 %shard_map.86 = (f32[128,1]{1,0:T(8,128)S(1)}, bf16[128,768]{1,0:T(8,128)(2,1)S(1)}, bf16[4,4,128,384]{3,2,1,0:T(8,128)(2,1)}, bf16[4,4,128,384]{3,2,1,0:T(8,128)(2,1)}) custom-call(s32[2]{0:T(128)S(1)} %pad_add_fusion.5.place_ref, bf16[128,768]{1,0:T(8,128)(2,1)S(1)} %fusion.2.embedded_ref, bf16[128,768]{1,0:T(8,128)(2,1)S(1)} %copy-done.5, ...), custom_call_target="tpu_custom_call" | custom-call | tf_op jit(solution)/shard_map/pallas_call | solution.py:251
  217.0 1.6 collective-permute-start.14
  218.6 5.2 %shard_map.87 = (bf16[4,768,256]{2,1,0:T(8,128)(2,1)S(1)}, bf16[4,768,256]{2,1,0:T(8,128)(2,1)}) custom-call(s32[2]{0:T(128)S(1)} %pad_add_fusion.5.place_ref, bf16[128,768]{1,0:T(8,128)(2,1)S(1)} %copy-done.2, bf16[128,768]{1,0:T(8,128)(2,1)S(1)} %get-tuple-element.52.grad_ref, f32[128,2048]{1,0:T(8,128)S(1)} %get-tuple-element.83.slope_ref, ...), custom_call_target="tpu_custom_call" | custom-call | tf_op jit(solution)/shard_map/pallas_call | solution.py:263
  224.0 1.7 add_convert_fusion
  225.6 3.9 %all-to-all-start.6 = ((bf16[4,4,128,384]{3,2,1,0:T(8,128)(2,1)}), bf16[4,4,128,384]{3,2,1,0:T(8,128)(2,1)S(1)}, u32[]{:S(2)}, u32[]{:S(2)}) async-start(bf16[4,4,128,384]{3,2,1,0:T(8,128)(2,1)} %add_convert_fusion), calls=%async_computation.6 | async-start | bytes 3145728 | tf_op jit(solution)/shard_map/all_to_all | solution.py:41
  229.5 2.7 fusion.20
  233.0 2.4 collective-permute-start.12
  235.5 14.1 %all-to-all-done.6 = bf16[4,4,128,384]{3,2,1,0:T(8,128)(2,1)S(1)} async-done(((bf16[4,4,128,384]{3,2,1,0:T(8,128)(2,1)}), bf16[4,4,128,384]{3,2,1,0:T(8,128)(2,1)S(1)}, u32[]{:S(2)}, u32[]{:S(2)}) %all-to-all-start.6) | async-done | bytes 1572896 | tf_op jit(solution)/shard_map/all_to_all | solution.py:41
  250.6 1.5 collective-permute-done.13
  255.0 1.8 collective-permute-start.17
  257.4 3.5 %all-to-all-start.7 = ((bf16[4,128,384]{2,1,0:T(8,128)(2,1)}), bf16[4,128,384]{2,1,0:T(8,128)(2,1)S(1)}, u32[]{:S(2)}, u32[]{:S(2)}) async-start(bf16[4,128,384]{2,1,0:T(8,128)(2,1)} %fusion.21), calls=%async_computation.7 | async-start | bytes 786432 | tf_op jit(solution)/shard_map/all_to_all | solution.py:41
  260.9 1.7 collective-permute-done.16
  262.7 4.3 %all-to-all-done.7 = bf16[4,128,384]{2,1,0:T(8,128)(2,1)S(1)} async-done(((bf16[4,128,384]{2,1,0:T(8,128)(2,1)}), bf16[4,128,384]{2,1,0:T(8,128)(2,1)S(1)}, u32[]{:S(2)}, u32[]{:S(2)}) %all-to-all-start.7) | async-done | bytes 393248 | tf_op jit(solution)/shard_map/all_to_all | solution.py:41
  267.2 11.0 %all_to_all.78 = bf16[8,96,128]{2,1,0:T(8,128)(2,1)S(1)} all-to-all(bf16[8,96,128]{2,1,0:T(8,128)(2,1)S(1)} %constant_dynamic-update-slice_fusion), channel_id=1, replica_groups=mesh['x'=4,'core'=2,'z'=8,'y'=4] {'z'}, dimensions={0} | all-to-all | bytes 393216 | tf_op jit(solution)/shard_map/all_to_all | solution.py:41
  279.0 8.3 %all-to-all-start.9 = ((f32[8,96,128]{2,1,0:T(8,128)}), f32[8,96,128]{2,1,0:T(8,128)S(1)}, u32[]{:S(2)}, u32[]{:S(2)}) async-start(f32[8,96,128]{2,1,0:T(8,128)} %broadcast_in_dim.147), calls=%async_computation.9 | async-start | bytes 786432 | tf_op jit(solution)/shard_map/all_to_all | solution.py:41
  287.9 7.5 %all-to-all-done.9 = f32[8,96,128]{2,1,0:T(8,128)S(1)} async-done(((f32[8,96,128]{2,1,0:T(8,128)}), f32[8,96,128]{2,1,0:T(8,128)S(1)}, u32[]{:S(2)}, u32[]{:S(2)}) %all-to-all-start.9) | async-done | bytes 393248 | tf_op jit(solution)/shard_map/all_to_all | solution.py:41
  (151 shorter events, 25.2 us)
Async XLA Ops:
  0.6 19.4 %copy-start = (bf16[64,768]{1,0:T(8,128)(2,1)S(1)}, bf16[64,768]{1,0:T(8,128)(2,1)}, u32[]{:S(2)}) copy-start(bf16[64,768]{1,0:T(8,128)(2,1)} %param.11) | copy-start | bytes 294916
  7.9 20.6 %all-to-all-start = ((s32[32,1,128]{2,1,0:T(1,128)}), s32[32,1,128]{2,1,0:T(1,128)S(1)}, u32[]{:S(2)}, u32[]{:S(2)}) async-start(s32[32,1,128]{2,1,0:T(1,128)} %bitcast.2), calls=%async_computation | async-start | bytes 32768 | tf_op jit(solution)/shard_map/all_to_all | solution.py:41
  35.0 23.0 %collective-permute-start = (bf16[512,768]{1,0:T(8,128)(2,1)S(1)}, bf16[512,768]{1,0:T(8,128)(2,1)}, u32[]{:S(2)}, u32[]{:S(2)}) collective-permute-start(bf16[512,768]{1,0:T(8,128)(2,1)S(1)} %broadcast_select_fusion.1), channel_id=1, source_target_pairs={{0,1},{1,0},{2,3},{3,2},{4,5},{5,4},{6,7},{7,6},{8,9},{9,8},{10,11... | collective-permute-start | bytes 2359304 | tf_op jit(solution)/shard_map/ppermute | solution.py:49
  36.4 24.7 %all-to-all-start.1 = ((bf16[32,16,768]{2,1,0:T(8,128)(2,1)}), bf16[32,16,768]{2,1,0:T(8,128)(2,1)S(1)}, u32[]{:S(2)}, u32[]{:S(2)}) async-start(bf16[32,16,768]{2,1,0:T(8,128)(2,1)} %broadcast_in_dim.124), calls=%async_computation.1 | async-start | bytes 1572864 | tf_op jit(solution)/shard_map/all_to_all | solution.py:41
  60.6 17.1 %collective-permute-start.4 = (bf16[512,768]{1,0:T(8,128)(2,1)}, bf16[512,768]{1,0:T(8,128)(2,1)S(1)}, u32[]{:S(2)}, u32[]{:S(2)}) collective-permute-start(bf16[512,768]{1,0:T(8,128)(2,1)} %get-tuple-element.81), channel_id=1, source_target_pairs={{0,1},{1,0},{2,3},{3,2},{4,5},{5,4},{6,7},{7,6},{8,9},{9,8},{10,11... | collective-permute-start | bytes 2359304 | tf_op jit(solution)/shard_map/ppermute | solution.py:49
  61.1 33.0 %collective-permute-start.3 = (bf16[32,16,768]{2,1,0:T(8,128)(2,1)S(1)}, bf16[32,16,768]{2,1,0:T(8,128)(2,1)}, u32[]{:S(2)}, u32[]{:S(2)}) collective-permute-start(bf16[32,16,768]{2,1,0:T(8,128)(2,1)S(1)} %all-to-all-done.1), channel_id=1, source_target_pairs={{0,192},{64,128},{128,64},{192,0},{1,193},{65,129},{129,65},{193,1... | collective-permute-start | bytes 2359304 | tf_op jit(solution)/shard_map/ppermute | solution.py:49
  63.6 30.4 %collective-permute-start.1 = (bf16[32,16,768]{2,1,0:T(8,128)(2,1)S(1)}, bf16[32,16,768]{2,1,0:T(8,128)(2,1)}, u32[]{:S(2)}, u32[]{:S(2)}) collective-permute-start(bf16[32,16,768]{2,1,0:T(8,128)(2,1)S(1)} %all-to-all-done.1), channel_id=1, source_target_pairs={{0,64},{64,0},{128,192},{192,128},{1,65},{65,1},{129,193},{193,129... | collective-permute-start | bytes 2359304 | tf_op jit(solution)/shard_map/ppermute | solution.py:49
  63.6 31.4 %all-to-all-start.2 = ((bf16[8,64,768]{2,1,0:T(8,128)(2,1)}), bf16[8,64,768]{2,1,0:T(8,128)(2,1)S(1)}, u32[]{:S(2)}, u32[]{:S(2)}) async-start(bf16[8,64,768]{2,1,0:T(8,128)(2,1)} %bitcast.8), calls=%async_computation.2 | async-start | bytes 1572864 | tf_op jit(solution)/shard_map/all_to_all | solution.py:41
  80.5 14.5 %collective-permute-start.5 = (bf16[512,768]{1,0:T(8,128)(2,1)}, bf16[512,768]{1,0:T(8,128)(2,1)S(1)}, u32[]{:S(2)}, u32[]{:S(2)}) collective-permute-start(bf16[512,768]{1,0:T(8,128)(2,1)} %get-tuple-element.77), channel_id=1, source_target_pairs={{0,3},{1,2},{2,1},{3,0},{4,7},{5,6},{6,5},{7,4},{8,11},{9,10},{10,... | collective-permute-start | bytes 2359304 | tf_op jit(solution)/shard_map/ppermute | solution.py:49
  95.0 0.9 copy-start.11
  95.9 44.0 %all-to-all-start.3 = ((bf16[8,64,768]{2,1,0:T(8,128)(2,1)}), bf16[8,64,768]{2,1,0:T(8,128)(2,1)S(1)}, u32[]{:S(2)}, u32[]{:S(2)}) async-start(bf16[8,64,768]{2,1,0:T(8,128)(2,1)} %bitcast.10), calls=%async_computation.3 | async-start | bytes 1572864 | tf_op jit(solution)/shard_map/all_to_all | solution.py:41
  102.0 13.3 %collective-permute-start.6 = (bf16[512,768]{1,0:T(8,128)(2,1)S(1)}, bf16[512,768]{1,0:T(8,128)(2,1)}, u32[]{:S(2)}, u32[]{:S(2)}) collective-permute-start(bf16[512,768]{1,0:T(8,128)(2,1)S(1)} %get-tuple-element.76), channel_id=1, source_target_pairs={{0,2},{1,3},{2,0},{3,1},{4,6},{5,7},{6,4},{7,5},{8,10},{9,11},{10,... | collective-permute-start | bytes 2359304 | tf_op jit(solution)/shard_map/ppermute | solution.py:49
  103.2 14.6 %collective-permute-start.2 = (bf16[32,16,768]{2,1,0:T(8,128)(2,1)S(1)}, bf16[32,16,768]{2,1,0:T(8,128)(2,1)}, u32[]{:S(2)}, u32[]{:S(2)}) collective-permute-start(bf16[32,16,768]{2,1,0:T(8,128)(2,1)S(1)} %all-to-all-done.1), channel_id=1, source_target_pairs={{0,128},{64,192},{128,0},{192,64},{1,129},{65,193},{129,1},{193,65... | collective-permute-start | bytes 2359304 | tf_op jit(solution)/shard_map/ppermute | solution.py:49
  104.5 35.4 %collective-permute-start.7 = (bf16[512,768]{1,0:T(8,128)(2,1)}, bf16[512,768]{1,0:T(8,128)(2,1)}, u32[]{:S(2)}, u32[]{:S(2)}) collective-permute-start(bf16[512,768]{1,0:T(8,128)(2,1)} %get-tuple-element.80), channel_id=1, source_target_pairs={{0,3},{1,2},{2,1},{3,0},{4,7},{5,6},{6,5},{7,4},{8,11},{9,10},{10,... | collective-permute-start | bytes 2359304 | tf_op jit(solution)/shard_map/ppermute | solution.py:49
  142.9 13.6 %copy-start.10 = (bf16[512,768]{1,0:T(8,128)(2,1)S(1)}, bf16[512,768]{1,0:T(8,128)(2,1)}, u32[]{:S(2)}) copy-start(bf16[512,768]{1,0:T(8,128)(2,1)} %get-tuple-element.79) | copy-start | bytes 2359300
  149.4 36.4 %collective-permute-start.8 = (bf16[4,32,16,768]{3,2,0,1:T(8,128)(2,1)}, bf16[4,32,16,768]{3,2,0,1:T(8,128)(2,1)}, u32[]{:S(2)}, u32[]{:S(2)}) collective-permute-start(bf16[4,32,16,768]{3,2,0,1:T(8,128)(2,1)} %bitcast_dynamic-update-slice_fusion.3), channel_id=1, source_target_pairs={{0,32},{32,0},{1,33},{33,1},{2,34},{34,2},{3,35},{35,3},{4,36},{36... | collective-permute-start | bytes 9437192 | tf_op jit(solution)/shard_map/ppermute | solution.py:49
  149.9 30.3 %all-to-all-start.4 = ((bf16[8,64,768]{2,1,0:T(8,128)(2,1)}), bf16[8,64,768]{2,1,0:T(8,128)(2,1)S(1)}, u32[]{:S(2)}, u32[]{:S(2)}) async-start(bf16[8,64,768]{2,1,0:T(8,128)(2,1)} %bitcast.49), calls=%async_computation.4 | async-start | bytes 1572864 | tf_op jit(solution)/shard_map/all_to_all | solution.py:41
  156.5 20.5 %collective-permute-start.9 = (bf16[512,768]{1,0:T(8,128)(2,1)S(1)}, bf16[512,768]{1,0:T(8,128)(2,1)}, u32[]{:S(2)}, u32[]{:S(2)}) collective-permute-start(bf16[512,768]{1,0:T(8,128)(2,1)S(1)} %copy-done.10), channel_id=1, source_target_pairs={{0,2},{1,3},{2,0},{3,1},{4,6},{5,7},{6,4},{7,5},{8,10},{9,11},{10,... | collective-permute-start | bytes 2359304 | tf_op jit(solution)/shard_map/ppermute | solution.py:49
  180.2 8.8 %copy-start.3 = (bf16[8,64,768]{2,1,0:T(8,128)(2,1)}, bf16[8,64,768]{2,1,0:T(8,128)(2,1)S(1)}, u32[]{:S(2)}) copy-start(bf16[8,64,768]{2,1,0:T(8,128)(2,1)S(1)} %all-to-all-done.4) | copy-start | bytes 2359300
  180.2 28.1 %all-to-all-start.5 = ((bf16[8,64,768]{2,1,0:T(8,128)(2,1)}), bf16[8,64,768]{2,1,0:T(8,128)(2,1)}, u32[]{:S(2)}, u32[]{:S(2)}) async-start(bf16[8,64,768]{2,1,0:T(8,128)(2,1)} %bitcast.51), calls=%async_computation.5 | async-start | bytes 1572864 | tf_op jit(solution)/shard_map/all_to_all | solution.py:41
  189.3 3.8 %copy-start.8 = (bf16[4,2,32,8,768]{4,3,1,0,2:T(8,128)(2,1)}, bf16[4,2,32,8,768]{4,3,1,0,2:T(8,128)(2,1)S(1)}, u32[]{:S(2)}) copy-start(bf16[4,2,32,8,768]{4,3,1,0,2:T(8,128)(2,1)S(1)} %pad_maximum_fusion) | copy-start | bytes 9437188
  189.5 1.2 copy-start.2
  208.3 1.1 copy-start.4
  209.4 0.9 copy-start.5
  217.0 6.8 %copy-start.6 = (f32[128,1]{1,0:T(8,128)}, f32[128,1]{1,0:T(8,128)S(1)}, u32[]{:S(2)}) copy-start(f32[128,1]{1,0:T(8,128)S(1)} %get-tuple-element.51) | copy-start | bytes 1540
  217.0 6.9 %copy-start.9 = (bf16[4,4,128,384]{3,2,1,0:T(8,128)(2,1)S(1)}, bf16[4,4,128,384]{3,2,1,0:T(8,128)(2,1)}, u32[]{:S(2)}) copy-start(bf16[4,4,128,384]{3,2,1,0:T(8,128)(2,1)} %get-tuple-element.55) | copy-start | bytes 4718596
  217.0 6.9 %collective-permute-start.14 = (bf16[4,4,128,384]{3,2,1,0:T(8,128)(2,1)}, bf16[4,4,128,384]{3,2,1,0:T(8,128)(2,1)S(1)}, u32[]{:S(2)}, u32[]{:S(2)}) collective-permute-start(bf16[4,4,128,384]{3,2,1,0:T(8,128)(2,1)} %get-tuple-element.56), channel_id=1, source_target_pairs={{0,32},{32,0},{1,33},{33,1},{2,34},{34,2},{3,35},{35,3},{4,36},{36... | collective-permute-start | bytes 4718600 | tf_op jit(solution)/shard_map/ppermute | solution.py:49
  223.8 5.7 %collective-permute-start.10 = (bf16[4,768,256]{2,1,0:T(8,128)(2,1)}, bf16[4,768,256]{2,1,0:T(8,128)(2,1)}, u32[]{:S(2)}, u32[]{:S(2)}) collective-permute-start(bf16[4,768,256]{2,1,0:T(8,128)(2,1)} %get-tuple-element.54), channel_id=1, source_target_pairs={{0,32},{32,0},{1,33},{33,1},{2,34},{34,2},{3,35},{35,3},{4,36},{36... | collective-permute-start | bytes 4718600 | tf_op jit(solution)/shard_map/ppermute | solution.py:49
  225.6 24.0 %all-to-all-start.6 = ((bf16[4,4,128,384]{3,2,1,0:T(8,128)(2,1)}), bf16[4,4,128,384]{3,2,1,0:T(8,128)(2,1)S(1)}, u32[]{:S(2)}, u32[]{:S(2)}) async-start(bf16[4,4,128,384]{3,2,1,0:T(8,128)(2,1)} %add_convert_fusion), calls=%async_computation.6 | async-start | bytes 3145728 | tf_op jit(solution)/shard_map/all_to_all | solution.py:41
  232.3 19.9 %collective-permute-start.13 = (bf16[768,256]{1,0:T(8,128)(2,1)}, bf16[768,256]{1,0:T(8,128)(2,1)S(1)}, u32[]{:S(2)}, u32[]{:S(2)}) collective-permute-start(bf16[768,256]{1,0:T(8,128)(2,1)} %get-tuple-element.64), channel_id=1, source_target_pairs={{0,192},{64,128},{128,64},{192,0},{1,193},{65,129},{129,65},{193,1... | collective-permute-start | bytes 1179656 | tf_op jit(solution)/shard_map/ppermute | solution.py:49
  233.0 19.1 %collective-permute-start.12 = (bf16[768,256]{1,0:T(8,128)(2,1)}, bf16[768,256]{1,0:T(8,128)(2,1)S(1)}, u32[]{:S(2)}, u32[]{:S(2)}) collective-permute-start(bf16[768,256]{1,0:T(8,128)(2,1)} %get-tuple-element.65), channel_id=1, source_target_pairs={{0,128},{64,192},{128,0},{192,64},{1,129},{65,193},{129,1},{193,65... | collective-permute-start | bytes 1179656 | tf_op jit(solution)/shard_map/ppermute | solution.py:49
  235.5 17.0 %collective-permute-start.11 = (bf16[768,256]{1,0:T(8,128)(2,1)}, bf16[768,256]{1,0:T(8,128)(2,1)S(1)}, u32[]{:S(2)}, u32[]{:S(2)}) collective-permute-start(bf16[768,256]{1,0:T(8,128)(2,1)} %get-tuple-element.66), channel_id=1, source_target_pairs={{0,64},{64,0},{128,192},{192,128},{1,65},{65,1},{129,193},{193,129... | collective-permute-start | bytes 1179656 | tf_op jit(solution)/shard_map/ppermute | solution.py:49
  252.5 34.9 %copy-start.7 = (f32[128,1]{1,0:T(8,128)S(1)}, f32[128,1]{1,0:T(8,128)}, u32[]{:S(2)}) copy-start(f32[128,1]{1,0:T(8,128)} %copy-done.6) | copy-start | bytes 1540
  253.7 7.1 %collective-permute-start.15 = (bf16[8,24,256]{2,1,0:T(8,128)(2,1)S(1)}, bf16[8,24,256]{2,1,0:T(8,128)(2,1)S(1)}, u32[]{:S(2)}, u32[]{:S(2)}) collective-permute-start(bf16[8,24,256]{2,1,0:T(8,128)(2,1)S(1)} %get-tuple-element.90), channel_id=1, source_target_pairs={{0,1},{1,0},{2,3},{3,2},{4,5},{5,4},{6,7},{7,6},{8,9},{9,8},{10,11... | collective-permute-start | bytes 294920 | tf_op jit(solution)/shard_map/ppermute | solution.py:49
  255.0 5.9 %collective-permute-start.17 = (bf16[8,24,256]{2,1,0:T(8,128)(2,1)S(1)}, bf16[8,24,256]{2,1,0:T(8,128)(2,1)S(1)}, u32[]{:S(2)}, u32[]{:S(2)}) collective-permute-start(bf16[8,24,256]{2,1,0:T(8,128)(2,1)S(1)} %get-tuple-element.91), channel_id=1, source_target_pairs={{0,3},{1,2},{2,1},{3,0},{4,7},{5,6},{6,5},{7,4},{8,11},{9,10},{10,... | collective-permute-start | bytes 294920 | tf_op jit(solution)/shard_map/ppermute | solution.py:49
  256.8 5.8 %collective-permute-start.16 = (bf16[8,24,256]{2,1,0:T(8,128)(2,1)S(1)}, bf16[8,24,256]{2,1,0:T(8,128)(2,1)S(1)}, u32[]{:S(2)}, u32[]{:S(2)}) collective-permute-start(bf16[8,24,256]{2,1,0:T(8,128)(2,1)S(1)} %get-tuple-element.92), channel_id=1, source_target_pairs={{0,2},{1,3},{2,0},{3,1},{4,6},{5,7},{6,4},{7,5},{8,10},{9,11},{10,... | collective-permute-start | bytes 294920 | tf_op jit(solution)/shard_map/ppermute | solution.py:49
  257.4 9.7 %all-to-all-start.7 = ((bf16[4,128,384]{2,1,0:T(8,128)(2,1)}), bf16[4,128,384]{2,1,0:T(8,128)(2,1)S(1)}, u32[]{:S(2)}, u32[]{:S(2)}) async-start(bf16[4,128,384]{2,1,0:T(8,128)(2,1)} %fusion.21), calls=%async_computation.7 | async-start | bytes 786432 | tf_op jit(solution)/shard_map/all_to_all | solution.py:41
  262.7 33.7 %copy-start.1 = (bf16[64,768]{1,0:T(8,128)(2,1)S(1)}, bf16[64,768]{1,0:T(8,128)(2,1)}, u32[]{:S(2)}) copy-start(bf16[64,768]{1,0:T(8,128)(2,1)} %param.11) | copy-start | bytes 294916
  279.0 16.4 %all-to-all-start.9 = ((f32[8,96,128]{2,1,0:T(8,128)}), f32[8,96,128]{2,1,0:T(8,128)S(1)}, u32[]{:S(2)}, u32[]{:S(2)}) async-start(f32[8,96,128]{2,1,0:T(8,128)} %broadcast_in_dim.147), calls=%async_computation.9 | async-start | bytes 786432 | tf_op jit(solution)/shard_map/all_to_all | solution.py:41
  295.6 0.7 copy-start.12
where the time goes:
time: 298 us; the launch traced here: 296 us
  waiting for transfers between devices  113 us (38%)
  starting transfers between devices  72.6 us (24%)
  local copies, waits for them, and re-layouts  52.9 us (18%)
  other arithmetic  25.5 us (9%)
  Pallas kernels  17.7 us (6%)
  blocking collectives  11 us (4%)
    ppermute x18, waiting for transfers between devices, swap(): lax.ppermute(value, axis, [(i, i ^ by) for i in range(lax.axis_size(axis))])  64.2 us
    all_to_all x9, starting transfers between devices, exchange(): return lax.all_to_all(value, axes, split_axis=0, concat_axis=0, tiled=True)  53.6 us
    all_to_all x9, waiting for transfers between devices, exchange(): return lax.all_to_all(value, axes, split_axis=0, concat_axis=0, tiled=True)  48.9 us
    gather x4, local copies, waits for them, and re-layouts, find(): passage_table.at[ids].get(mode='promise_in_bounds')  33.5 us
    ppermute x18, starting transfers between devices, swap(): lax.ppermute(value, axis, [(i, i ^ by) for i in range(lax.axis_size(axis))])  19 us
    all_to_all x1, blocking collectives, exchange(): return lax.all_to_all(value, axes, split_axis=0, concat_axis=0, tiled=True)  11 us
    select_n x4, other arithmetic, find(): jnp.where(own[by, :, cuts[part]].reshape(-1, 1), found[i], jnp.zeros((),...  8.15 us
    dynamic_update_slice x4, local copies, waits for them, and re-layouts, shards(): lax.dynamic_update_index_in_dim(gathered, parts[by], my_x ^ by, 0)  7.43 us
  transfers between devices with their start and end apart: 27, of which 14 were waited for; matrix products, arithmetic and copies ran while one was open for 19% of the time, Pallas kernels for 2%

commit v1 on v0

--- a/solution.py
+++ b/solution.py
@@ -81,6 +81,14 @@
         placed = placed + contract_first(item.astype(jnp.float32).astype(jnp.bfloat16), at_slot)
     code_ref[...] = (placed[:PAIRS] * 64.0 + placed[PAIRS : 2 * PAIRS]).astype(jnp.int32)
     query_ref[...] = placed[2 * PAIRS : 3 * PAIRS].astype(jnp.int32)
+
+
+def arrange_kernel(place_ref, *refs):
+    part_refs, out_ref = refs[:GRP], refs[GRP]
+    for by_core in range(CORE):
+        for by_x in range(X):
+            at = place_ref[0] ^ by_x, place_ref[1] ^ by_core
+            out_ref[at] = part_refs[by_core * X + by_x][...]
 
 
 def score_kernel(scale, place_ref, embedded_ref, positives_ref, hidden_ref, query_ref, *refs):
@@ -203,35 +211,35 @@
     gathered = spread(after(piece, found_10), ("z", "y"), SHARD)
     found_00, found_11 = find([(0, 0), (1, 1)], found_10)
     near_11 = swap(found_11, "y", 1)
-    own_0 = after(found_00 + near_10, gathered)
+    own_0 = after(found_00 + after(near_10, found_11), gathered)
     rows_0 = exchange(own_0, "z")
+    found_30, found_01, found_20 = find([(3, 0), (0, 1), (2, 0)], own_0)
+    near_30, near_20 = swap(found_30, "y", 3), swap(found_20, "y", 2)
     gathered = after(gathered, own_0)
     parts = [gathered] + [swap(gathered, "x", by) for by in range(1, X)]
-    found_30, found_01, found_20 = find([(3, 0), (0, 1), (2, 0)], own_0)
-    near_30, near_20 = swap(found_30, "y", 3), swap(found_20, "y", 2)
     found_31, found_21 = find([(3, 1), (2, 1)], found_30)
     near_31, near_21 = swap(found_31, "y", 3), swap(found_21, "y", 2)
-    rows_1 = exchange(after(found_01 + near_11, rows_0, near_30, found_31, parts[1], parts[3]), "z")
-    other_0 = near_20 + near_30
-    rows_2 = exchange(after(other_0, rows_1, near_31), "z")
+    own_1 = found_01 + near_11
+    rows_1 = exchange(
+        after(own_1, rows_0, near_30, near_20, found_31, parts[1], parts[3]), "z"
+    )
+    rows_2 = exchange(after(near_20 + near_30, rows_1, near_21, parts[2]), "z")
     other_1 = near_21 + near_31
     rows_3 = exchange(after(other_1, rows_2), "z")
     chunks = [rows_0, rows_1, rows_2, rows_3]
-    parts = after(tuple(parts), rows_1, other_0, near_31)
-    gathered = jnp.zeros((X, *gathered.shape), gathered.dtype)
-    for by in range(X):
-        gathered = lax.dynamic_update_index_in_dim(gathered, parts[by], my_x ^ by, 0)
-    twin = swap(gathered, "core", 1)
-    gathered, twin = after((gathered, twin), other_1)
+    parts = after(tuple(parts + [swap(part, "core", 1) for part in parts]), rows_1, other_1)
+    halves = pl.pallas_call(
+        arrange_kernel,
+        out_shape=jax.ShapeDtypeStruct((X, CORE, SHARD, *piece.shape), piece.dtype),
+        in_specs=[in_smem] + [in_vmem] * GRP,
+        **limits,
+    )(place, *parts)
     slot_query = slot_query.reshape(Z, 2, q_dev)
     slot_query = jnp.where(my_y // 2 == 0, slot_query, slot_query[:, ::-1])
     slot_query = jnp.concatenate(
         [slot_query[:, pair, cut].reshape(1, -1) for pair in range(2) for cut in cuts], axis=1
     )
 
-    halves = jnp.stack(
-        [jnp.where(my_core == 0, gathered, twin), jnp.where(my_core == 0, twin, gathered)], axis=1
-    )
     inner_full = [
         columns_to_rows(halves[g // CORE, g % CORE, :, :deep], wide).reshape(width, wide)
         for g in range(GRP)

time: 298 us -> 318 us (1.067)
  waiting for transfers between devices: 113 us -> 123 us
  Pallas kernels: 17.7 us -> 23.4 us
  matrix products: 2.3 us -> 7.9 us
  local copies, waits for them, and re-layouts: 52.9 us -> 48.7 us
  starting transfers between devices: 72.6 us -> 76.4 us
    dynamic_update_slice x4 -> x0, local copies, waits for them, and re-layouts: 7.43 us -> none  [shards(): lax.dynamic_update_index_in_dim(gathered, parts[by], my_x ^ by, 0)]
    all_to_all x9, waiting for transfers between devices: 48.9 us -> 55.1 us  [exchange(): return lax.all_to_all(value, axes, split_axis=0, concat_axis=0, tiled=True)]
    pallas_call x0 -> x1, Pallas kernels: none -> 5.7 us  [shards(): pl.pallas_call(arrange_kernel, out_shape=jax.ShapeDtypeStruct((X, CORE, S...]
    dot_general x8, matrix products: 1.71 us -> 7.31 us  [shards(): jnp.dot(queries, part, preferred_element_type=jnp.float32)]
    transpose x0 -> x2, local copies, waits for them, and re-layouts: none -> 4.22 us  [shards(): halves[:, :, :, deep:].transpose(2, 0, 1, 3, 4).reshape(hid, width)]
    ppermute x18 -> x21, waiting for transfers between devices: 64.2 us -> 68.1 us  [swap(): lax.ppermute(value, axis, [(i, i ^ by) for i in range(lax.axis_size(axis))])]
    another operation x4 -> x2, other arithmetic: 3.54 us -> 0.11 us  [the longest x2 3.43 us: shards(): jnp.stack([jnp.where(my_core == 0, gathered, twin), jnp.where(my_core ==...]
    ppermute x18 -> x21, starting transfers between devices: 19 us -> 21.6 us  [swap(): lax.ppermute(value, axis, [(i, i ^ by) for i in range(lax.axis_size(axis))])]
  transfers between devices with their start and end apart: 27 -> 30, of which waited for: 14 -> 13; matrix products, arithmetic and copies ran while one was open for 19% -> 21% of each run, Pallas kernels for 2% -> 3%
where the time goes in v1:
time: 318 us; the launch traced here: 316 us
  waiting for transfers between devices  123 us (39%)
  starting transfers between devices  76.4 us (24%)
  local copies, waits for them, and re-layouts  48.7 us (15%)
  other arithmetic  24 us (8%)
  Pallas kernels  23.4 us (7%)
  blocking collectives  11.2 us (4%)
  matrix products  7.9 us (2%)
    ppermute x21, waiting for transfers between devices, swap(): lax.ppermute(value, axis, [(i, i ^ by) for i in range(lax.axis_size(axis))])  68.1 us
    all_to_all x9, waiting for transfers between devices, exchange(): return lax.all_to_all(value, axes, split_axis=0, concat_axis=0, tiled=True)  55.1 us
    all_to_all x9, starting transfers between devices, exchange(): return lax.all_to_all(value, axes, split_axis=0, concat_axis=0, tiled=True)  54.8 us
    gather x4, local copies, waits for them, and re-layouts, find(): passage_table.at[ids].get(mode='promise_in_bounds')  33.6 us
    ppermute x21, starting transfers between devices, swap(): lax.ppermute(value, axis, [(i, i ^ by) for i in range(lax.axis_size(axis))])  21.6 us
    all_to_all x1, blocking collectives, exchange(): return lax.all_to_all(value, axes, split_axis=0, concat_axis=0, tiled=True)  11.2 us
    select_n x4, other arithmetic, find(): jnp.where(own[by, :, cuts[part]].reshape(-1, 1), found[i], jnp.zeros((),...  7.69 us
    dot_general x8, matrix products, shards(): jnp.dot(queries, part, preferred_element_type=jnp.float32)  7.31 us
  transfers between devices with their start and end apart: 30, of which 13 were waited for; matrix products, arithmetic and copies ran while one was open for 21% of the time, Pallas kernels for 3%

profile of v1, /device:TPU:1, one launch (start us, length us, event | category | flops | bytes accessed | tf_op | source)
XLA Modules:
  0.0 316.1 jit_solution(6415036520482526756)
XLA Ops:
  1.5 5.8 %shard_map.85 = (s32[16,128]{1,0:T(8,128)S(1)}, s32[16,128]{1,0:T(8,128)S(1)}) custom-call(s32[128,16]{1,0:T(8,128)S(1)} %copy.33.ids_ref), custom_call_target="tpu_custom_call" | custom-call | tf_op jit(solution)/shard_map/pallas_call | solution.py:182
  7.9 12.0 %all-to-all-start = ((s32[32,1,128]{2,1,0:T(1,128)}), s32[32,1,128]{2,1,0:T(1,128)S(1)}, u32[]{:S(2)}, u32[]{:S(2)}) async-start(s32[32,1,128]{2,1,0:T(1,128)} %bitcast.2), calls=%async_computation | async-start | bytes 32768 | tf_op jit(solution)/shard_map/all_to_all | solution.py:41
  20.8 7.7 %all-to-all-done = s32[32,1,128]{2,1,0:T(1,128)S(1)} async-done(((s32[32,1,128]{2,1,0:T(1,128)}), s32[32,1,128]{2,1,0:T(1,128)S(1)}, u32[]{:S(2)}, u32[]{:S(2)}) %all-to-all-start) | async-done | bytes 16416 | tf_op jit(solution)/shard_map/all_to_all | solution.py:41
  28.9 6.0 %gather_fusion = bf16[512,768]{1,0:T(8,128)(2,1)S(1)} fusion(bf16[4096,768]{1,0:T(8,128)(2,1)} %param.9, s32[1024]{0:T(1024)S(1)} %pad_clamp_fusion.1), kind=kCustom, calls=%fused_computation | custom fusion | bytes 1574912 | tf_op jit(solution)/shard_map/gather | solution.py:198
  36.9 3.9 %all-to-all-start.1 = ((bf16[32,16,768]{2,1,0:T(8,128)(2,1)}), bf16[32,16,768]{2,1,0:T(8,128)(2,1)S(1)}, u32[]{:S(2)}, u32[]{:S(2)}) async-start(bf16[32,16,768]{2,1,0:T(8,128)(2,1)} %broadcast_in_dim.107), calls=%async_computation.1 | async-start | bytes 1572864 | tf_op jit(solution)/shard_map/all_to_all | solution.py:41
  42.2 8.1 %gather_fusion.1 = bf16[1024,768]{1,0:T(8,128)(2,1)S(1)} fusion(bf16[4096,768]{1,0:T(8,128)(2,1)} %param.9, s32[1024]{0:T(1024)S(1)} %fusion.39), kind=kCustom, calls=%fused_computation.1 | custom fusion | bytes 3149824 | tf_op jit(solution)/shard_map/gather | solution.py:198
  52.3 14.1 %collective-permute-done = bf16[512,768]{1,0:T(8,128)(2,1)} collective-permute-done((bf16[512,768]{1,0:T(8,128)(2,1)}, bf16[512,768]{1,0:T(8,128)(2,1)}, u32[]{:S(2)}, u32[]{:S(2)}) %collective-permute-start) | collective-permute-done | bytes 786464 | tf_op jit(solution)/shard_map/ppermute | solution.py:49
  66.4 2.2 fusion.14
  68.6 2.5 collective-permute-start.3
  71.1 7.5 %all-to-all-start.2 = ((bf16[8,64,768]{2,1,0:T(8,128)(2,1)}), bf16[8,64,768]{2,1,0:T(8,128)(2,1)S(1)}, u32[]{:S(2)}, u32[]{:S(2)}) async-start(bf16[8,64,768]{2,1,0:T(8,128)(2,1)} %bitcast.8), calls=%async_computation.2 | async-start | bytes 1572864 | tf_op jit(solution)/shard_map/all_to_all | solution.py:41
  78.6 10.3 %gather_fusion.2 = bf16[1536,768]{1,0:T(8,128)(2,1)} fusion(bf16[4096,768]{1,0:T(8,128)(2,1)} %param.9, s32[2048]{0:T(1024)S(1)} %pad_clamp_fusion), kind=kCustom, calls=%fused_computation.2 | custom fusion | bytes 4724736 | tf_op jit(solution)/shard_map/gather | solution.py:198
  88.9 2.8 slice_select_fusion.2
  91.7 2.5 collective-permute-start.10
  94.9 1.4 collective-permute-start.2
  96.3 9.2 %gather_fusion.3 = bf16[1024,768]{1,0:T(8,128)(2,1)} fusion(bf16[4096,768]{1,0:T(8,128)(2,1)} %param.9, s32[1024]{0:T(1024)S(1)} %fusion.40), kind=kCustom, calls=%fused_computation.3 | custom fusion | bytes 3149824 | tf_op jit(solution)/shard_map/gather | solution.py:198
  105.5 2.8 slice_select_fusion
  108.3 1.2 collective-permute-start.11
  109.6 37.1 %collective-permute-done.9 = bf16[512,768]{1,0:T(8,128)(2,1)} collective-permute-done((bf16[512,768]{1,0:T(8,128)(2,1)S(1)}, bf16[512,768]{1,0:T(8,128)(2,1)}, u32[]{:S(2)}, u32[]{:S(2)}) %collective-permute-start.9) | collective-permute-done | bytes 786464 | tf_op jit(solution)/shard_map/ppermute | solution.py:49
  146.7 6.8 %all-to-all-start.3 = ((bf16[8,64,768]{2,1,0:T(8,128)(2,1)}), bf16[8,64,768]{2,1,0:T(8,128)(2,1)S(1)}, u32[]{:S(2)}, u32[]{:S(2)}) async-start(bf16[8,64,768]{2,1,0:T(8,128)(2,1)} %bitcast.10), calls=%async_computation.3 | async-start | bytes 1572864 | tf_op jit(solution)/shard_map/all_to_all | solution.py:41
  153.5 2.1 collective-permute-start.12
  157.7 2.4 add.187
  160.2 13.0 %collective-permute-done.12 = bf16[512,768]{1,0:T(8,128)(2,1)} collective-permute-done((bf16[512,768]{1,0:T(8,128)(2,1)S(1)}, bf16[512,768]{1,0:T(8,128)(2,1)}, u32[]{:S(2)}, u32[]{:S(2)}) %collective-permute-start.12) | collective-permute-done | bytes 786464 | tf_op jit(solution)/shard_map/ppermute | solution.py:49
  173.2 2.5 add.184
  175.7 1.4 all-to-all-done.3
  177.1 4.9 %all-to-all-start.4 = ((bf16[8,64,768]{2,1,0:T(8,128)(2,1)}), bf16[8,64,768]{2,1,0:T(8,128)(2,1)S(1)}, u32[]{:S(2)}, u32[]{:S(2)}) async-start(bf16[8,64,768]{2,1,0:T(8,128)(2,1)} %bitcast.182), calls=%async_computation.4 | async-start | bytes 1572864 | tf_op jit(solution)/shard_map/all_to_all | solution.py:41
  182.0 5.7 %shard_map.86 = bf16[4,2,32,16,768]{4,3,2,1,0:T(8,128)(2,1)} custom-call(s32[2]{0:T(128)S(1)} %pad_add_fusion.5.place_ref, bf16[32,16,768]{2,1,0:T(8,128)(2,1)S(1)} %all-to-all-done.1.refs_0_, bf16[32,16,768]{2,1,0:T(8,128)(2,1)} %collective-permute-done.1.refs_1_, bf16[32,16,768]{2,1,0:T(8,128)(2,1)} %collective-permute-done.2.refs_2_, ...), custom_call_target="tpu_custom_call" | custom-call | tf_op jit(solution)/shard_map/pallas_call | solution.py:231
  187.7 2.2 slice_bitcast_fusion.1
  196.5 2.0 slice_bitcast_fusion
  198.5 5.1 %all-to-all-done.4 = bf16[8,64,768]{2,1,0:T(8,128)(2,1)S(1)} async-done(((bf16[8,64,768]{2,1,0:T(8,128)(2,1)}), bf16[8,64,768]{2,1,0:T(8,128)(2,1)S(1)}, u32[]{:S(2)}, u32[]{:S(2)}) %all-to-all-start.4) | async-done | bytes 786464 | tf_op jit(solution)/shard_map/all_to_all | solution.py:41
  203.6 4.4 %all-to-all-start.5 = ((bf16[8,64,768]{2,1,0:T(8,128)(2,1)}), bf16[8,64,768]{2,1,0:T(8,128)(2,1)}, u32[]{:S(2)}, u32[]{:S(2)}) async-start(bf16[8,64,768]{2,1,0:T(8,128)(2,1)} %bitcast.181), calls=%async_computation.5 | async-start | bytes 1572864 | tf_op jit(solution)/shard_map/all_to_all | solution.py:41
  208.1 2.3 copy.42
  212.4 1.7 fusion.12
  214.6 15.0 %all-to-all-done.5 = bf16[8,64,768]{2,1,0:T(8,128)(2,1)} async-done(((bf16[8,64,768]{2,1,0:T(8,128)(2,1)}), bf16[8,64,768]{2,1,0:T(8,128)(2,1)}, u32[]{:S(2)}, u32[]{:S(2)}) %all-to-all-start.5) | async-done | bytes 786464 | tf_op jit(solution)/shard_map/all_to_all | solution.py:41
  231.7 6.7 %shard_map.87 = (f32[128,1]{1,0:T(8,128)S(1)}, bf16[128,768]{1,0:T(8,128)(2,1)S(1)}, bf16[4,4,128,384]{3,2,1,0:T(8,128)(2,1)}, bf16[4,4,128,384]{3,2,1,0:T(8,128)(2,1)}) custom-call(s32[2]{0:T(128)S(1)} %pad_add_fusion.5.place_ref, bf16[128,768]{1,0:T(8,128)(2,1)S(1)} %fusion.embedded_ref, bf16[128,768]{1,0:T(8,128)(2,1)S(1)} %copy-done.5, ...), custom_call_target="tpu_custom_call" | custom-call | tf_op jit(solution)/shard_map/pallas_call | solution.py:259
  239.6 5.2 %shard_map.88 = (bf16[4,768,256]{2,1,0:T(8,128)(2,1)S(1)}, bf16[4,768,256]{2,1,0:T(8,128)(2,1)}) custom-call(s32[2]{0:T(128)S(1)} %pad_add_fusion.5.place_ref, bf16[128,768]{1,0:T(8,128)(2,1)S(1)} %copy-done.2, bf16[128,768]{1,0:T(8,128)(2,1)S(1)} %get-tuple-element.58.grad_ref, f32[128,2048]{1,0:T(8,128)S(1)} %get-tuple-element.84.slope_ref, ...), custom_call_target="tpu_custom_call" | custom-call | tf_op jit(solution)/shard_map/pallas_call | solution.py:271
  244.8 1.7 add_convert_fusion
  246.5 3.6 %all-to-all-start.6 = ((bf16[4,4,128,384]{3,2,1,0:T(8,128)(2,1)}), bf16[4,4,128,384]{3,2,1,0:T(8,128)(2,1)S(1)}, u32[]{:S(2)}, u32[]{:S(2)}) async-start(bf16[4,4,128,384]{3,2,1,0:T(8,128)(2,1)} %add_convert_fusion), calls=%async_computation.6 | async-start | bytes 3145728 | tf_op jit(solution)/shard_map/all_to_all | solution.py:41
  250.1 2.7 fusion.18
  253.6 2.5 collective-permute-start.15
  256.1 14.3 %all-to-all-done.6 = bf16[4,4,128,384]{3,2,1,0:T(8,128)(2,1)S(1)} async-done(((bf16[4,4,128,384]{3,2,1,0:T(8,128)(2,1)}), bf16[4,4,128,384]{3,2,1,0:T(8,128)(2,1)S(1)}, u32[]{:S(2)}, u32[]{:S(2)}) %all-to-all-start.6) | async-done | bytes 1572896 | tf_op jit(solution)/shard_map/all_to_all | solution.py:41
  271.3 1.5 collective-permute-done.16
  274.6 1.8 collective-permute-start.20
  277.0 3.5 %all-to-all-start.7 = ((bf16[4,128,384]{2,1,0:T(8,128)(2,1)}), bf16[4,128,384]{2,1,0:T(8,128)(2,1)S(1)}, u32[]{:S(2)}, u32[]{:S(2)}) async-start(bf16[4,128,384]{2,1,0:T(8,128)(2,1)} %fusion.19), calls=%async_computation.7 | async-start | bytes 786432 | tf_op jit(solution)/shard_map/all_to_all | solution.py:41
  280.5 1.9 collective-permute-done.19
  282.5 4.2 %all-to-all-done.7 = bf16[4,128,384]{2,1,0:T(8,128)(2,1)S(1)} async-done(((bf16[4,128,384]{2,1,0:T(8,128)(2,1)}), bf16[4,128,384]{2,1,0:T(8,128)(2,1)S(1)}, u32[]{:S(2)}, u32[]{:S(2)}) %all-to-all-start.7) | async-done | bytes 393248 | tf_op jit(solution)/shard_map/all_to_all | solution.py:41
  286.8 11.2 %all_to_all.78 = bf16[8,96,128]{2,1,0:T(8,128)(2,1)S(1)} all-to-all(bf16[8,96,128]{2,1,0:T(8,128)(2,1)S(1)} %constant_dynamic-update-slice_fusion), channel_id=1, replica_groups=mesh['x'=4,'core'=2,'z'=8,'y'=4] {'z'}, dimensions={0} | all-to-all | bytes 393216 | tf_op jit(solution)/shard_map/all_to_all | solution.py:41
  298.8 8.3 %all-to-all-start.9 = ((f32[8,96,128]{2,1,0:T(8,128)}), f32[8,96,128]{2,1,0:T(8,128)S(1)}, u32[]{:S(2)}, u32[]{:S(2)}) async-start(f32[8,96,128]{2,1,0:T(8,128)} %broadcast_in_dim.126), calls=%async_computation.9 | async-start | bytes 786432 | tf_op jit(solution)/shard_map/all_to_all | solution.py:41
  307.7 7.5 %all-to-all-done.9 = f32[8,96,128]{2,1,0:T(8,128)S(1)} async-done(((f32[8,96,128]{2,1,0:T(8,128)}), f32[8,96,128]{2,1,0:T(8,128)S(1)}, u32[]{:S(2)}, u32[]{:S(2)}) %all-to-all-start.9) | async-done | bytes 393248 | tf_op jit(solution)/shard_map/all_to_all | solution.py:41
  (160 shorter events, 29.9 us)
Async XLA Ops:
  0.6 19.4 %copy-start = (bf16[64,768]{1,0:T(8,128)(2,1)S(1)}, bf16[64,768]{1,0:T(8,128)(2,1)}, u32[]{:S(2)}) copy-start(bf16[64,768]{1,0:T(8,128)(2,1)} %param.11) | copy-start | bytes 294916
  7.9 20.6 %all-to-all-start = ((s32[32,1,128]{2,1,0:T(1,128)}), s32[32,1,128]{2,1,0:T(1,128)S(1)}, u32[]{:S(2)}, u32[]{:S(2)}) async-start(s32[32,1,128]{2,1,0:T(1,128)} %bitcast.2), calls=%async_computation | async-start | bytes 32768 | tf_op jit(solution)/shard_map/all_to_all | solution.py:41
  36.9 31.7 %all-to-all-start.1 = ((bf16[32,16,768]{2,1,0:T(8,128)(2,1)}), bf16[32,16,768]{2,1,0:T(8,128)(2,1)S(1)}, u32[]{:S(2)}, u32[]{:S(2)}) async-start(bf16[32,16,768]{2,1,0:T(8,128)(2,1)} %broadcast_in_dim.107), calls=%async_computation.1 | async-start | bytes 1572864 | tf_op jit(solution)/shard_map/all_to_all | solution.py:41
  40.9 25.5 %collective-permute-start = (bf16[512,768]{1,0:T(8,128)(2,1)}, bf16[512,768]{1,0:T(8,128)(2,1)}, u32[]{:S(2)}, u32[]{:S(2)}) collective-permute-start(bf16[512,768]{1,0:T(8,128)(2,1)} %broadcast_select_fusion), channel_id=1, source_target_pairs={{0,1},{1,0},{2,3},{3,2},{4,5},{5,4},{6,7},{7,6},{8,9},{9,8},{10,11... | collective-permute-start | bytes 2359304 | tf_op jit(solution)/shard_map/ppermute | solution.py:49
  51.3 37.6 %collective-permute-start.8 = (bf16[512,768]{1,0:T(8,128)(2,1)}, bf16[512,768]{1,0:T(8,128)(2,1)S(1)}, u32[]{:S(2)}, u32[]{:S(2)}) collective-permute-start(bf16[512,768]{1,0:T(8,128)(2,1)} %slice_select_fusion.5), channel_id=1, source_target_pairs={{0,1},{1,0},{2,3},{3,2},{4,5},{5,4},{6,7},{7,6},{8,9},{9,8},{10,11... | collective-permute-start | bytes 2359304 | tf_op jit(solution)/shard_map/ppermute | solution.py:49
  68.6 39.7 %collective-permute-start.3 = (bf16[32,16,768]{2,1,0:T(8,128)(2,1)S(1)}, bf16[32,16,768]{2,1,0:T(8,128)(2,1)}, u32[]{:S(2)}, u32[]{:S(2)}) collective-permute-start(bf16[32,16,768]{2,1,0:T(8,128)(2,1)S(1)} %all-to-all-done.1.refs_0_), channel_id=1, source_target_pairs={{0,192},{64,128},{128,64},{192,0},{1,193},{65,129},{129,65},{193,1... | collective-permute-start | bytes 2359304 | tf_op jit(solution)/shard_map/ppermute | solution.py:49
  71.1 38.5 %collective-permute-start.1 = (bf16[32,16,768]{2,1,0:T(8,128)(2,1)S(1)}, bf16[32,16,768]{2,1,0:T(8,128)(2,1)}, u32[]{:S(2)}, u32[]{:S(2)}) collective-permute-start(bf16[32,16,768]{2,1,0:T(8,128)(2,1)S(1)} %all-to-all-done.1.refs_0_), channel_id=1, source_target_pairs={{0,64},{64,0},{128,192},{192,128},{1,65},{65,1},{129,193},{193,129... | collective-permute-start | bytes 2359304 | tf_op jit(solution)/shard_map/ppermute | solution.py:49
  71.1 75.6 %all-to-all-start.2 = ((bf16[8,64,768]{2,1,0:T(8,128)(2,1)}), bf16[8,64,768]{2,1,0:T(8,128)(2,1)S(1)}, u32[]{:S(2)}, u32[]{:S(2)}) async-start(bf16[8,64,768]{2,1,0:T(8,128)(2,1)} %bitcast.8), calls=%async_computation.2 | async-start | bytes 1572864 | tf_op jit(solution)/shard_map/all_to_all | solution.py:41
  91.7 17.8 %collective-permute-start.10 = (bf16[512,768]{1,0:T(8,128)(2,1)}, bf16[512,768]{1,0:T(8,128)(2,1)S(1)}, u32[]{:S(2)}, u32[]{:S(2)}) collective-permute-start(bf16[512,768]{1,0:T(8,128)(2,1)} %get-tuple-element.79), channel_id=1, source_target_pairs={{0,2},{1,3},{2,0},{3,1},{4,6},{5,7},{6,4},{7,5},{8,10},{9,11},{10,... | collective-permute-start | bytes 2359304 | tf_op jit(solution)/shard_map/ppermute | solution.py:49
  94.2 52.5 %collective-permute-start.9 = (bf16[512,768]{1,0:T(8,128)(2,1)S(1)}, bf16[512,768]{1,0:T(8,128)(2,1)}, u32[]{:S(2)}, u32[]{:S(2)}) collective-permute-start(bf16[512,768]{1,0:T(8,128)(2,1)S(1)} %get-tuple-element.80), channel_id=1, source_target_pairs={{0,3},{1,2},{2,1},{3,0},{4,7},{5,6},{6,5},{7,4},{8,11},{9,10},{10,... | collective-permute-start | bytes 2359304 | tf_op jit(solution)/shard_map/ppermute | solution.py:49
  94.9 61.7 %collective-permute-start.2 = (bf16[32,16,768]{2,1,0:T(8,128)(2,1)S(1)}, bf16[32,16,768]{2,1,0:T(8,128)(2,1)}, u32[]{:S(2)}, u32[]{:S(2)}) collective-permute-start(bf16[32,16,768]{2,1,0:T(8,128)(2,1)S(1)} %all-to-all-done.1.refs_0_), channel_id=1, source_target_pairs={{0,128},{64,192},{128,0},{192,64},{1,129},{65,193},{129,1},{193,65... | collective-permute-start | bytes 2359304 | tf_op jit(solution)/shard_map/ppermute | solution.py:49
  108.3 48.8 %collective-permute-start.11 = (bf16[512,768]{1,0:T(8,128)(2,1)}, bf16[512,768]{1,0:T(8,128)(2,1)}, u32[]{:S(2)}, u32[]{:S(2)}) collective-permute-start(bf16[512,768]{1,0:T(8,128)(2,1)} %get-tuple-element.82), channel_id=1, source_target_pairs={{0,2},{1,3},{2,0},{3,1},{4,6},{5,7},{6,4},{7,5},{8,10},{9,11},{10,... | collective-permute-start | bytes 2359304 | tf_op jit(solution)/shard_map/ppermute | solution.py:49
  109.6 37.1 %copy-start.11 = (bf16[512,768]{1,0:T(8,128)(2,1)}, bf16[512,768]{1,0:T(8,128)(2,1)S(1)}, u32[]{:S(2)}) copy-start(bf16[512,768]{1,0:T(8,128)(2,1)S(1)} %collective-permute-done.10) | copy-start | bytes 2359300
  146.7 6.8 %copy-start.12 = (bf16[512,768]{1,0:T(8,128)(2,1)S(1)}, bf16[512,768]{1,0:T(8,128)(2,1)}, u32[]{:S(2)}) copy-start(bf16[512,768]{1,0:T(8,128)(2,1)} %get-tuple-element.83) | copy-start | bytes 2359300
  146.7 30.4 %all-to-all-start.3 = ((bf16[8,64,768]{2,1,0:T(8,128)(2,1)}), bf16[8,64,768]{2,1,0:T(8,128)(2,1)S(1)}, u32[]{:S(2)}, u32[]{:S(2)}) async-start(bf16[8,64,768]{2,1,0:T(8,128)(2,1)} %bitcast.10), calls=%async_computation.3 | async-start | bytes 1572864 | tf_op jit(solution)/shard_map/all_to_all | solution.py:41
  153.5 19.7 %collective-permute-start.12 = (bf16[512,768]{1,0:T(8,128)(2,1)S(1)}, bf16[512,768]{1,0:T(8,128)(2,1)}, u32[]{:S(2)}, u32[]{:S(2)}) collective-permute-start(bf16[512,768]{1,0:T(8,128)(2,1)S(1)} %copy-done.12), channel_id=1, source_target_pairs={{0,3},{1,2},{2,1},{3,0},{4,7},{5,6},{6,5},{7,4},{8,11},{9,10},{10,... | collective-permute-start | bytes 2359304 | tf_op jit(solution)/shard_map/ppermute | solution.py:49
  155.6 26.4 %collective-permute-start.4 = (bf16[32,16,768]{2,1,0:T(8,128)(2,1)S(1)}, bf16[32,16,768]{2,1,0:T(8,128)(2,1)}, u32[]{:S(2)}, u32[]{:S(2)}) collective-permute-start(bf16[32,16,768]{2,1,0:T(8,128)(2,1)S(1)} %all-to-all-done.1.refs_0_), channel_id=1, source_target_pairs={{0,32},{32,0},{1,33},{33,1},{2,34},{34,2},{3,35},{35,3},{4,36},{36... | collective-permute-start | bytes 2359304 | tf_op jit(solution)/shard_map/ppermute | solution.py:49
  156.6 25.3 %collective-permute-start.7 = (bf16[32,16,768]{2,1,0:T(8,128)(2,1)}, bf16[32,16,768]{2,1,0:T(8,128)(2,1)}, u32[]{:S(2)}, u32[]{:S(2)}) collective-permute-start(bf16[32,16,768]{2,1,0:T(8,128)(2,1)} %collective-permute-done.3.refs_3_), channel_id=1, source_target_pairs={{0,32},{32,0},{1,33},{33,1},{2,34},{34,2},{3,35},{35,3},{4,36},{36... | collective-permute-start | bytes 2359304 | tf_op jit(solution)/shard_map/ppermute | solution.py:49
  156.6 25.3 %collective-permute-start.6 = (bf16[32,16,768]{2,1,0:T(8,128)(2,1)}, bf16[32,16,768]{2,1,0:T(8,128)(2,1)}, u32[]{:S(2)}, u32[]{:S(2)}) collective-permute-start(bf16[32,16,768]{2,1,0:T(8,128)(2,1)} %collective-permute-done.2.refs_2_), channel_id=1, source_target_pairs={{0,32},{32,0},{1,33},{33,1},{2,34},{34,2},{3,35},{35,3},{4,36},{36... | collective-permute-start | bytes 2359304 | tf_op jit(solution)/shard_map/ppermute | solution.py:49
  157.1 24.8 %collective-permute-start.5 = (bf16[32,16,768]{2,1,0:T(8,128)(2,1)}, bf16[32,16,768]{2,1,0:T(8,128)(2,1)}, u32[]{:S(2)}, u32[]{:S(2)}) collective-permute-start(bf16[32,16,768]{2,1,0:T(8,128)(2,1)} %collective-permute-done.1.refs_1_), channel_id=1, source_target_pairs={{0,32},{32,0},{1,33},{33,1},{2,34},{34,2},{3,35},{35,3},{4,36},{36... | collective-permute-start | bytes 2359304 | tf_op jit(solution)/shard_map/ppermute | solution.py:49
  177.1 26.5 %all-to-all-start.4 = ((bf16[8,64,768]{2,1,0:T(8,128)(2,1)}), bf16[8,64,768]{2,1,0:T(8,128)(2,1)S(1)}, u32[]{:S(2)}, u32[]{:S(2)}) async-start(bf16[8,64,768]{2,1,0:T(8,128)(2,1)} %bitcast.182), calls=%async_computation.4 | async-start | bytes 1572864 | tf_op jit(solution)/shard_map/all_to_all | solution.py:41
  187.7 8.8 %slice-start = ((s8[6291456]{0:T(1024)(128)(4,1)}), s8[4194304]{0:T(1024)(128)(4,1)S(1)}, s32[]{:S(2)}) async-start(s8[6291456]{0:T(1024)(128)(4,1)} %bitcast.179), calls=%async_computation.10 | async-start | bytes 8388608
  190.0 0.9 copy-start.2
  190.1 6.4 %slice-start.1 = ((s8[6291456]{0:T(1024)(128)(4,1)}), s8[2097152]{0:T(1024)(128)(4,1)S(1)}, s32[]{:S(2)}) async-start(s8[6291456]{0:T(1024)(128)(4,1)} %bitcast.179), calls=%async_computation.11 | async-start | bytes 4194304
  203.6 6.8 %copy-start.3 = (bf16[8,64,768]{2,1,0:T(8,128)(2,1)}, bf16[8,64,768]{2,1,0:T(8,128)(2,1)S(1)}, u32[]{:S(2)}) copy-start(bf16[8,64,768]{2,1,0:T(8,128)(2,1)S(1)} %all-to-all-done.4) | copy-start | bytes 2359300
  203.6 26.0 %all-to-all-start.5 = ((bf16[8,64,768]{2,1,0:T(8,128)(2,1)}), bf16[8,64,768]{2,1,0:T(8,128)(2,1)}, u32[]{:S(2)}, u32[]{:S(2)}) async-start(bf16[8,64,768]{2,1,0:T(8,128)(2,1)} %bitcast.181), calls=%async_computation.5 | async-start | bytes 1572864 | tf_op jit(solution)/shard_map/all_to_all | solution.py:41
  210.4 3.7 %copy-start.8 = (bf16[32,4,2,8,768]{4,3,2,1,0:T(8,128)(2,1)}, bf16[32,4,2,8,768]{4,3,2,1,0:T(8,128)(2,1)S(1)}, u32[]{:S(2)}) copy-start(bf16[32,4,2,8,768]{4,3,2,1,0:T(8,128)(2,1)S(1)} %copy.42) | copy-start | bytes 9437188
  229.6 1.1 copy-start.4
  230.7 0.9 copy-start.5
  238.3 6.4 %copy-start.6 = (f32[128,1]{1,0:T(8,128)}, f32[128,1]{1,0:T(8,128)S(1)}, u32[]{:S(2)}) copy-start(f32[128,1]{1,0:T(8,128)S(1)} %get-tuple-element.57) | copy-start | bytes 1540
  238.4 6.5 %collective-permute-start.17 = (bf16[4,4,128,384]{3,2,1,0:T(8,128)(2,1)}, bf16[4,4,128,384]{3,2,1,0:T(8,128)(2,1)S(1)}, u32[]{:S(2)}, u32[]{:S(2)}) collective-permute-start(bf16[4,4,128,384]{3,2,1,0:T(8,128)(2,1)} %get-tuple-element.62), channel_id=1, source_target_pairs={{0,32},{32,0},{1,33},{33,1},{2,34},{34,2},{3,35},{35,3},{4,36},{36... | collective-permute-start | bytes 4718600 | tf_op jit(solution)/shard_map/ppermute | solution.py:49
  239.6 5.2 %copy-start.9 = (bf16[4,4,128,384]{3,2,1,0:T(8,128)(2,1)S(1)}, bf16[4,4,128,384]{3,2,1,0:T(8,128)(2,1)}, u32[]{:S(2)}) copy-start(bf16[4,4,128,384]{3,2,1,0:T(8,128)(2,1)} %get-tuple-element.61) | copy-start | bytes 4718596
  244.8 5.3 %collective-permute-start.13 = (bf16[4,768,256]{2,1,0:T(8,128)(2,1)}, bf16[4,768,256]{2,1,0:T(8,128)(2,1)}, u32[]{:S(2)}, u32[]{:S(2)}) collective-permute-start(bf16[4,768,256]{2,1,0:T(8,128)(2,1)} %get-tuple-element.60), channel_id=1, source_target_pairs={{0,32},{32,0},{1,33},{33,1},{2,34},{34,2},{3,35},{35,3},{4,36},{36... | collective-permute-start | bytes 4718600 | tf_op jit(solution)/shard_map/ppermute | solution.py:49
  246.5 23.9 %all-to-all-start.6 = ((bf16[4,4,128,384]{3,2,1,0:T(8,128)(2,1)}), bf16[4,4,128,384]{3,2,1,0:T(8,128)(2,1)S(1)}, u32[]{:S(2)}, u32[]{:S(2)}) async-start(bf16[4,4,128,384]{3,2,1,0:T(8,128)(2,1)} %add_convert_fusion), calls=%async_computation.6 | async-start | bytes 3145728 | tf_op jit(solution)/shard_map/all_to_all | solution.py:41
  252.8 20.4 %copy-start.10 = (bf16[768,256]{1,0:T(8,128)(2,1)S(1)}, bf16[768,256]{1,0:T(8,128)(2,1)}, u32[]{:S(2)}) copy-start(bf16[768,256]{1,0:T(8,128)(2,1)} %get-tuple-element.63) | copy-start | bytes 1179652
  252.8 20.0 %collective-permute-start.16 = (bf16[768,256]{1,0:T(8,128)(2,1)}, bf16[768,256]{1,0:T(8,128)(2,1)S(1)}, u32[]{:S(2)}, u32[]{:S(2)}) collective-permute-start(bf16[768,256]{1,0:T(8,128)(2,1)} %get-tuple-element.75), channel_id=1, source_target_pairs={{0,192},{64,128},{128,64},{192,0},{1,193},{65,129},{129,65},{193,1... | collective-permute-start | bytes 1179656 | tf_op jit(solution)/shard_map/ppermute | solution.py:49
  253.6 19.2 %collective-permute-start.15 = (bf16[768,256]{1,0:T(8,128)(2,1)}, bf16[768,256]{1,0:T(8,128)(2,1)S(1)}, u32[]{:S(2)}, u32[]{:S(2)}) collective-permute-start(bf16[768,256]{1,0:T(8,128)(2,1)} %get-tuple-element.76), channel_id=1, source_target_pairs={{0,128},{64,192},{128,0},{192,64},{1,129},{65,193},{129,1},{193,65... | collective-permute-start | bytes 1179656 | tf_op jit(solution)/shard_map/ppermute | solution.py:49
  256.1 17.1 %collective-permute-start.14 = (bf16[768,256]{1,0:T(8,128)(2,1)}, bf16[768,256]{1,0:T(8,128)(2,1)S(1)}, u32[]{:S(2)}, u32[]{:S(2)}) collective-permute-start(bf16[768,256]{1,0:T(8,128)(2,1)} %get-tuple-element.77), channel_id=1, source_target_pairs={{0,64},{64,0},{128,192},{192,128},{1,65},{65,1},{129,193},{193,129... | collective-permute-start | bytes 1179656 | tf_op jit(solution)/shard_map/ppermute | solution.py:49
  273.4 7.1 %collective-permute-start.18 = (bf16[8,24,256]{2,1,0:T(8,128)(2,1)S(1)}, bf16[8,24,256]{2,1,0:T(8,128)(2,1)S(1)}, u32[]{:S(2)}, u32[]{:S(2)}) collective-permute-start(bf16[8,24,256]{2,1,0:T(8,128)(2,1)S(1)} %get-tuple-element.91), channel_id=1, source_target_pairs={{0,1},{1,0},{2,3},{3,2},{4,5},{5,4},{6,7},{7,6},{8,9},{9,8},{10,11... | collective-permute-start | bytes 294920 | tf_op jit(solution)/shard_map/ppermute | solution.py:49
  274.6 5.9 %collective-permute-start.20 = (bf16[8,24,256]{2,1,0:T(8,128)(2,1)S(1)}, bf16[8,24,256]{2,1,0:T(8,128)(2,1)S(1)}, u32[]{:S(2)}, u32[]{:S(2)}) collective-permute-start(bf16[8,24,256]{2,1,0:T(8,128)(2,1)S(1)} %get-tuple-element.92), channel_id=1, source_target_pairs={{0,3},{1,2},{2,1},{3,0},{4,7},{5,6},{6,5},{7,4},{8,11},{9,10},{10,... | collective-permute-start | bytes 294920 | tf_op jit(solution)/shard_map/ppermute | solution.py:49
  276.4 6.0 %collective-permute-start.19 = (bf16[8,24,256]{2,1,0:T(8,128)(2,1)S(1)}, bf16[8,24,256]{2,1,0:T(8,128)(2,1)S(1)}, u32[]{:S(2)}, u32[]{:S(2)}) collective-permute-start(bf16[8,24,256]{2,1,0:T(8,128)(2,1)S(1)} %get-tuple-element.93), channel_id=1, source_target_pairs={{0,2},{1,3},{2,0},{3,1},{4,6},{5,7},{6,4},{7,5},{8,10},{9,11},{10,... | collective-permute-start | bytes 294920 | tf_op jit(solution)/shard_map/ppermute | solution.py:49
  277.0 9.7 %all-to-all-start.7 = ((bf16[4,128,384]{2,1,0:T(8,128)(2,1)}), bf16[4,128,384]{2,1,0:T(8,128)(2,1)S(1)}, u32[]{:S(2)}, u32[]{:S(2)}) async-start(bf16[4,128,384]{2,1,0:T(8,128)(2,1)} %fusion.19), calls=%async_computation.7 | async-start | bytes 786432 | tf_op jit(solution)/shard_map/all_to_all | solution.py:41
  280.5 26.6 %copy-start.7 = (f32[128,1]{1,0:T(8,128)S(1)}, f32[128,1]{1,0:T(8,128)}, u32[]{:S(2)}) copy-start(f32[128,1]{1,0:T(8,128)} %copy-done.6) | copy-start | bytes 1540
  298.8 16.4 %all-to-all-start.9 = ((f32[8,96,128]{2,1,0:T(8,128)}), f32[8,96,128]{2,1,0:T(8,128)S(1)}, u32[]{:S(2)}, u32[]{:S(2)}) async-start(f32[8,96,128]{2,1,0:T(8,128)} %broadcast_in_dim.126), calls=%async_computation.9 | async-start | bytes 786432 | tf_op jit(solution)/shard_map/all_to_all | solution.py:41
  315.2 0.9 copy-start.1
  315.4 0.7 copy-start.13

commit v2 on v1

--- a/solution.py
+++ b/solution.py
@@ -209,15 +209,14 @@
     (found_10,) = find([(1, 0)])
     near_10 = swap(found_10, "y", 1)
     gathered = spread(after(piece, found_10), ("z", "y"), SHARD)
-    found_00, found_11 = find([(0, 0), (1, 1)], found_10)
-    near_11 = swap(found_11, "y", 1)
+    found_00, found_01 = find([(0, 0), (0, 1)], found_10)
+    found_11, found_30, found_20 = find([(1, 1), (3, 0), (2, 0)], found_00, found_01)
+    near_11, near_30, near_20 = swap(found_11, "y", 1), swap(found_30, "y", 3), swap(found_20, "y", 2)
     own_0 = after(found_00 + after(near_10, found_11), gathered)
     rows_0 = exchange(own_0, "z")
-    found_30, found_01, found_20 = find([(3, 0), (0, 1), (2, 0)], own_0)
-    near_30, near_20 = swap(found_30, "y", 3), swap(found_20, "y", 2)
     gathered = after(gathered, own_0)
     parts = [gathered] + [swap(gathered, "x", by) for by in range(1, X)]
-    found_31, found_21 = find([(3, 1), (2, 1)], found_30)
+    found_31, found_21 = find([(3, 1), (2, 1)], own_0, near_11)
     near_31, near_21 = swap(found_31, "y", 3), swap(found_21, "y", 2)
     own_1 = found_01 + near_11
     rows_1 = exchange(

time: 318 us -> 297 us (0.934)
  waiting for transfers between devices: 123 us -> 93.5 us
  starting transfers between devices: 76.4 us -> 85.8 us
    ppermute x21, waiting for transfers between devices: 68.1 us -> 45.2 us  [swap(): lax.ppermute(value, axis, [(i, i ^ by) for i in range(lax.axis_size(axis))])]
    ppermute x21, starting transfers between devices: 21.6 us -> 30 us  [swap(): lax.ppermute(value, axis, [(i, i ^ by) for i in range(lax.axis_size(axis))])]
    all_to_all x9, waiting for transfers between devices: 55.1 us -> 48.3 us  [exchange(): return lax.all_to_all(value, axes, split_axis=0, concat_axis=0, tiled=True)]
  transfers between devices with their start and end apart: 30 -> 30, of which waited for: 13 -> 15; matrix products, arithmetic and copies ran while one was open for 21% -> 22% of each run, Pallas kernels for 3% -> 4%
where the time goes in v2:
time: 297 us; the launch traced here: 295 us
  waiting for transfers between devices  93.5 us (31%)
  starting transfers between devices  85.8 us (29%)
  local copies, waits for them, and re-layouts  48.1 us (16%)
  other arithmetic  24.3 us (8%)
  Pallas kernels  23.4 us (8%)
  blocking collectives  11.1 us (4%)
  matrix products  7.9 us (3%)
    all_to_all x9, starting transfers between devices, exchange(): return lax.all_to_all(value, axes, split_axis=0, concat_axis=0, tiled=True)  55.8 us
    all_to_all x9, waiting for transfers between devices, exchange(): return lax.all_to_all(value, axes, split_axis=0, concat_axis=0, tiled=True)  48.3 us
    ppermute x21, waiting for transfers between devices, swap(): lax.ppermute(value, axis, [(i, i ^ by) for i in range(lax.axis_size(axis))])  45.2 us
    gather x4, local copies, waits for them, and re-layouts, find(): passage_table.at[ids].get(mode='promise_in_bounds')  32.9 us
    ppermute x21, starting transfers between devices, swap(): lax.ppermute(value, axis, [(i, i ^ by) for i in range(lax.axis_size(axis))])  30 us
    all_to_all x1, blocking collectives, exchange(): return lax.all_to_all(value, axes, split_axis=0, concat_axis=0, tiled=True)  11.1 us
    dot_general x8, matrix products, shards(): jnp.dot(queries, part, preferred_element_type=jnp.float32)  7.31 us
    select_n x4, other arithmetic, find(): jnp.where(own[by, :, cuts[part]].reshape(-1, 1), found[i], jnp.zeros((),...  7.03 us
  transfers between devices with their start and end apart: 30, of which 15 were waited for; matrix products, arithmetic and copies ran while one was open for 22% of the time, Pallas kernels for 4%

profile of v2, /device:TPU:1, one launch (start us, length us, event | category | flops | bytes accessed | tf_op | source)
XLA Modules:
  0.0 295.3 jit_solution(13134059561605895104)
XLA Ops:
  1.5 5.8 %shard_map.85 = (s32[16,128]{1,0:T(8,128)S(1)}, s32[16,128]{1,0:T(8,128)S(1)}) custom-call(s32[128,16]{1,0:T(8,128)S(1)} %copy.33.ids_ref), custom_call_target="tpu_custom_call" | custom-call | tf_op jit(solution)/shard_map/pallas_call | solution.py:182
  7.9 12.0 %all-to-all-start = ((s32[32,1,128]{2,1,0:T(1,128)}), s32[32,1,128]{2,1,0:T(1,128)S(1)}, u32[]{:S(2)}, u32[]{:S(2)}) async-start(s32[32,1,128]{2,1,0:T(1,128)} %bitcast.2), calls=%async_computation | async-start | bytes 32768 | tf_op jit(solution)/shard_map/all_to_all | solution.py:41
  20.8 7.7 %all-to-all-done = s32[32,1,128]{2,1,0:T(1,128)S(1)} async-done(((s32[32,1,128]{2,1,0:T(1,128)}), s32[32,1,128]{2,1,0:T(1,128)S(1)}, u32[]{:S(2)}, u32[]{:S(2)}) %all-to-all-start) | async-done | bytes 16416 | tf_op jit(solution)/shard_map/all_to_all | solution.py:41
  28.9 6.0 %gather_fusion = bf16[512,768]{1,0:T(8,128)(2,1)S(1)} fusion(bf16[4096,768]{1,0:T(8,128)(2,1)} %param.9, s32[1024]{0:T(1024)S(1)} %pad_clamp_fusion.1), kind=kCustom, calls=%fused_computation | custom fusion | bytes 1574912 | tf_op jit(solution)/shard_map/gather | solution.py:198
  36.9 3.9 %all-to-all-start.1 = ((bf16[32,16,768]{2,1,0:T(8,128)(2,1)}), bf16[32,16,768]{2,1,0:T(8,128)(2,1)S(1)}, u32[]{:S(2)}, u32[]{:S(2)}) async-start(bf16[32,16,768]{2,1,0:T(8,128)(2,1)} %broadcast_in_dim.107), calls=%async_computation.1 | async-start | bytes 1572864 | tf_op jit(solution)/shard_map/all_to_all | solution.py:41
  42.3 8.1 %gather_fusion.1 = bf16[1024,768]{1,0:T(8,128)(2,1)S(1)} fusion(bf16[4096,768]{1,0:T(8,128)(2,1)} %param.9, s32[1024]{0:T(1024)S(1)} %fusion.37), kind=kCustom, calls=%fused_computation.1 | custom fusion | bytes 3149824 | tf_op jit(solution)/shard_map/gather | solution.py:198
  50.3 1.4 slice_select_fusion.5
  52.0 9.7 %gather_fusion.2 = bf16[1536,768]{1,0:T(8,128)(2,1)S(1)} fusion(bf16[4096,768]{1,0:T(8,128)(2,1)} %param.9, s32[2048]{0:T(1024)S(1)} %pad_clamp_fusion), kind=kCustom, calls=%fused_computation.2 | custom fusion | bytes 4724736 | tf_op jit(solution)/shard_map/gather | solution.py:198
  61.7 1.7 slice_select_fusion.2
  63.8 2.5 collective-permute-done
  66.3 2.2 add.181
  68.5 7.5 %all-to-all-start.2 = ((bf16[8,64,768]{2,1,0:T(8,128)(2,1)}), bf16[8,64,768]{2,1,0:T(8,128)(2,1)S(1)}, u32[]{:S(2)}, u32[]{:S(2)}) async-start(bf16[8,64,768]{2,1,0:T(8,128)(2,1)} %bitcast.8), calls=%async_computation.2 | async-start | bytes 1572864 | tf_op jit(solution)/shard_map/all_to_all | solution.py:41
  76.0 2.5 collective-permute-start.10
  79.5 2.5 collective-permute-start.3
  83.3 2.7 collective-permute-start.2
  86.0 9.2 %gather_fusion.3 = bf16[1024,768]{1,0:T(8,128)(2,1)} fusion(bf16[4096,768]{1,0:T(8,128)(2,1)} %param.9, s32[1024]{0:T(1024)S(1)} %fusion.38), kind=kCustom, calls=%fused_computation.3 | custom fusion | bytes 3149824 | tf_op jit(solution)/shard_map/gather | solution.py:198
  95.2 2.9 slice_select_fusion
  98.1 4.1 %collective-permute-done.10 = bf16[512,768]{1,0:T(8,128)(2,1)S(1)} collective-permute-done((bf16[512,768]{1,0:T(8,128)(2,1)}, bf16[512,768]{1,0:T(8,128)(2,1)S(1)}, u32[]{:S(2)}, u32[]{:S(2)}) %collective-permute-start.10) | collective-permute-done | bytes 786464 | tf_op jit(solution)/shard_map/ppermute | solution.py:49
  104.4 26.2 %collective-permute-done.9 = bf16[512,768]{1,0:T(8,128)(2,1)} collective-permute-done((bf16[512,768]{1,0:T(8,128)(2,1)}, bf16[512,768]{1,0:T(8,128)(2,1)}, u32[]{:S(2)}, u32[]{:S(2)}) %collective-permute-start.9) | collective-permute-done | bytes 786464 | tf_op jit(solution)/shard_map/ppermute | solution.py:49
  130.7 6.4 %all-to-all-start.3 = ((bf16[8,64,768]{2,1,0:T(8,128)(2,1)}), bf16[8,64,768]{2,1,0:T(8,128)(2,1)S(1)}, u32[]{:S(2)}, u32[]{:S(2)}) async-start(bf16[8,64,768]{2,1,0:T(8,128)(2,1)} %bitcast.10), calls=%async_computation.3 | async-start | bytes 1572864 | tf_op jit(solution)/shard_map/all_to_all | solution.py:41
  137.5 4.4 %collective-permute-start.4 = (bf16[32,16,768]{2,1,0:T(8,128)(2,1)S(1)}, bf16[32,16,768]{2,1,0:T(8,128)(2,1)}, u32[]{:S(2)}, u32[]{:S(2)}) collective-permute-start(bf16[32,16,768]{2,1,0:T(8,128)(2,1)S(1)} %all-to-all-done.1.refs_0_), channel_id=1, source_target_pairs={{0,32},{32,0},{1,33},{33,1},{2,34},{34,2},{3,35},{35,3},{4,36},{36... | collective-permute-start | bytes 2359304 | tf_op jit(solution)/shard_map/ppermute | solution.py:49
  143.0 2.4 add.187
  145.5 8.0 %collective-permute-done.12 = bf16[512,768]{1,0:T(8,128)(2,1)S(1)} collective-permute-done((bf16[512,768]{1,0:T(8,128)(2,1)}, bf16[512,768]{1,0:T(8,128)(2,1)S(1)}, u32[]{:S(2)}, u32[]{:S(2)}) %collective-permute-start.12) | collective-permute-done | bytes 786464 | tf_op jit(solution)/shard_map/ppermute | solution.py:49
  153.4 2.2 add.184
  157.0 5.1 %all-to-all-start.4 = ((bf16[8,64,768]{2,1,0:T(8,128)(2,1)}), bf16[8,64,768]{2,1,0:T(8,128)(2,1)S(1)}, u32[]{:S(2)}, u32[]{:S(2)}) async-start(bf16[8,64,768]{2,1,0:T(8,128)(2,1)} %bitcast.182), calls=%async_computation.4 | async-start | bytes 1572864 | tf_op jit(solution)/shard_map/all_to_all | solution.py:41
  162.1 5.7 %shard_map.86 = bf16[4,2,32,16,768]{4,3,2,1,0:T(8,128)(2,1)} custom-call(s32[2]{0:T(128)S(1)} %pad_add_fusion.5.place_ref, bf16[32,16,768]{2,1,0:T(8,128)(2,1)S(1)} %all-to-all-done.1.refs_0_, bf16[32,16,768]{2,1,0:T(8,128)(2,1)} %collective-permute-done.1.refs_1_, bf16[32,16,768]{2,1,0:T(8,128)(2,1)} %collective-permute-done.2.refs_2_, ...), custom_call_target="tpu_custom_call" | custom-call | tf_op jit(solution)/shard_map/pallas_call | solution.py:230
  167.8 2.2 slice_bitcast_fusion.1
  176.6 2.0 slice_bitcast_fusion
  178.6 1.6 all-to-all-done.4
  180.2 5.0 %all-to-all-start.5 = ((bf16[8,64,768]{2,1,0:T(8,128)(2,1)}), bf16[8,64,768]{2,1,0:T(8,128)(2,1)}, u32[]{:S(2)}, u32[]{:S(2)}) async-start(bf16[8,64,768]{2,1,0:T(8,128)(2,1)} %bitcast.181), calls=%async_computation.5 | async-start | bytes 1572864 | tf_op jit(solution)/shard_map/all_to_all | solution.py:41
  185.2 2.3 copy.42
  189.5 1.7 fusion.12
  191.8 11.1 %all-to-all-done.5 = bf16[8,64,768]{2,1,0:T(8,128)(2,1)} async-done(((bf16[8,64,768]{2,1,0:T(8,128)(2,1)}), bf16[8,64,768]{2,1,0:T(8,128)(2,1)}, u32[]{:S(2)}, u32[]{:S(2)}) %all-to-all-start.5) | async-done | bytes 786464 | tf_op jit(solution)/shard_map/all_to_all | solution.py:41
  205.0 6.7 %shard_map.87 = (f32[128,1]{1,0:T(8,128)S(1)}, bf16[128,768]{1,0:T(8,128)(2,1)S(1)}, bf16[4,4,128,384]{3,2,1,0:T(8,128)(2,1)}, bf16[4,4,128,384]{3,2,1,0:T(8,128)(2,1)}) custom-call(s32[2]{0:T(128)S(1)} %pad_add_fusion.5.place_ref, bf16[128,768]{1,0:T(8,128)(2,1)S(1)} %fusion.embedded_ref, bf16[128,768]{1,0:T(8,128)(2,1)S(1)} %copy-done.5, ...), custom_call_target="tpu_custom_call" | custom-call | tf_op jit(solution)/shard_map/pallas_call | solution.py:258
  211.7 6.5 %collective-permute-start.17 = (bf16[4,4,128,384]{3,2,1,0:T(8,128)(2,1)}, bf16[4,4,128,384]{3,2,1,0:T(8,128)(2,1)S(1)}, u32[]{:S(2)}, u32[]{:S(2)}) collective-permute-start(bf16[4,4,128,384]{3,2,1,0:T(8,128)(2,1)} %get-tuple-element.62), channel_id=1, source_target_pairs={{0,32},{32,0},{1,33},{33,1},{2,34},{34,2},{3,35},{35,3},{4,36},{36... | collective-permute-start | bytes 4718600 | tf_op jit(solution)/shard_map/ppermute | solution.py:49
  218.2 5.2 %shard_map.88 = (bf16[4,768,256]{2,1,0:T(8,128)(2,1)S(1)}, bf16[4,768,256]{2,1,0:T(8,128)(2,1)}) custom-call(s32[2]{0:T(128)S(1)} %pad_add_fusion.5.place_ref, bf16[128,768]{1,0:T(8,128)(2,1)S(1)} %copy-done.2, bf16[128,768]{1,0:T(8,128)(2,1)S(1)} %get-tuple-element.58.grad_ref, f32[128,2048]{1,0:T(8,128)S(1)} %get-tuple-element.86.slope_ref, ...), custom_call_target="tpu_custom_call" | custom-call | tf_op jit(solution)/shard_map/pallas_call | solution.py:270
  223.4 1.7 add_convert_fusion
  225.1 3.6 %all-to-all-start.6 = ((bf16[4,4,128,384]{3,2,1,0:T(8,128)(2,1)}), bf16[4,4,128,384]{3,2,1,0:T(8,128)(2,1)S(1)}, u32[]{:S(2)}, u32[]{:S(2)}) async-start(bf16[4,4,128,384]{3,2,1,0:T(8,128)(2,1)} %add_convert_fusion), calls=%async_computation.6 | async-start | bytes 3145728 | tf_op jit(solution)/shard_map/all_to_all | solution.py:41
  228.7 2.8 fusion.16
  231.4 2.5 collective-permute-start.16
  234.7 14.3 %all-to-all-done.6 = bf16[4,4,128,384]{3,2,1,0:T(8,128)(2,1)S(1)} async-done(((bf16[4,4,128,384]{3,2,1,0:T(8,128)(2,1)}), bf16[4,4,128,384]{3,2,1,0:T(8,128)(2,1)S(1)}, u32[]{:S(2)}, u32[]{:S(2)}) %all-to-all-start.6) | async-done | bytes 1572896 | tf_op jit(solution)/shard_map/all_to_all | solution.py:41
  249.9 1.5 collective-permute-done.16
  253.2 1.8 collective-permute-start.20
  255.6 4.1 %all-to-all-start.7 = ((bf16[4,128,384]{2,1,0:T(8,128)(2,1)}), bf16[4,128,384]{2,1,0:T(8,128)(2,1)S(1)}, u32[]{:S(2)}, u32[]{:S(2)}) async-start(bf16[4,128,384]{2,1,0:T(8,128)(2,1)} %fusion.17), calls=%async_computation.7 | async-start | bytes 786432 | tf_op jit(solution)/shard_map/all_to_all | solution.py:41
  261.1 4.8 %all-to-all-done.7 = bf16[4,128,384]{2,1,0:T(8,128)(2,1)S(1)} async-done(((bf16[4,128,384]{2,1,0:T(8,128)(2,1)}), bf16[4,128,384]{2,1,0:T(8,128)(2,1)S(1)}, u32[]{:S(2)}, u32[]{:S(2)}) %all-to-all-start.7) | async-done | bytes 393248 | tf_op jit(solution)/shard_map/all_to_all | solution.py:41
  266.0 11.1 %all_to_all.78 = bf16[8,96,128]{2,1,0:T(8,128)(2,1)S(1)} all-to-all(bf16[8,96,128]{2,1,0:T(8,128)(2,1)S(1)} %constant_dynamic-update-slice_fusion), channel_id=1, replica_groups=mesh['x'=4,'core'=2,'z'=8,'y'=4] {'z'}, dimensions={0} | all-to-all | bytes 393216 | tf_op jit(solution)/shard_map/all_to_all | solution.py:41
  278.0 8.3 %all-to-all-start.9 = ((f32[8,96,128]{2,1,0:T(8,128)}), f32[8,96,128]{2,1,0:T(8,128)S(1)}, u32[]{:S(2)}, u32[]{:S(2)}) async-start(f32[8,96,128]{2,1,0:T(8,128)} %broadcast_in_dim.126), calls=%async_computation.9 | async-start | bytes 786432 | tf_op jit(solution)/shard_map/all_to_all | solution.py:41
  286.9 7.5 %all-to-all-done.9 = f32[8,96,128]{2,1,0:T(8,128)S(1)} async-done(((f32[8,96,128]{2,1,0:T(8,128)}), f32[8,96,128]{2,1,0:T(8,128)S(1)}, u32[]{:S(2)}, u32[]{:S(2)}) %all-to-all-start.9) | async-done | bytes 393248 | tf_op jit(solution)/shard_map/all_to_all | solution.py:41
  (167 shorter events, 33.2 us)
Async XLA Ops:
  0.6 19.4 %copy-start = (bf16[64,768]{1,0:T(8,128)(2,1)S(1)}, bf16[64,768]{1,0:T(8,128)(2,1)}, u32[]{:S(2)}) copy-start(bf16[64,768]{1,0:T(8,128)(2,1)} %param.11) | copy-start | bytes 294916
  7.9 20.6 %all-to-all-start = ((s32[32,1,128]{2,1,0:T(1,128)}), s32[32,1,128]{2,1,0:T(1,128)S(1)}, u32[]{:S(2)}, u32[]{:S(2)}) async-start(s32[32,1,128]{2,1,0:T(1,128)} %bitcast.2), calls=%async_computation | async-start | bytes 32768 | tf_op jit(solution)/shard_map/all_to_all | solution.py:41
  36.9 31.7 %all-to-all-start.1 = ((bf16[32,16,768]{2,1,0:T(8,128)(2,1)}), bf16[32,16,768]{2,1,0:T(8,128)(2,1)S(1)}, u32[]{:S(2)}, u32[]{:S(2)}) async-start(bf16[32,16,768]{2,1,0:T(8,128)(2,1)} %broadcast_in_dim.107), calls=%async_computation.1 | async-start | bytes 1572864 | tf_op jit(solution)/shard_map/all_to_all | solution.py:41
  40.8 25.5 %collective-permute-start = (bf16[512,768]{1,0:T(8,128)(2,1)}, bf16[512,768]{1,0:T(8,128)(2,1)}, u32[]{:S(2)}, u32[]{:S(2)}) collective-permute-start(bf16[512,768]{1,0:T(8,128)(2,1)} %broadcast_select_fusion), channel_id=1, source_target_pairs={{0,1},{1,0},{2,3},{3,2},{4,5},{5,4},{6,7},{7,6},{8,9},{9,8},{10,11... | collective-permute-start | bytes 2359304 | tf_op jit(solution)/shard_map/ppermute | solution.py:49
  61.7 4.6 %copy-start.10 = (bf16[512,768]{1,0:T(8,128)(2,1)S(1)}, bf16[512,768]{1,0:T(8,128)(2,1)}, u32[]{:S(2)}) copy-start(bf16[512,768]{1,0:T(8,128)(2,1)} %get-tuple-element.85) | copy-start | bytes 2359300
  63.4 19.8 %collective-permute-start.8 = (bf16[512,768]{1,0:T(8,128)(2,1)}, bf16[512,768]{1,0:T(8,128)(2,1)S(1)}, u32[]{:S(2)}, u32[]{:S(2)}) collective-permute-start(bf16[512,768]{1,0:T(8,128)(2,1)} %get-tuple-element.81), channel_id=1, source_target_pairs={{0,1},{1,0},{2,3},{3,2},{4,5},{5,4},{6,7},{7,6},{8,9},{9,8},{10,11... | collective-permute-start | bytes 2359304 | tf_op jit(solution)/shard_map/ppermute | solution.py:49
  68.5 62.1 %all-to-all-start.2 = ((bf16[8,64,768]{2,1,0:T(8,128)(2,1)}), bf16[8,64,768]{2,1,0:T(8,128)(2,1)S(1)}, u32[]{:S(2)}, u32[]{:S(2)}) async-start(bf16[8,64,768]{2,1,0:T(8,128)(2,1)} %bitcast.8), calls=%async_computation.2 | async-start | bytes 1572864 | tf_op jit(solution)/shard_map/all_to_all | solution.py:41
  76.0 26.2 %collective-permute-start.10 = (bf16[512,768]{1,0:T(8,128)(2,1)}, bf16[512,768]{1,0:T(8,128)(2,1)S(1)}, u32[]{:S(2)}, u32[]{:S(2)}) collective-permute-start(bf16[512,768]{1,0:T(8,128)(2,1)} %get-tuple-element.79), channel_id=1, source_target_pairs={{0,2},{1,3},{2,0},{3,1},{4,6},{5,7},{6,4},{7,5},{8,10},{9,11},{10,... | collective-permute-start | bytes 2359304 | tf_op jit(solution)/shard_map/ppermute | solution.py:49
  78.7 51.9 %collective-permute-start.9 = (bf16[512,768]{1,0:T(8,128)(2,1)}, bf16[512,768]{1,0:T(8,128)(2,1)}, u32[]{:S(2)}, u32[]{:S(2)}) collective-permute-start(bf16[512,768]{1,0:T(8,128)(2,1)} %get-tuple-element.80), channel_id=1, source_target_pairs={{0,3},{1,2},{2,1},{3,0},{4,7},{5,6},{6,5},{7,4},{8,11},{9,10},{10,... | collective-permute-start | bytes 2359304 | tf_op jit(solution)/shard_map/ppermute | solution.py:49
  79.5 51.1 %collective-permute-start.3 = (bf16[32,16,768]{2,1,0:T(8,128)(2,1)S(1)}, bf16[32,16,768]{2,1,0:T(8,128)(2,1)}, u32[]{:S(2)}, u32[]{:S(2)}) collective-permute-start(bf16[32,16,768]{2,1,0:T(8,128)(2,1)S(1)} %all-to-all-done.1.refs_0_), channel_id=1, source_target_pairs={{0,192},{64,128},{128,64},{192,0},{1,193},{65,129},{129,65},{193,1... | collective-permute-start | bytes 2359304 | tf_op jit(solution)/shard_map/ppermute | solution.py:49
  82.0 48.6 %collective-permute-start.1 = (bf16[32,16,768]{2,1,0:T(8,128)(2,1)S(1)}, bf16[32,16,768]{2,1,0:T(8,128)(2,1)}, u32[]{:S(2)}, u32[]{:S(2)}) collective-permute-start(bf16[32,16,768]{2,1,0:T(8,128)(2,1)S(1)} %all-to-all-done.1.refs_0_), channel_id=1, source_target_pairs={{0,64},{64,0},{128,192},{192,128},{1,65},{65,1},{129,193},{193,129... | collective-permute-start | bytes 2359304 | tf_op jit(solution)/shard_map/ppermute | solution.py:49
  83.3 2.8 copy-start.14
  83.3 58.7 %collective-permute-start.2 = (bf16[32,16,768]{2,1,0:T(8,128)(2,1)S(1)}, bf16[32,16,768]{2,1,0:T(8,128)(2,1)}, u32[]{:S(2)}, u32[]{:S(2)}) collective-permute-start(bf16[32,16,768]{2,1,0:T(8,128)(2,1)S(1)} %all-to-all-done.1.refs_0_), channel_id=1, source_target_pairs={{0,128},{64,192},{128,0},{192,64},{1,129},{65,193},{129,1},{193,65... | collective-permute-start | bytes 2359304 | tf_op jit(solution)/shard_map/ppermute | solution.py:49
  95.2 8.1 %copy-start.9 = (bf16[512,768]{1,0:T(8,128)(2,1)S(1)}, bf16[512,768]{1,0:T(8,128)(2,1)}, u32[]{:S(2)}) copy-start(bf16[512,768]{1,0:T(8,128)(2,1)} %get-tuple-element.84) | copy-start | bytes 2359300
  95.2 8.1 %copy-start.15 = (bf16[512,768]{1,0:T(8,128)(2,1)S(1)}, bf16[512,768]{1,0:T(8,128)(2,1)}, u32[]{:S(2)}) copy-start(bf16[512,768]{1,0:T(8,128)(2,1)} %copy-done.14) | copy-start | bytes 2359300
  102.2 28.4 %copy-start.13 = (bf16[512,768]{1,0:T(8,128)(2,1)}, bf16[512,768]{1,0:T(8,128)(2,1)S(1)}, u32[]{:S(2)}) copy-start(bf16[512,768]{1,0:T(8,128)(2,1)S(1)} %collective-permute-done.10) | copy-start | bytes 2359300
  102.2 40.2 %collective-permute-start.11 = (bf16[512,768]{1,0:T(8,128)(2,1)}, bf16[512,768]{1,0:T(8,128)(2,1)}, u32[]{:S(2)}, u32[]{:S(2)}) collective-permute-start(bf16[512,768]{1,0:T(8,128)(2,1)} %get-tuple-element.82), channel_id=1, source_target_pairs={{0,2},{1,3},{2,0},{3,1},{4,6},{5,7},{6,4},{7,5},{8,10},{9,11},{10,... | collective-permute-start | bytes 2359304 | tf_op jit(solution)/shard_map/ppermute | solution.py:49
  130.7 26.3 %all-to-all-start.3 = ((bf16[8,64,768]{2,1,0:T(8,128)(2,1)}), bf16[8,64,768]{2,1,0:T(8,128)(2,1)S(1)}, u32[]{:S(2)}, u32[]{:S(2)}) async-start(bf16[8,64,768]{2,1,0:T(8,128)(2,1)} %bitcast.10), calls=%async_computation.3 | async-start | bytes 1572864 | tf_op jit(solution)/shard_map/all_to_all | solution.py:41
  137.0 16.4 %collective-permute-start.12 = (bf16[512,768]{1,0:T(8,128)(2,1)}, bf16[512,768]{1,0:T(8,128)(2,1)S(1)}, u32[]{:S(2)}, u32[]{:S(2)}) collective-permute-start(bf16[512,768]{1,0:T(8,128)(2,1)} %get-tuple-element.83), channel_id=1, source_target_pairs={{0,3},{1,2},{2,1},{3,0},{4,7},{5,6},{6,5},{7,4},{8,11},{9,10},{10,... | collective-permute-start | bytes 2359304 | tf_op jit(solution)/shard_map/ppermute | solution.py:49
  137.5 24.5 %collective-permute-start.4 = (bf16[32,16,768]{2,1,0:T(8,128)(2,1)S(1)}, bf16[32,16,768]{2,1,0:T(8,128)(2,1)}, u32[]{:S(2)}, u32[]{:S(2)}) collective-permute-start(bf16[32,16,768]{2,1,0:T(8,128)(2,1)S(1)} %all-to-all-done.1.refs_0_), channel_id=1, source_target_pairs={{0,32},{32,0},{1,33},{33,1},{2,34},{34,2},{3,35},{35,3},{4,36},{36... | collective-permute-start | bytes 2359304 | tf_op jit(solution)/shard_map/ppermute | solution.py:49
  141.9 20.1 %collective-permute-start.7 = (bf16[32,16,768]{2,1,0:T(8,128)(2,1)}, bf16[32,16,768]{2,1,0:T(8,128)(2,1)}, u32[]{:S(2)}, u32[]{:S(2)}) collective-permute-start(bf16[32,16,768]{2,1,0:T(8,128)(2,1)} %collective-permute-done.3.refs_3_), channel_id=1, source_target_pairs={{0,32},{32,0},{1,33},{33,1},{2,34},{34,2},{3,35},{35,3},{4,36},{36... | collective-permute-start | bytes 2359304 | tf_op jit(solution)/shard_map/ppermute | solution.py:49
  141.9 20.1 %collective-permute-start.6 = (bf16[32,16,768]{2,1,0:T(8,128)(2,1)}, bf16[32,16,768]{2,1,0:T(8,128)(2,1)}, u32[]{:S(2)}, u32[]{:S(2)}) collective-permute-start(bf16[32,16,768]{2,1,0:T(8,128)(2,1)} %collective-permute-done.2.refs_2_), channel_id=1, source_target_pairs={{0,32},{32,0},{1,33},{33,1},{2,34},{34,2},{3,35},{35,3},{4,36},{36... | collective-permute-start | bytes 2359304 | tf_op jit(solution)/shard_map/ppermute | solution.py:49
  142.5 19.6 %collective-permute-start.5 = (bf16[32,16,768]{2,1,0:T(8,128)(2,1)}, bf16[32,16,768]{2,1,0:T(8,128)(2,1)}, u32[]{:S(2)}, u32[]{:S(2)}) collective-permute-start(bf16[32,16,768]{2,1,0:T(8,128)(2,1)} %collective-permute-done.1.refs_1_), channel_id=1, source_target_pairs={{0,32},{32,0},{1,33},{33,1},{2,34},{34,2},{3,35},{35,3},{4,36},{36... | collective-permute-start | bytes 2359304 | tf_op jit(solution)/shard_map/ppermute | solution.py:49
  157.0 23.2 %all-to-all-start.4 = ((bf16[8,64,768]{2,1,0:T(8,128)(2,1)}), bf16[8,64,768]{2,1,0:T(8,128)(2,1)S(1)}, u32[]{:S(2)}, u32[]{:S(2)}) async-start(bf16[8,64,768]{2,1,0:T(8,128)(2,1)} %bitcast.182), calls=%async_computation.4 | async-start | bytes 1572864 | tf_op jit(solution)/shard_map/all_to_all | solution.py:41
  167.8 8.8 %slice-start = ((s8[6291456]{0:T(1024)(128)(4,1)}), s8[4194304]{0:T(1024)(128)(4,1)S(1)}, s32[]{:S(2)}) async-start(s8[6291456]{0:T(1024)(128)(4,1)} %bitcast.179), calls=%async_computation.10 | async-start | bytes 8388608
  170.1 0.9 copy-start.2
  170.2 6.4 %slice-start.1 = ((s8[6291456]{0:T(1024)(128)(4,1)}), s8[2097152]{0:T(1024)(128)(4,1)S(1)}, s32[]{:S(2)}) async-start(s8[6291456]{0:T(1024)(128)(4,1)} %bitcast.179), calls=%async_computation.11 | async-start | bytes 4194304
  180.2 7.3 %copy-start.3 = (bf16[8,64,768]{2,1,0:T(8,128)(2,1)}, bf16[8,64,768]{2,1,0:T(8,128)(2,1)S(1)}, u32[]{:S(2)}) copy-start(bf16[8,64,768]{2,1,0:T(8,128)(2,1)S(1)} %all-to-all-done.4) | copy-start | bytes 2359300
  180.2 22.8 %all-to-all-start.5 = ((bf16[8,64,768]{2,1,0:T(8,128)(2,1)}), bf16[8,64,768]{2,1,0:T(8,128)(2,1)}, u32[]{:S(2)}, u32[]{:S(2)}) async-start(bf16[8,64,768]{2,1,0:T(8,128)(2,1)} %bitcast.181), calls=%async_computation.5 | async-start | bytes 1572864 | tf_op jit(solution)/shard_map/all_to_all | solution.py:41
  187.5 3.7 %copy-start.8 = (bf16[32,4,2,8,768]{4,3,2,1,0:T(8,128)(2,1)}, bf16[32,4,2,8,768]{4,3,2,1,0:T(8,128)(2,1)S(1)}, u32[]{:S(2)}) copy-start(bf16[32,4,2,8,768]{4,3,2,1,0:T(8,128)(2,1)S(1)} %copy.42) | copy-start | bytes 9437188
  203.0 1.1 copy-start.4
  204.1 0.9 copy-start.5
  211.7 11.7 %copy-start.6 = (f32[128,1]{1,0:T(8,128)}, f32[128,1]{1,0:T(8,128)S(1)}, u32[]{:S(2)}) copy-start(f32[128,1]{1,0:T(8,128)S(1)} %get-tuple-element.57) | copy-start | bytes 1540
  211.7 11.7 %collective-permute-start.17 = (bf16[4,4,128,384]{3,2,1,0:T(8,128)(2,1)}, bf16[4,4,128,384]{3,2,1,0:T(8,128)(2,1)S(1)}, u32[]{:S(2)}, u32[]{:S(2)}) collective-permute-start(bf16[4,4,128,384]{3,2,1,0:T(8,128)(2,1)} %get-tuple-element.62), channel_id=1, source_target_pairs={{0,32},{32,0},{1,33},{33,1},{2,34},{34,2},{3,35},{35,3},{4,36},{36... | collective-permute-start | bytes 4718600 | tf_op jit(solution)/shard_map/ppermute | solution.py:49
  218.2 5.2 %copy-start.11 = (bf16[4,4,128,384]{3,2,1,0:T(8,128)(2,1)S(1)}, bf16[4,4,128,384]{3,2,1,0:T(8,128)(2,1)}, u32[]{:S(2)}) copy-start(bf16[4,4,128,384]{3,2,1,0:T(8,128)(2,1)} %get-tuple-element.61) | copy-start | bytes 4718596
  223.4 5.2 %collective-permute-start.13 = (bf16[4,768,256]{2,1,0:T(8,128)(2,1)}, bf16[4,768,256]{2,1,0:T(8,128)(2,1)}, u32[]{:S(2)}, u32[]{:S(2)}) collective-permute-start(bf16[4,768,256]{2,1,0:T(8,128)(2,1)} %get-tuple-element.60), channel_id=1, source_target_pairs={{0,32},{32,0},{1,33},{33,1},{2,34},{34,2},{3,35},{35,3},{4,36},{36... | collective-permute-start | bytes 4718600 | tf_op jit(solution)/shard_map/ppermute | solution.py:49
  225.1 23.9 %all-to-all-start.6 = ((bf16[4,4,128,384]{3,2,1,0:T(8,128)(2,1)}), bf16[4,4,128,384]{3,2,1,0:T(8,128)(2,1)S(1)}, u32[]{:S(2)}, u32[]{:S(2)}) async-start(bf16[4,4,128,384]{3,2,1,0:T(8,128)(2,1)} %add_convert_fusion), calls=%async_computation.6 | async-start | bytes 3145728 | tf_op jit(solution)/shard_map/all_to_all | solution.py:41
  231.4 20.4 %copy-start.12 = (bf16[768,256]{1,0:T(8,128)(2,1)S(1)}, bf16[768,256]{1,0:T(8,128)(2,1)}, u32[]{:S(2)}) copy-start(bf16[768,256]{1,0:T(8,128)(2,1)} %get-tuple-element.63) | copy-start | bytes 1179652
  231.4 20.0 %collective-permute-start.16 = (bf16[768,256]{1,0:T(8,128)(2,1)}, bf16[768,256]{1,0:T(8,128)(2,1)S(1)}, u32[]{:S(2)}, u32[]{:S(2)}) collective-permute-start(bf16[768,256]{1,0:T(8,128)(2,1)} %get-tuple-element.75), channel_id=1, source_target_pairs={{0,192},{64,128},{128,64},{192,0},{1,193},{65,129},{129,65},{193,1... | collective-permute-start | bytes 1179656 | tf_op jit(solution)/shard_map/ppermute | solution.py:49
  233.9 17.6 %collective-permute-start.15 = (bf16[768,256]{1,0:T(8,128)(2,1)}, bf16[768,256]{1,0:T(8,128)(2,1)S(1)}, u32[]{:S(2)}, u32[]{:S(2)}) collective-permute-start(bf16[768,256]{1,0:T(8,128)(2,1)} %get-tuple-element.76), channel_id=1, source_target_pairs={{0,128},{64,192},{128,0},{192,64},{1,129},{65,193},{129,1},{193,65... | collective-permute-start | bytes 1179656 | tf_op jit(solution)/shard_map/ppermute | solution.py:49
  234.4 17.4 %collective-permute-start.14 = (bf16[768,256]{1,0:T(8,128)(2,1)}, bf16[768,256]{1,0:T(8,128)(2,1)S(1)}, u32[]{:S(2)}, u32[]{:S(2)}) collective-permute-start(bf16[768,256]{1,0:T(8,128)(2,1)} %get-tuple-element.77), channel_id=1, source_target_pairs={{0,64},{64,0},{128,192},{192,128},{1,65},{65,1},{129,193},{193,129... | collective-permute-start | bytes 1179656 | tf_op jit(solution)/shard_map/ppermute | solution.py:49
  252.0 7.7 %collective-permute-start.18 = (bf16[8,24,256]{2,1,0:T(8,128)(2,1)S(1)}, bf16[8,24,256]{2,1,0:T(8,128)(2,1)S(1)}, u32[]{:S(2)}, u32[]{:S(2)}) collective-permute-start(bf16[8,24,256]{2,1,0:T(8,128)(2,1)S(1)} %get-tuple-element.93), channel_id=1, source_target_pairs={{0,1},{1,0},{2,3},{3,2},{4,5},{5,4},{6,7},{7,6},{8,9},{9,8},{10,11... | collective-permute-start | bytes 294920 | tf_op jit(solution)/shard_map/ppermute | solution.py:49
  253.2 6.5 %collective-permute-start.20 = (bf16[8,24,256]{2,1,0:T(8,128)(2,1)S(1)}, bf16[8,24,256]{2,1,0:T(8,128)(2,1)S(1)}, u32[]{:S(2)}, u32[]{:S(2)}) collective-permute-start(bf16[8,24,256]{2,1,0:T(8,128)(2,1)S(1)} %get-tuple-element.94), channel_id=1, source_target_pairs={{0,3},{1,2},{2,1},{3,0},{4,7},{5,6},{6,5},{7,4},{8,11},{9,10},{10,... | collective-permute-start | bytes 294920 | tf_op jit(solution)/shard_map/ppermute | solution.py:49
  255.0 6.0 %collective-permute-start.19 = (bf16[8,24,256]{2,1,0:T(8,128)(2,1)S(1)}, bf16[8,24,256]{2,1,0:T(8,128)(2,1)S(1)}, u32[]{:S(2)}, u32[]{:S(2)}) collective-permute-start(bf16[8,24,256]{2,1,0:T(8,128)(2,1)S(1)} %get-tuple-element.95), channel_id=1, source_target_pairs={{0,2},{1,3},{2,0},{3,1},{4,6},{5,7},{6,4},{7,5},{8,10},{9,11},{10,... | collective-permute-start | bytes 294920 | tf_op jit(solution)/shard_map/ppermute | solution.py:49
  255.6 10.3 %all-to-all-start.7 = ((bf16[4,128,384]{2,1,0:T(8,128)(2,1)}), bf16[4,128,384]{2,1,0:T(8,128)(2,1)S(1)}, u32[]{:S(2)}, u32[]{:S(2)}) async-start(bf16[4,128,384]{2,1,0:T(8,128)(2,1)} %fusion.17), calls=%async_computation.7 | async-start | bytes 786432 | tf_op jit(solution)/shard_map/all_to_all | solution.py:41
  259.7 26.6 %copy-start.7 = (f32[128,1]{1,0:T(8,128)S(1)}, f32[128,1]{1,0:T(8,128)}, u32[]{:S(2)}) copy-start(f32[128,1]{1,0:T(8,128)} %copy-done.6) | copy-start | bytes 1540
  278.0 16.4 %all-to-all-start.9 = ((f32[8,96,128]{2,1,0:T(8,128)}), f32[8,96,128]{2,1,0:T(8,128)S(1)}, u32[]{:S(2)}, u32[]{:S(2)}) async-start(f32[8,96,128]{2,1,0:T(8,128)} %broadcast_in_dim.126), calls=%async_computation.9 | async-start | bytes 786432 | tf_op jit(solution)/shard_map/all_to_all | solution.py:41
  294.4 0.9 copy-start.1
  (1 other events, 0.7 us)

commit v3 on v2

--- a/solution.py
+++ b/solution.py
@@ -206,21 +206,22 @@
     outer_piece = lax.dynamic_slice(outer_weight, (group * deep, 0), (deep, width))
     piece = jnp.concatenate([rows_to_columns(inner_piece, deep), outer_piece], axis=0)
 
-    (found_10,) = find([(1, 0)])
-    near_10 = swap(found_10, "y", 1)
+    found_10, found_30 = find([(1, 0), (3, 0)])
+    near_10, near_30 = swap(found_10, "y", 1), swap(found_30, "y", 3)
     gathered = spread(after(piece, found_10), ("z", "y"), SHARD)
-    found_00, found_01 = find([(0, 0), (0, 1)], found_10)
-    found_11, found_30, found_20 = find([(1, 1), (3, 0), (2, 0)], found_00, found_01)
-    near_11, near_30, near_20 = swap(found_11, "y", 1), swap(found_30, "y", 3), swap(found_20, "y", 2)
-    own_0 = after(found_00 + after(near_10, found_11), gathered)
+    found_11, found_31, found_00 = find([(1, 1), (3, 1), (0, 0)], found_10)
+    near_11, near_31 = swap(found_11, "y", 1), swap(found_31, "y", 3)
+    found_20, found_01 = find([(2, 0), (0, 1)], found_11, near_10, near_30)
+    near_20 = swap(found_20, "y", 2)
+    own_0 = after(found_00 + after(near_10, found_11, found_31), gathered, near_30)
     rows_0 = exchange(own_0, "z")
     gathered = after(gathered, own_0)
     parts = [gathered] + [swap(gathered, "x", by) for by in range(1, X)]
-    found_31, found_21 = find([(3, 1), (2, 1)], own_0, near_11)
-    near_31, near_21 = swap(found_31, "y", 3), swap(found_21, "y", 2)
-    own_1 = found_01 + near_11
+    (found_21,) = find([(2, 1)], own_0)
+    near_21 = swap(found_21, "y", 2)
+    own_1 = found_01 + after(near_11, own_0)
     rows_1 = exchange(
-        after(own_1, rows_0, near_30, near_20, found_31, parts[1], parts[3]), "z"
+        after(own_1, rows_0, near_31, near_20, found_21, parts[1], parts[3]), "z"
     )
     rows_2 = exchange(after(near_20 + near_30, rows_1, near_21, parts[2]), "z")
     other_1 = near_21 + near_31

time: 297 us -> 277 us (0.933)
  waiting for transfers between devices: 93.5 us -> 62.2 us
  starting transfers between devices: 85.8 us -> 95.3 us
    ppermute x21, waiting for transfers between devices: 45.2 us -> 20.3 us  [swap(): lax.ppermute(value, axis, [(i, i ^ by) for i in range(lax.axis_size(axis))])]
    ppermute x21, starting transfers between devices: 30 us -> 37.9 us  [swap(): lax.ppermute(value, axis, [(i, i ^ by) for i in range(lax.axis_size(axis))])]
    all_to_all x9, waiting for transfers between devices: 48.3 us -> 41.8 us  [exchange(): return lax.all_to_all(value, axes, split_axis=0, concat_axis=0, tiled=True)]
  transfers between devices with their start and end apart: 30 -> 30, of which waited for: 15 -> 15; matrix products, arithmetic and copies ran while one was open for 22% -> 23% of each run, Pallas kernels for 4% -> 4%
where the time goes in v3:
time: 277 us; the launch traced here: 276 us
  starting transfers between devices  95.3 us (34%)
  waiting for transfers between devices  62.2 us (22%)
  local copies, waits for them, and re-layouts  50.6 us (18%)
  other arithmetic  24.2 us (9%)
  Pallas kernels  23.2 us (8%)
  blocking collectives  11.1 us (4%)
  matrix products  8.02 us (3%)
    all_to_all x9, starting transfers between devices, exchange(): return lax.all_to_all(value, axes, split_axis=0, concat_axis=0, tiled=True)  57.4 us
    all_to_all x9, waiting for transfers between devices, exchange(): return lax.all_to_all(value, axes, split_axis=0, concat_axis=0, tiled=True)  41.8 us
    ppermute x21, starting transfers between devices, swap(): lax.ppermute(value, axis, [(i, i ^ by) for i in range(lax.axis_size(axis))])  37.9 us
    gather x4, local copies, waits for them, and re-layouts, find(): passage_table.at[ids].get(mode='promise_in_bounds')  33.5 us
    ppermute x21, waiting for transfers between devices, swap(): lax.ppermute(value, axis, [(i, i ^ by) for i in range(lax.axis_size(axis))])  20.3 us
    all_to_all x1, blocking collectives, exchange(): return lax.all_to_all(value, axes, split_axis=0, concat_axis=0, tiled=True)  11.1 us
    select_n x4, other arithmetic, find(): jnp.where(own[by, :, cuts[part]].reshape(-1, 1), found[i], jnp.zeros((),...  7.88 us
    dot_general x8, matrix products, shards(): jnp.dot(queries, part, preferred_element_type=jnp.float32)  7.43 us
  transfers between devices with their start and end apart: 30, of which 15 were waited for; matrix products, arithmetic and copies ran while one was open for 23% of the time, Pallas kernels for 4%

profile of v3, /device:TPU:1, one launch (start us, length us, event | category | flops | bytes accessed | tf_op | source)
XLA Modules:
  0.0 275.8 jit_solution(123981195147565066)
XLA Ops:
  1.5 5.8 %shard_map.85 = (s32[16,128]{1,0:T(8,128)S(1)}, s32[16,128]{1,0:T(8,128)S(1)}) custom-call(s32[128,16]{1,0:T(8,128)S(1)} %copy.33.ids_ref), custom_call_target="tpu_custom_call" | custom-call | tf_op jit(solution)/shard_map/pallas_call | solution.py:182
  7.9 12.0 %all-to-all-start = ((s32[32,1,128]{2,1,0:T(1,128)}), s32[32,1,128]{2,1,0:T(1,128)S(1)}, u32[]{:S(2)}, u32[]{:S(2)}) async-start(s32[32,1,128]{2,1,0:T(1,128)} %bitcast.2), calls=%async_computation | async-start | bytes 32768 | tf_op jit(solution)/shard_map/all_to_all | solution.py:41
  20.8 7.7 %all-to-all-done = s32[32,1,128]{2,1,0:T(1,128)S(1)} async-done(((s32[32,1,128]{2,1,0:T(1,128)}), s32[32,1,128]{2,1,0:T(1,128)S(1)}, u32[]{:S(2)}, u32[]{:S(2)}) %all-to-all-start) | async-done | bytes 16416 | tf_op jit(solution)/shard_map/all_to_all | solution.py:41
  29.0 8.1 %gather_fusion = bf16[1024,768]{1,0:T(8,128)(2,1)S(1)} fusion(bf16[4096,768]{1,0:T(8,128)(2,1)} %param.9, s32[1024]{0:T(1024)S(1)} %fusion.39), kind=kCustom, calls=%fused_computation | custom fusion | bytes 3149824 | tf_op jit(solution)/shard_map/gather | solution.py:198
  39.1 3.9 %all-to-all-start.1 = ((bf16[32,16,768]{2,1,0:T(8,128)(2,1)}), bf16[32,16,768]{2,1,0:T(8,128)(2,1)S(1)}, u32[]{:S(2)}, u32[]{:S(2)}) async-start(bf16[32,16,768]{2,1,0:T(8,128)(2,1)} %broadcast_in_dim.107), calls=%async_computation.1 | async-start | bytes 1572864 | tf_op jit(solution)/shard_map/all_to_all | solution.py:41
  44.3 1.8 collective-permute-start.1
  46.3 10.3 %gather_fusion.1 = bf16[1536,768]{1,0:T(8,128)(2,1)} fusion(bf16[4096,768]{1,0:T(8,128)(2,1)} %param.9, s32[2048]{0:T(1024)S(1)} %pad_clamp_fusion), kind=kCustom, calls=%fused_computation.1 | custom fusion | bytes 4724736 | tf_op jit(solution)/shard_map/gather | solution.py:198
  56.6 2.7 slice_select_fusion.3
  60.5 7.9 %collective-permute-done = bf16[512,768]{1,0:T(8,128)(2,1)S(1)} collective-permute-done((bf16[512,768]{1,0:T(8,128)(2,1)}, bf16[512,768]{1,0:T(8,128)(2,1)S(1)}, u32[]{:S(2)}, u32[]{:S(2)}) %collective-permute-start) | collective-permute-done | bytes 786464 | tf_op jit(solution)/shard_map/ppermute | solution.py:49
  68.4 2.2 fusion.14
  72.2 6.8 %all-to-all-start.2 = ((bf16[8,64,768]{2,1,0:T(8,128)(2,1)}), bf16[8,64,768]{2,1,0:T(8,128)(2,1)S(1)}, u32[]{:S(2)}, u32[]{:S(2)}) async-start(bf16[8,64,768]{2,1,0:T(8,128)(2,1)} %bitcast.8), calls=%async_computation.2 | async-start | bytes 1572864 | tf_op jit(solution)/shard_map/all_to_all | solution.py:41
  79.1 9.2 %gather_fusion.2 = bf16[1024,768]{1,0:T(8,128)(2,1)} fusion(bf16[4096,768]{1,0:T(8,128)(2,1)} %param.9, s32[1024]{0:T(1024)S(1)} %fusion.40), kind=kCustom, calls=%fused_computation.2 | custom fusion | bytes 3149824 | tf_op jit(solution)/shard_map/gather | solution.py:198
  88.3 2.5 collective-permute-start.4
  90.8 3.0 %slice_select_fusion = (bf16[512,768]{1,0:T(8,128)(2,1)}, bf16[512,768]{1,0:T(8,128)(2,1)}) fusion(bf16[1024,768]{1,0:T(8,128)(2,1)} %gather_fusion.2, pred[512]{0:T(512)(128)(4,1)S(1)} %broadcast_in_dim.120, bf16[512,768]{1,0:T(8,128)(2,1)} %collective-permute-done.9, pred[512]{0:T(512)(128)(4,1)S(1)} %broadcast_in_dim.117), kind=kLoop, calls=%fused_computation.31 | loop fusion | flops 1179648 | bytes 3933184 | tf_op jit(solution)/shard_map/jit(_where)/select_n | solution.py:200
  93.8 2.5 collective-permute-start.11
  97.8 6.0 %gather_fusion.3 = bf16[512,768]{1,0:T(8,128)(2,1)S(1)} fusion(bf16[4096,768]{1,0:T(8,128)(2,1)} %param.9, s32[1024]{0:T(1024)S(1)} %pad_clamp_fusion.1), kind=kCustom, calls=%fused_computation.3 | custom fusion | bytes 1574912 | tf_op jit(solution)/shard_map/gather | solution.py:198
  106.3 4.5 %collective-permute-done.11 = bf16[512,768]{1,0:T(8,128)(2,1)} collective-permute-done((bf16[512,768]{1,0:T(8,128)(2,1)}, bf16[512,768]{1,0:T(8,128)(2,1)}, u32[]{:S(2)}, u32[]{:S(2)}) %collective-permute-start.11) | collective-permute-done | bytes 786464 | tf_op jit(solution)/shard_map/ppermute | solution.py:49
  110.8 6.4 %all-to-all-start.3 = ((bf16[8,64,768]{2,1,0:T(8,128)(2,1)}), bf16[8,64,768]{2,1,0:T(8,128)(2,1)S(1)}, u32[]{:S(2)}, u32[]{:S(2)}) async-start(bf16[8,64,768]{2,1,0:T(8,128)(2,1)} %bitcast.183), calls=%async_computation.3 | async-start | bytes 1572864 | tf_op jit(solution)/shard_map/all_to_all | solution.py:41
  117.2 2.8 %collective-permute-start.12 = (bf16[512,768]{1,0:T(8,128)(2,1)}, bf16[512,768]{1,0:T(8,128)(2,1)}, u32[]{:S(2)}, u32[]{:S(2)}) collective-permute-start(bf16[512,768]{1,0:T(8,128)(2,1)} %broadcast_select_fusion), channel_id=1, source_target_pairs={{0,2},{1,3},{2,0},{3,1},{4,6},{5,7},{6,4},{7,5},{8,10},{9,11},{10,... | collective-permute-start | bytes 2359304 | tf_op jit(solution)/shard_map/ppermute | solution.py:49
  120.0 5.3 %collective-permute-start.5 = (bf16[32,16,768]{2,1,0:T(8,128)(2,1)S(1)}, bf16[32,16,768]{2,1,0:T(8,128)(2,1)}, u32[]{:S(2)}, u32[]{:S(2)}) collective-permute-start(bf16[32,16,768]{2,1,0:T(8,128)(2,1)S(1)} %all-to-all-done.1.refs_0_), channel_id=1, source_target_pairs={{0,32},{32,0},{1,33},{33,1},{2,34},{34,2},{3,35},{35,3},{4,36},{36... | collective-permute-start | bytes 2359304 | tf_op jit(solution)/shard_map/ppermute | solution.py:49
  125.3 2.3 collective-permute-start.7
  128.1 2.4 add.187
  130.5 2.3 collective-permute-done.12
  132.8 2.5 add.184
  135.9 5.8 %all-to-all-start.4 = ((bf16[8,64,768]{2,1,0:T(8,128)(2,1)}), bf16[8,64,768]{2,1,0:T(8,128)(2,1)S(1)}, u32[]{:S(2)}, u32[]{:S(2)}) async-start(bf16[8,64,768]{2,1,0:T(8,128)(2,1)} %bitcast.182), calls=%async_computation.4 | async-start | bytes 1572864 | tf_op jit(solution)/shard_map/all_to_all | solution.py:41
  142.9 5.4 %shard_map.86 = bf16[4,2,32,16,768]{4,3,2,1,0:T(8,128)(2,1)} custom-call(s32[2]{0:T(128)S(1)} %pad_add_fusion.5.place_ref, bf16[32,16,768]{2,1,0:T(8,128)(2,1)S(1)} %all-to-all-done.1.refs_0_, bf16[32,16,768]{2,1,0:T(8,128)(2,1)} %collective-permute-done.2.refs_1_, bf16[32,16,768]{2,1,0:T(8,128)(2,1)} %collective-permute-done.3.refs_2_, ...), custom_call_target="tpu_custom_call" | custom-call | tf_op jit(solution)/shard_map/pallas_call | solution.py:231
  148.2 2.2 slice_bitcast_fusion.1
  157.2 1.9 slice_bitcast_fusion
  159.0 6.6 %all-to-all-start.5 = ((bf16[8,64,768]{2,1,0:T(8,128)(2,1)}), bf16[8,64,768]{2,1,0:T(8,128)(2,1)}, u32[]{:S(2)}, u32[]{:S(2)}) async-start(bf16[8,64,768]{2,1,0:T(8,128)(2,1)} %bitcast.181), calls=%async_computation.5 | async-start | bytes 1572864 | tf_op jit(solution)/shard_map/all_to_all | solution.py:41
  165.7 2.3 copy.42
  170.0 1.7 fusion.12
  172.3 7.6 %all-to-all-done.5 = bf16[8,64,768]{2,1,0:T(8,128)(2,1)} async-done(((bf16[8,64,768]{2,1,0:T(8,128)(2,1)}), bf16[8,64,768]{2,1,0:T(8,128)(2,1)}, u32[]{:S(2)}, u32[]{:S(2)}) %all-to-all-start.5) | async-done | bytes 786464 | tf_op jit(solution)/shard_map/all_to_all | solution.py:41
  182.0 6.7 %shard_map.87 = (f32[128,1]{1,0:T(8,128)S(1)}, bf16[128,768]{1,0:T(8,128)(2,1)S(1)}, bf16[4,4,128,384]{3,2,1,0:T(8,128)(2,1)}, bf16[4,4,128,384]{3,2,1,0:T(8,128)(2,1)}) custom-call(s32[2]{0:T(128)S(1)} %pad_add_fusion.5.place_ref, bf16[128,768]{1,0:T(8,128)(2,1)S(1)} %fusion.embedded_ref, bf16[128,768]{1,0:T(8,128)(2,1)S(1)} %copy-done.7, ...), custom_call_target="tpu_custom_call" | custom-call | tf_op jit(solution)/shard_map/pallas_call | solution.py:259
  188.7 10.2 %collective-permute-start.17 = (bf16[4,4,128,384]{3,2,1,0:T(8,128)(2,1)}, bf16[4,4,128,384]{3,2,1,0:T(8,128)(2,1)S(1)}, u32[]{:S(2)}, u32[]{:S(2)}) collective-permute-start(bf16[4,4,128,384]{3,2,1,0:T(8,128)(2,1)} %get-tuple-element.64), channel_id=1, source_target_pairs={{0,32},{32,0},{1,33},{33,1},{2,34},{34,2},{3,35},{35,3},{4,36},{36... | collective-permute-start | bytes 4718600 | tf_op jit(solution)/shard_map/ppermute | solution.py:49
  198.9 5.3 %shard_map.88 = (bf16[4,768,256]{2,1,0:T(8,128)(2,1)S(1)}, bf16[4,768,256]{2,1,0:T(8,128)(2,1)}) custom-call(s32[2]{0:T(128)S(1)} %pad_add_fusion.5.place_ref, bf16[128,768]{1,0:T(8,128)(2,1)S(1)} %copy-done.2, bf16[128,768]{1,0:T(8,128)(2,1)S(1)} %get-tuple-element.60.grad_ref, f32[128,2048]{1,0:T(8,128)S(1)} %get-tuple-element.87.slope_ref, ...), custom_call_target="tpu_custom_call" | custom-call | tf_op jit(solution)/shard_map/pallas_call | solution.py:271
  204.2 1.7 add_convert_fusion
  205.8 4.1 %all-to-all-start.6 = ((bf16[4,4,128,384]{3,2,1,0:T(8,128)(2,1)}), bf16[4,4,128,384]{3,2,1,0:T(8,128)(2,1)S(1)}, u32[]{:S(2)}, u32[]{:S(2)}) async-start(bf16[4,4,128,384]{3,2,1,0:T(8,128)(2,1)} %add_convert_fusion), calls=%async_computation.6 | async-start | bytes 3145728 | tf_op jit(solution)/shard_map/all_to_all | solution.py:41
  209.9 2.7 fusion.18
  213.4 2.5 collective-permute-start.15
  215.9 14.0 %all-to-all-done.6 = bf16[4,4,128,384]{3,2,1,0:T(8,128)(2,1)S(1)} async-done(((bf16[4,4,128,384]{3,2,1,0:T(8,128)(2,1)}), bf16[4,4,128,384]{3,2,1,0:T(8,128)(2,1)S(1)}, u32[]{:S(2)}, u32[]{:S(2)}) %all-to-all-start.6) | async-done | bytes 1572896 | tf_op jit(solution)/shard_map/all_to_all | solution.py:41
  230.9 1.6 collective-permute-done.16
  234.3 1.8 collective-permute-start.20
  236.7 3.5 %all-to-all-start.7 = ((bf16[4,128,384]{2,1,0:T(8,128)(2,1)}), bf16[4,128,384]{2,1,0:T(8,128)(2,1)S(1)}, u32[]{:S(2)}, u32[]{:S(2)}) async-start(bf16[4,128,384]{2,1,0:T(8,128)(2,1)} %fusion.19), calls=%async_computation.7 | async-start | bytes 786432 | tf_op jit(solution)/shard_map/all_to_all | solution.py:41
  240.2 1.7 collective-permute-done.19
  241.9 4.4 %all-to-all-done.7 = bf16[4,128,384]{2,1,0:T(8,128)(2,1)S(1)} async-done(((bf16[4,128,384]{2,1,0:T(8,128)(2,1)}), bf16[4,128,384]{2,1,0:T(8,128)(2,1)S(1)}, u32[]{:S(2)}, u32[]{:S(2)}) %all-to-all-start.7) | async-done | bytes 393248 | tf_op jit(solution)/shard_map/all_to_all | solution.py:41
  246.5 11.1 %all_to_all.78 = bf16[8,96,128]{2,1,0:T(8,128)(2,1)S(1)} all-to-all(bf16[8,96,128]{2,1,0:T(8,128)(2,1)S(1)} %constant_dynamic-update-slice_fusion), channel_id=1, replica_groups=mesh['x'=4,'core'=2,'z'=8,'y'=4] {'z'}, dimensions={0} | all-to-all | bytes 393216 | tf_op jit(solution)/shard_map/all_to_all | solution.py:41
  258.4 8.3 %all-to-all-start.9 = ((f32[8,96,128]{2,1,0:T(8,128)}), f32[8,96,128]{2,1,0:T(8,128)S(1)}, u32[]{:S(2)}, u32[]{:S(2)}) async-start(f32[8,96,128]{2,1,0:T(8,128)} %broadcast_in_dim.126), calls=%async_computation.9 | async-start | bytes 786432 | tf_op jit(solution)/shard_map/all_to_all | solution.py:41
  267.3 7.5 %all-to-all-done.9 = f32[8,96,128]{2,1,0:T(8,128)S(1)} async-done(((f32[8,96,128]{2,1,0:T(8,128)}), f32[8,96,128]{2,1,0:T(8,128)S(1)}, u32[]{:S(2)}, u32[]{:S(2)}) %all-to-all-start.9) | async-done | bytes 393248 | tf_op jit(solution)/shard_map/all_to_all | solution.py:41
  (162 shorter events, 33.3 us)
Async XLA Ops:
  0.6 19.4 %copy-start = (bf16[64,768]{1,0:T(8,128)(2,1)S(1)}, bf16[64,768]{1,0:T(8,128)(2,1)}, u32[]{:S(2)}) copy-start(bf16[64,768]{1,0:T(8,128)(2,1)} %param.11) | copy-start | bytes 294916
  7.9 20.6 %all-to-all-start = ((s32[32,1,128]{2,1,0:T(1,128)}), s32[32,1,128]{2,1,0:T(1,128)S(1)}, u32[]{:S(2)}, u32[]{:S(2)}) async-start(s32[32,1,128]{2,1,0:T(1,128)} %bitcast.2), calls=%async_computation | async-start | bytes 32768 | tf_op jit(solution)/shard_map/all_to_all | solution.py:41
  39.1 32.2 %all-to-all-start.1 = ((bf16[32,16,768]{2,1,0:T(8,128)(2,1)}), bf16[32,16,768]{2,1,0:T(8,128)(2,1)S(1)}, u32[]{:S(2)}, u32[]{:S(2)}) async-start(bf16[32,16,768]{2,1,0:T(8,128)(2,1)} %broadcast_in_dim.107), calls=%async_computation.1 | async-start | bytes 1572864 | tf_op jit(solution)/shard_map/all_to_all | solution.py:41
  43.0 25.4 %collective-permute-start = (bf16[512,768]{1,0:T(8,128)(2,1)}, bf16[512,768]{1,0:T(8,128)(2,1)S(1)}, u32[]{:S(2)}, u32[]{:S(2)}) collective-permute-start(bf16[512,768]{1,0:T(8,128)(2,1)} %get-tuple-element.86), channel_id=1, source_target_pairs={{0,1},{1,0},{2,3},{3,2},{4,5},{5,4},{6,7},{7,6},{8,9},{9,8},{10,11... | collective-permute-start | bytes 2359304 | tf_op jit(solution)/shard_map/ppermute | solution.py:49
  44.3 27.0 %collective-permute-start.1 = (bf16[512,768]{1,0:T(8,128)(2,1)S(1)}, bf16[512,768]{1,0:T(8,128)(2,1)S(1)}, u32[]{:S(2)}, u32[]{:S(2)}) collective-permute-start(bf16[512,768]{1,0:T(8,128)(2,1)S(1)} %get-tuple-element.85), channel_id=1, source_target_pairs={{0,3},{1,2},{2,1},{3,0},{4,7},{5,6},{6,5},{7,4},{8,11},{9,10},{10,... | collective-permute-start | bytes 2359304 | tf_op jit(solution)/shard_map/ppermute | solution.py:49
  59.3 31.5 %collective-permute-start.9 = (bf16[512,768]{1,0:T(8,128)(2,1)}, bf16[512,768]{1,0:T(8,128)(2,1)}, u32[]{:S(2)}, u32[]{:S(2)}) collective-permute-start(bf16[512,768]{1,0:T(8,128)(2,1)} %get-tuple-element.82), channel_id=1, source_target_pairs={{0,1},{1,0},{2,3},{3,2},{4,5},{5,4},{6,7},{7,6},{8,9},{9,8},{10,11... | collective-permute-start | bytes 2359304 | tf_op jit(solution)/shard_map/ppermute | solution.py:49
  59.9 45.0 %collective-permute-start.10 = (bf16[512,768]{1,0:T(8,128)(2,1)}, bf16[512,768]{1,0:T(8,128)(2,1)}, u32[]{:S(2)}, u32[]{:S(2)}) collective-permute-start(bf16[512,768]{1,0:T(8,128)(2,1)} %get-tuple-element.81), channel_id=1, source_target_pairs={{0,3},{1,2},{2,1},{3,0},{4,7},{5,6},{6,5},{7,4},{8,11},{9,10},{10,... | collective-permute-start | bytes 2359304 | tf_op jit(solution)/shard_map/ppermute | solution.py:49
  71.3 0.9 copy-start.13
  72.2 38.6 %all-to-all-start.2 = ((bf16[8,64,768]{2,1,0:T(8,128)(2,1)}), bf16[8,64,768]{2,1,0:T(8,128)(2,1)S(1)}, u32[]{:S(2)}, u32[]{:S(2)}) async-start(bf16[8,64,768]{2,1,0:T(8,128)(2,1)} %bitcast.8), calls=%async_computation.2 | async-start | bytes 1572864 | tf_op jit(solution)/shard_map/all_to_all | solution.py:41
  88.3 17.1 %collective-permute-start.4 = (bf16[32,16,768]{2,1,0:T(8,128)(2,1)S(1)}, bf16[32,16,768]{2,1,0:T(8,128)(2,1)S(1)}, u32[]{:S(2)}, u32[]{:S(2)}) collective-permute-start(bf16[32,16,768]{2,1,0:T(8,128)(2,1)S(1)} %all-to-all-done.1.refs_0_), channel_id=1, source_target_pairs={{0,192},{64,128},{128,64},{192,0},{1,193},{65,129},{129,65},{193,1... | collective-permute-start | bytes 2359304 | tf_op jit(solution)/shard_map/ppermute | solution.py:49
  90.8 15.6 %collective-permute-start.2 = (bf16[32,16,768]{2,1,0:T(8,128)(2,1)S(1)}, bf16[32,16,768]{2,1,0:T(8,128)(2,1)}, u32[]{:S(2)}, u32[]{:S(2)}) collective-permute-start(bf16[32,16,768]{2,1,0:T(8,128)(2,1)S(1)} %all-to-all-done.1.refs_0_), channel_id=1, source_target_pairs={{0,64},{64,0},{128,192},{192,128},{1,65},{65,1},{129,193},{193,129... | collective-permute-start | bytes 2359304 | tf_op jit(solution)/shard_map/ppermute | solution.py:49
  93.8 17.1 %collective-permute-start.11 = (bf16[512,768]{1,0:T(8,128)(2,1)}, bf16[512,768]{1,0:T(8,128)(2,1)}, u32[]{:S(2)}, u32[]{:S(2)}) collective-permute-start(bf16[512,768]{1,0:T(8,128)(2,1)} %get-tuple-element.83), channel_id=1, source_target_pairs={{0,2},{1,3},{2,0},{3,1},{4,6},{5,7},{6,4},{7,5},{8,10},{9,11},{10,... | collective-permute-start | bytes 2359304 | tf_op jit(solution)/shard_map/ppermute | solution.py:49
  96.5 28.8 %collective-permute-start.3 = (bf16[32,16,768]{2,1,0:T(8,128)(2,1)S(1)}, bf16[32,16,768]{2,1,0:T(8,128)(2,1)}, u32[]{:S(2)}, u32[]{:S(2)}) collective-permute-start(bf16[32,16,768]{2,1,0:T(8,128)(2,1)S(1)} %all-to-all-done.1.refs_0_), channel_id=1, source_target_pairs={{0,128},{64,192},{128,0},{192,64},{1,129},{65,193},{129,1},{193,65... | collective-permute-start | bytes 2359304 | tf_op jit(solution)/shard_map/ppermute | solution.py:49
  105.3 25.2 %copy-start.5 = (bf16[32,16,768]{2,1,0:T(8,128)(2,1)}, bf16[32,16,768]{2,1,0:T(8,128)(2,1)S(1)}, u32[]{:S(2)}) copy-start(bf16[32,16,768]{2,1,0:T(8,128)(2,1)S(1)} %collective-permute-done.4.refs_3_) | copy-start | bytes 2359300
  110.8 25.0 %all-to-all-start.3 = ((bf16[8,64,768]{2,1,0:T(8,128)(2,1)}), bf16[8,64,768]{2,1,0:T(8,128)(2,1)S(1)}, u32[]{:S(2)}, u32[]{:S(2)}) async-start(bf16[8,64,768]{2,1,0:T(8,128)(2,1)} %bitcast.183), calls=%async_computation.3 | async-start | bytes 1572864 | tf_op jit(solution)/shard_map/all_to_all | solution.py:41
  117.2 15.6 %collective-permute-start.12 = (bf16[512,768]{1,0:T(8,128)(2,1)}, bf16[512,768]{1,0:T(8,128)(2,1)}, u32[]{:S(2)}, u32[]{:S(2)}) collective-permute-start(bf16[512,768]{1,0:T(8,128)(2,1)} %broadcast_select_fusion), channel_id=1, source_target_pairs={{0,2},{1,3},{2,0},{3,1},{4,6},{5,7},{6,4},{7,5},{8,10},{9,11},{10,... | collective-permute-start | bytes 2359304 | tf_op jit(solution)/shard_map/ppermute | solution.py:49
  120.0 15.9 %collective-permute-start.5 = (bf16[32,16,768]{2,1,0:T(8,128)(2,1)S(1)}, bf16[32,16,768]{2,1,0:T(8,128)(2,1)}, u32[]{:S(2)}, u32[]{:S(2)}) collective-permute-start(bf16[32,16,768]{2,1,0:T(8,128)(2,1)S(1)} %all-to-all-done.1.refs_0_), channel_id=1, source_target_pairs={{0,32},{32,0},{1,33},{33,1},{2,34},{34,2},{3,35},{35,3},{4,36},{36... | collective-permute-start | bytes 2359304 | tf_op jit(solution)/shard_map/ppermute | solution.py:49
  125.3 10.6 %collective-permute-start.8 = (bf16[32,16,768]{2,1,0:T(8,128)(2,1)S(1)}, bf16[32,16,768]{2,1,0:T(8,128)(2,1)}, u32[]{:S(2)}, u32[]{:S(2)}) collective-permute-start(bf16[32,16,768]{2,1,0:T(8,128)(2,1)S(1)} %collective-permute-done.4.refs_3_), channel_id=1, source_target_pairs={{0,32},{32,0},{1,33},{33,1},{2,34},{34,2},{3,35},{35,3},{4,36},{36... | collective-permute-start | bytes 2359304 | tf_op jit(solution)/shard_map/ppermute | solution.py:49
  125.3 10.6 %collective-permute-start.7 = (bf16[32,16,768]{2,1,0:T(8,128)(2,1)}, bf16[32,16,768]{2,1,0:T(8,128)(2,1)}, u32[]{:S(2)}, u32[]{:S(2)}) collective-permute-start(bf16[32,16,768]{2,1,0:T(8,128)(2,1)} %collective-permute-done.3.refs_2_), channel_id=1, source_target_pairs={{0,32},{32,0},{1,33},{33,1},{2,34},{34,2},{3,35},{35,3},{4,36},{36... | collective-permute-start | bytes 2359304 | tf_op jit(solution)/shard_map/ppermute | solution.py:49
  127.6 8.3 %collective-permute-start.6 = (bf16[32,16,768]{2,1,0:T(8,128)(2,1)}, bf16[32,16,768]{2,1,0:T(8,128)(2,1)}, u32[]{:S(2)}, u32[]{:S(2)}) collective-permute-start(bf16[32,16,768]{2,1,0:T(8,128)(2,1)} %collective-permute-done.2.refs_1_), channel_id=1, source_target_pairs={{0,32},{32,0},{1,33},{33,1},{2,34},{34,2},{3,35},{35,3},{4,36},{36... | collective-permute-start | bytes 2359304 | tf_op jit(solution)/shard_map/ppermute | solution.py:49
  135.9 23.1 %all-to-all-start.4 = ((bf16[8,64,768]{2,1,0:T(8,128)(2,1)}), bf16[8,64,768]{2,1,0:T(8,128)(2,1)S(1)}, u32[]{:S(2)}, u32[]{:S(2)}) async-start(bf16[8,64,768]{2,1,0:T(8,128)(2,1)} %bitcast.182), calls=%async_computation.4 | async-start | bytes 1572864 | tf_op jit(solution)/shard_map/all_to_all | solution.py:41
  141.7 1.1 copy-start.6
  148.2 8.9 %slice-start = ((s8[6291456]{0:T(1024)(128)(4,1)}), s8[4194304]{0:T(1024)(128)(4,1)S(1)}, s32[]{:S(2)}) async-start(s8[6291456]{0:T(1024)(128)(4,1)} %bitcast.179), calls=%async_computation.10 | async-start | bytes 8388608
  150.6 0.9 copy-start.2
  150.6 6.5 %slice-start.1 = ((s8[6291456]{0:T(1024)(128)(4,1)}), s8[2097152]{0:T(1024)(128)(4,1)S(1)}, s32[]{:S(2)}) async-start(s8[6291456]{0:T(1024)(128)(4,1)} %bitcast.179), calls=%async_computation.11 | async-start | bytes 4194304
  159.0 9.0 %copy-start.3 = (bf16[8,64,768]{2,1,0:T(8,128)(2,1)}, bf16[8,64,768]{2,1,0:T(8,128)(2,1)S(1)}, u32[]{:S(2)}) copy-start(bf16[8,64,768]{2,1,0:T(8,128)(2,1)S(1)} %all-to-all-done.4) | copy-start | bytes 2359300
  159.0 20.9 %all-to-all-start.5 = ((bf16[8,64,768]{2,1,0:T(8,128)(2,1)}), bf16[8,64,768]{2,1,0:T(8,128)(2,1)}, u32[]{:S(2)}, u32[]{:S(2)}) async-start(bf16[8,64,768]{2,1,0:T(8,128)(2,1)} %bitcast.181), calls=%async_computation.5 | async-start | bytes 1572864 | tf_op jit(solution)/shard_map/all_to_all | solution.py:41
  168.0 3.7 %copy-start.10 = (bf16[32,4,2,8,768]{4,3,2,1,0:T(8,128)(2,1)}, bf16[32,4,2,8,768]{4,3,2,1,0:T(8,128)(2,1)S(1)}, u32[]{:S(2)}) copy-start(bf16[32,4,2,8,768]{4,3,2,1,0:T(8,128)(2,1)S(1)} %copy.42) | copy-start | bytes 9437188
  179.9 1.1 copy-start.4
  181.1 0.9 copy-start.7
  188.7 15.5 %copy-start.8 = (f32[128,1]{1,0:T(8,128)}, f32[128,1]{1,0:T(8,128)S(1)}, u32[]{:S(2)}) copy-start(f32[128,1]{1,0:T(8,128)S(1)} %get-tuple-element.59) | copy-start | bytes 1540
  188.7 15.5 %collective-permute-start.17 = (bf16[4,4,128,384]{3,2,1,0:T(8,128)(2,1)}, bf16[4,4,128,384]{3,2,1,0:T(8,128)(2,1)S(1)}, u32[]{:S(2)}, u32[]{:S(2)}) collective-permute-start(bf16[4,4,128,384]{3,2,1,0:T(8,128)(2,1)} %get-tuple-element.64), channel_id=1, source_target_pairs={{0,32},{32,0},{1,33},{33,1},{2,34},{34,2},{3,35},{35,3},{4,36},{36... | collective-permute-start | bytes 4718600 | tf_op jit(solution)/shard_map/ppermute | solution.py:49
  198.9 5.3 %copy-start.11 = (bf16[4,4,128,384]{3,2,1,0:T(8,128)(2,1)S(1)}, bf16[4,4,128,384]{3,2,1,0:T(8,128)(2,1)}, u32[]{:S(2)}) copy-start(bf16[4,4,128,384]{3,2,1,0:T(8,128)(2,1)} %get-tuple-element.63) | copy-start | bytes 4718596
  204.1 5.8 %collective-permute-start.13 = (bf16[4,768,256]{2,1,0:T(8,128)(2,1)}, bf16[4,768,256]{2,1,0:T(8,128)(2,1)}, u32[]{:S(2)}, u32[]{:S(2)}) collective-permute-start(bf16[4,768,256]{2,1,0:T(8,128)(2,1)} %get-tuple-element.62), channel_id=1, source_target_pairs={{0,32},{32,0},{1,33},{33,1},{2,34},{34,2},{3,35},{35,3},{4,36},{36... | collective-permute-start | bytes 4718600 | tf_op jit(solution)/shard_map/ppermute | solution.py:49
  205.8 24.1 %all-to-all-start.6 = ((bf16[4,4,128,384]{3,2,1,0:T(8,128)(2,1)}), bf16[4,4,128,384]{3,2,1,0:T(8,128)(2,1)S(1)}, u32[]{:S(2)}, u32[]{:S(2)}) async-start(bf16[4,4,128,384]{3,2,1,0:T(8,128)(2,1)} %add_convert_fusion), calls=%async_computation.6 | async-start | bytes 3145728 | tf_op jit(solution)/shard_map/all_to_all | solution.py:41
  212.7 20.1 %copy-start.12 = (bf16[768,256]{1,0:T(8,128)(2,1)S(1)}, bf16[768,256]{1,0:T(8,128)(2,1)}, u32[]{:S(2)}) copy-start(bf16[768,256]{1,0:T(8,128)(2,1)} %get-tuple-element.65) | copy-start | bytes 1179652
  212.7 19.9 %collective-permute-start.16 = (bf16[768,256]{1,0:T(8,128)(2,1)}, bf16[768,256]{1,0:T(8,128)(2,1)S(1)}, u32[]{:S(2)}, u32[]{:S(2)}) collective-permute-start(bf16[768,256]{1,0:T(8,128)(2,1)} %get-tuple-element.77), channel_id=1, source_target_pairs={{0,192},{64,128},{128,64},{192,0},{1,193},{65,129},{129,65},{193,1... | collective-permute-start | bytes 1179656 | tf_op jit(solution)/shard_map/ppermute | solution.py:49
  213.4 19.2 %collective-permute-start.15 = (bf16[768,256]{1,0:T(8,128)(2,1)}, bf16[768,256]{1,0:T(8,128)(2,1)S(1)}, u32[]{:S(2)}, u32[]{:S(2)}) collective-permute-start(bf16[768,256]{1,0:T(8,128)(2,1)} %get-tuple-element.78), channel_id=1, source_target_pairs={{0,128},{64,192},{128,0},{192,64},{1,129},{65,193},{129,1},{193,65... | collective-permute-start | bytes 1179656 | tf_op jit(solution)/shard_map/ppermute | solution.py:49
  215.8 16.9 %collective-permute-start.14 = (bf16[768,256]{1,0:T(8,128)(2,1)}, bf16[768,256]{1,0:T(8,128)(2,1)S(1)}, u32[]{:S(2)}, u32[]{:S(2)}) collective-permute-start(bf16[768,256]{1,0:T(8,128)(2,1)} %get-tuple-element.79), channel_id=1, source_target_pairs={{0,64},{64,0},{128,192},{192,128},{1,65},{65,1},{129,193},{193,129... | collective-permute-start | bytes 1179656 | tf_op jit(solution)/shard_map/ppermute | solution.py:49
  233.0 7.2 %collective-permute-start.18 = (bf16[8,24,256]{2,1,0:T(8,128)(2,1)S(1)}, bf16[8,24,256]{2,1,0:T(8,128)(2,1)S(1)}, u32[]{:S(2)}, u32[]{:S(2)}) collective-permute-start(bf16[8,24,256]{2,1,0:T(8,128)(2,1)S(1)} %get-tuple-element.94), channel_id=1, source_target_pairs={{0,1},{1,0},{2,3},{3,2},{4,5},{5,4},{6,7},{7,6},{8,9},{9,8},{10,11... | collective-permute-start | bytes 294920 | tf_op jit(solution)/shard_map/ppermute | solution.py:49
  234.3 5.9 %collective-permute-start.20 = (bf16[8,24,256]{2,1,0:T(8,128)(2,1)S(1)}, bf16[8,24,256]{2,1,0:T(8,128)(2,1)S(1)}, u32[]{:S(2)}, u32[]{:S(2)}) collective-permute-start(bf16[8,24,256]{2,1,0:T(8,128)(2,1)S(1)} %get-tuple-element.95), channel_id=1, source_target_pairs={{0,3},{1,2},{2,1},{3,0},{4,7},{5,6},{6,5},{7,4},{8,11},{9,10},{10,... | collective-permute-start | bytes 294920 | tf_op jit(solution)/shard_map/ppermute | solution.py:49
  236.1 5.8 %collective-permute-start.19 = (bf16[8,24,256]{2,1,0:T(8,128)(2,1)S(1)}, bf16[8,24,256]{2,1,0:T(8,128)(2,1)S(1)}, u32[]{:S(2)}, u32[]{:S(2)}) collective-permute-start(bf16[8,24,256]{2,1,0:T(8,128)(2,1)S(1)} %get-tuple-element.96), channel_id=1, source_target_pairs={{0,2},{1,3},{2,0},{3,1},{4,6},{5,7},{6,4},{7,5},{8,10},{9,11},{10,... | collective-permute-start | bytes 294920 | tf_op jit(solution)/shard_map/ppermute | solution.py:49
  236.7 9.7 %all-to-all-start.7 = ((bf16[4,128,384]{2,1,0:T(8,128)(2,1)}), bf16[4,128,384]{2,1,0:T(8,128)(2,1)S(1)}, u32[]{:S(2)}, u32[]{:S(2)}) async-start(bf16[4,128,384]{2,1,0:T(8,128)(2,1)} %fusion.19), calls=%async_computation.7 | async-start | bytes 786432 | tf_op jit(solution)/shard_map/all_to_all | solution.py:41
  240.2 26.6 %copy-start.9 = (f32[128,1]{1,0:T(8,128)S(1)}, f32[128,1]{1,0:T(8,128)}, u32[]{:S(2)}) copy-start(f32[128,1]{1,0:T(8,128)} %copy-done.8) | copy-start | bytes 1540
  258.4 16.4 %all-to-all-start.9 = ((f32[8,96,128]{2,1,0:T(8,128)}), f32[8,96,128]{2,1,0:T(8,128)S(1)}, u32[]{:S(2)}, u32[]{:S(2)}) async-start(f32[8,96,128]{2,1,0:T(8,128)} %broadcast_in_dim.126), calls=%async_computation.9 | async-start | bytes 786432 | tf_op jit(solution)/shard_map/all_to_all | solution.py:41
  274.8 0.9 copy-start.1
  275.0 0.7 copy-start.14

commit v4 on v3

--- a/solution.py
+++ b/solution.py
@@ -91,34 +91,68 @@
             out_ref[at] = part_refs[by_core * X + by_x][...]
 
 
-def score_kernel(scale, place_ref, embedded_ref, positives_ref, hidden_ref, query_ref, *refs):
-    row_refs, (loss_ref, grad_ref, keep_ref, send_ref) = refs[:CHUNKS], refs[CHUNKS:]
+def weighted_rows(weight, rows):
+    high = weight.astype(jnp.bfloat16)
+    low = (weight - high.astype(jnp.float32)).astype(jnp.bfloat16)
+    return jnp.dot(high, rows, preferred_element_type=jnp.float32) + jnp.dot(
+        low, rows, preferred_element_type=jnp.float32
+    )
+
+
+def early_kernel(scale, embedded_ref, positives_ref, query_ref, *refs):
+    row_refs, (stats_ref, sum_ref) = refs[: CHUNKS - 1], refs[CHUNKS - 1 :]
+    embedded = embedded_ref[...]
+    positives = positives_ref[...].astype(jnp.float32)
+    q_dev = embedded.shape[0]
+    pos_scores = (
+        jnp.sum(embedded.astype(jnp.float32) * positives, axis=1, keepdims=True) * scale
+    )
+    per = row_refs[0].shape[0]
+    query = lax.broadcasted_iota(jnp.int32, (q_dev, per), 0)
+    scores, members, largest = [], [], pos_scores
+    for c in range(CHUNKS - 1):
+        score = contract_last(embedded, row_refs[c][...]) * scale
+        member = query_ref[:, c * per : (c + 1) * per] == query
+        seen = jnp.where(member, score, pos_scores)
+        largest = jnp.maximum(largest, jnp.max(seen, axis=1, keepdims=True))
+        scores.append(score)
+        members.append(member)
+    total = jnp.exp(pos_scores - largest)
+    grad = jnp.zeros(sum_ref.shape, jnp.float32)
+    for c in range(CHUNKS - 1):
+        weight = jnp.where(members[c], jnp.exp(scores[c] - largest), 0.0)
+        total = total + jnp.sum(weight, axis=1, keepdims=True)
+        grad = grad + weighted_rows(weight, row_refs[c][...])
+    stats_ref[0] = pos_scores
+    stats_ref[1] = largest
+    stats_ref[2] = total
+    sum_ref[...] = grad
+
+
+def score_kernel(
+    scale, place_ref, embedded_ref, positives_ref, hidden_ref, query_ref, stats_ref, sum_ref,
+    rows_ref, loss_ref, grad_ref, keep_ref, send_ref,
+):
     embedded = embedded_ref[...]
     positives = positives_ref[...].astype(jnp.float32)
     q_dev, width = embedded.shape
-    pos_scores = (
-        jnp.sum(embedded.astype(jnp.float32) * positives, axis=1, keepdims=True) * scale
-    )
-    total = jnp.exp(pos_scores)
-    per = row_refs[0].shape[0]
-    query = lax.broadcasted_iota(jnp.int32, (q_dev, per), 0)
-    scores, members = [], []
-    for c in range(CHUNKS):
-        score = contract_last(embedded, row_refs[c][...]) * scale
-        member = query_ref[:, c * per : (c + 1) * per] == query
-        total = total + jnp.sum(jnp.where(member, jnp.exp(score), 0.0), axis=1, keepdims=True)
-        scores.append(score)
-        members.append(member)
-    log_total = jnp.log(total)
+    pos_scores, early, total = stats_ref[0], stats_ref[1], stats_ref[2]
+    rows = rows_ref[...]
+    per = rows.shape[0]
+    score = contract_last(embedded, rows) * scale
+    member = query_ref[:, (CHUNKS - 1) * per :] == lax.broadcasted_iota(
+        jnp.int32, (q_dev, per), 0
+    )
+    largest = jnp.maximum(
+        early, jnp.max(jnp.where(member, score, early), axis=1, keepdims=True)
+    )
+    late = jnp.where(member, jnp.exp(score - largest), 0.0)
+    total = total * jnp.exp(early - largest) + jnp.sum(late, axis=1, keepdims=True)
+    log_total = largest + jnp.log(total)
     loss_ref[...] = log_total - pos_scores
     grad = (jnp.exp(pos_scores - log_total) - 1.0) * positives
-    for c in range(CHUNKS):
-        weight = jnp.where(members[c], jnp.exp(scores[c] - log_total), 0.0)
-        high = weight.astype(jnp.bfloat16)
-        low = (weight - high.astype(jnp.float32)).astype(jnp.bfloat16)
-        rows = row_refs[c][...]
-        grad = grad + jnp.dot(high, rows, preferred_element_type=jnp.float32)
-        grad = grad + jnp.dot(low, rows, preferred_element_type=jnp.float32)
+    grad = grad + jnp.exp(early - log_total) * sum_ref[...]
+    grad = grad + weighted_rows(late * (1.0 / total), rows)
     query_grad = (grad * scale).astype(jnp.bfloat16)
     grad_ref[...] = query_grad
     my_core = place_ref[1]
@@ -217,17 +251,15 @@
     rows_0 = exchange(own_0, "z")
     gathered = after(gathered, own_0)
     parts = [gathered] + [swap(gathered, "x", by) for by in range(1, X)]
-    (found_21,) = find([(2, 1)], own_0)
+    (found_21,) = find([(2, 1)], own_0, parts[1], parts[3])
     near_21 = swap(found_21, "y", 2)
     own_1 = found_01 + after(near_11, own_0)
-    rows_1 = exchange(
-        after(own_1, rows_0, near_31, near_20, found_21, parts[1], parts[3]), "z"
-    )
-    rows_2 = exchange(after(near_20 + near_30, rows_1, near_21, parts[2]), "z")
+    rows_1 = exchange(after(own_1, rows_0, near_31), "z")
+    rows_2 = exchange(after(near_20 + near_30, rows_1, parts[2], found_21), "z")
     other_1 = near_21 + near_31
     rows_3 = exchange(after(other_1, rows_2), "z")
     chunks = [rows_0, rows_1, rows_2, rows_3]
-    parts = after(tuple(parts + [swap(part, "core", 1) for part in parts]), rows_1, other_1)
+    parts = after(tuple(parts + [swap(part, "core", 1) for part in parts]), rows_1)
     halves = pl.pallas_call(
         arrange_kernel,
         out_shape=jax.ShapeDtypeStruct((X, CORE, SHARD, *piece.shape), piece.dtype),
@@ -256,6 +288,14 @@
 
     half = width // CORE
     outer_cut = jax.ShapeDtypeStruct((Y, X, hid // Y // X, half), jnp.bfloat16)
+    stats, early_sum = pl.pallas_call(
+        functools.partial(early_kernel, scale),
+        out_shape=[
+            jax.ShapeDtypeStruct((3, q_dev, 1), jnp.float32),
+            jax.ShapeDtypeStruct((q_dev, width), jnp.float32),
+        ],
+        **limits,
+    )(embedded, positives, slot_query, *chunks[:-1])
     losses, query_grad, outer, outer_sent = pl.pallas_call(
         functools.partial(score_kernel, scale),
         out_shape=[
@@ -264,9 +304,9 @@
             outer_cut,
             outer_cut,
         ],
-        in_specs=[in_smem] + [in_vmem] * (4 + CHUNKS),
+        in_specs=[in_smem] + [in_vmem] * 7,
         **limits,
-    )(place, embedded, positives, hidden, slot_query, *chunks)
+    )(place, embedded, positives, hidden, slot_query, stats, early_sum, chunks[-1])
     outer_sent = swap(outer_sent, "core", 1)
     inner, inner_sent = pl.pallas_call(
         inner_kernel,
@@ -295,7 +335,7 @@
         axis=1,
     )
     both = total_of(list(exchange(narrow(both), "z")))
-    both = spread(both, ("x", "core"), GRP)
+    both = spread(narrow(both), ("x", "core"), GRP).astype(jnp.float32)
     inner_deep = inner_rows * wide // lanes
     inner = rows_to_columns(both[:, :inner_deep], inner_rows)
     outer = rows_to_columns(both[:, inner_deep:], outer_rows // X)

time: 277 us -> 285 us (1.029)
  starting transfers between devices: 95.3 us -> 112 us
  waiting for transfers between devices: 62.2 us -> 53.5 us
    ppermute x21, starting transfers between devices: 37.9 us -> 54.1 us  [swap(): lax.ppermute(value, axis, [(i, i ^ by) for i in range(lax.axis_size(axis))])]
    all_to_all x9, waiting for transfers between devices: 41.8 us -> 35.3 us  [exchange(): return lax.all_to_all(value, axes, split_axis=0, concat_axis=0, tiled=True)]
    unnamed x39 -> x52, local copies, waits for them, and re-layouts: 5.83 us -> 8.29 us
  transfers between devices with their start and end apart: 30 -> 30, of which waited for: 15 -> 11; matrix products, arithmetic and copies ran while one was open for 23% -> 21% of each run, Pallas kernels for 4% -> 5%
where the time goes in v4:
time: 285 us; the launch traced here: 284 us
  starting transfers between devices  112 us (39%)
  waiting for transfers between devices  53.5 us (19%)
  local copies, waits for them, and re-layouts  51.9 us (18%)
  Pallas kernels  23.4 us (8%)
  other arithmetic  22.4 us (8%)
  blocking collectives  11.1 us (4%)
  matrix products  7.93 us (3%)
    all_to_all x9, starting transfers between devices, exchange(): return lax.all_to_all(value, axes, split_axis=0, concat_axis=0, tiled=True)  58.1 us
    ppermute x21, starting transfers between devices, swap(): lax.ppermute(value, axis, [(i, i ^ by) for i in range(lax.axis_size(axis))])  54.1 us
    all_to_all x9, waiting for transfers between devices, exchange(): return lax.all_to_all(value, axes, split_axis=0, concat_axis=0, tiled=True)  35.3 us
    gather x4, local copies, waits for them, and re-layouts, find(): passage_table.at[ids].get(mode='promise_in_bounds')  31.8 us
    ppermute x21, waiting for transfers between devices, swap(): lax.ppermute(value, axis, [(i, i ^ by) for i in range(lax.axis_size(axis))])  18.2 us
    all_to_all x1, blocking collectives, exchange(): return lax.all_to_all(value, axes, split_axis=0, concat_axis=0, tiled=True)  11.1 us
    unnamed x52, local copies, waits for them, and re-layouts  8.29 us
    dot_general x8, matrix products, shards(): jnp.dot(queries, part, preferred_element_type=jnp.float32)  7.32 us
  transfers between devices with their start and end apart: 30, of which 11 were waited for; matrix products, arithmetic and copies ran while one was open for 21% of the time, Pallas kernels for 5%

profile of v4, /device:TPU:1, one launch (start us, length us, event | category | flops | bytes accessed | tf_op | source)
XLA Modules:
  0.0 283.7 jit_solution(10755675881840245965)
XLA Ops:
  1.5 5.8 %shard_map.85 = (s32[16,128]{1,0:T(8,128)S(1)}, s32[16,128]{1,0:T(8,128)S(1)}) custom-call(s32[128,16]{1,0:T(8,128)S(1)} %copy.33.ids_ref), custom_call_target="tpu_custom_call" | custom-call | tf_op jit(solution)/shard_map/pallas_call | solution.py:216
  7.9 12.0 %all-to-all-start = ((s32[32,1,128]{2,1,0:T(1,128)}), s32[32,1,128]{2,1,0:T(1,128)S(1)}, u32[]{:S(2)}, u32[]{:S(2)}) async-start(s32[32,1,128]{2,1,0:T(1,128)} %bitcast.2), calls=%async_computation | async-start | bytes 32768 | tf_op jit(solution)/shard_map/all_to_all | solution.py:41
  20.8 7.7 %all-to-all-done = s32[32,1,128]{2,1,0:T(1,128)S(1)} async-done(((s32[32,1,128]{2,1,0:T(1,128)}), s32[32,1,128]{2,1,0:T(1,128)S(1)}, u32[]{:S(2)}, u32[]{:S(2)}) %all-to-all-start) | async-done | bytes 16416 | tf_op jit(solution)/shard_map/all_to_all | solution.py:41
  29.0 8.1 %gather_fusion = bf16[1024,768]{1,0:T(8,128)(2,1)S(1)} fusion(bf16[4096,768]{1,0:T(8,128)(2,1)} %param.9, s32[1024]{0:T(1024)S(1)} %fusion.40), kind=kCustom, calls=%fused_computation | custom fusion | bytes 3149824 | tf_op jit(solution)/shard_map/gather | solution.py:232
  37.0 1.4 slice_select_fusion.2
  39.3 3.9 %all-to-all-start.1 = ((bf16[32,16,768]{2,1,0:T(8,128)(2,1)}), bf16[32,16,768]{2,1,0:T(8,128)(2,1)S(1)}, u32[]{:S(2)}, u32[]{:S(2)}) async-start(bf16[32,16,768]{2,1,0:T(8,128)(2,1)} %broadcast_in_dim.107), calls=%async_computation.1 | async-start | bytes 1572864 | tf_op jit(solution)/shard_map/all_to_all | solution.py:41
  44.5 1.8 collective-permute-start.1
  46.4 9.7 %gather_fusion.1 = bf16[1536,768]{1,0:T(8,128)(2,1)S(1)} fusion(bf16[4096,768]{1,0:T(8,128)(2,1)} %param.9, s32[2048]{0:T(1024)S(1)} %pad_clamp_fusion), kind=kCustom, calls=%fused_computation.1 | custom fusion | bytes 4724736 | tf_op jit(solution)/shard_map/gather | solution.py:232
  56.3 1.4 slice_select_fusion.3
  58.0 10.8 %collective-permute-done = bf16[512,768]{1,0:T(8,128)(2,1)} collective-permute-done((bf16[512,768]{1,0:T(8,128)(2,1)}, bf16[512,768]{1,0:T(8,128)(2,1)}, u32[]{:S(2)}, u32[]{:S(2)}) %collective-permute-start) | collective-permute-done | bytes 786464 | tf_op jit(solution)/shard_map/ppermute | solution.py:49
  68.8 2.2 fusion.14
  72.0 6.5 %all-to-all-start.2 = ((bf16[8,64,768]{2,1,0:T(8,128)(2,1)}), bf16[8,64,768]{2,1,0:T(8,128)(2,1)S(1)}, u32[]{:S(2)}, u32[]{:S(2)}) async-start(bf16[8,64,768]{2,1,0:T(8,128)(2,1)} %bitcast.182), calls=%async_computation.2 | async-start | bytes 1572864 | tf_op jit(solution)/shard_map/all_to_all | solution.py:41
  78.5 2.0 collective-permute-start.10
  81.7 1.8 collective-permute-start.4
  83.8 8.1 %gather_fusion.2 = bf16[1024,768]{1,0:T(8,128)(2,1)S(1)} fusion(bf16[4096,768]{1,0:T(8,128)(2,1)} %param.9, s32[1024]{0:T(1024)S(1)} %fusion.41), kind=kCustom, calls=%fused_computation.2 | custom fusion | bytes 3149824 | tf_op jit(solution)/shard_map/gather | solution.py:232
  91.9 2.5 slice_select_fusion
  96.4 6.5 %collective-permute-start.5 = (bf16[32,16,768]{2,1,0:T(8,128)(2,1)S(1)}, bf16[32,16,768]{2,1,0:T(8,128)(2,1)}, u32[]{:S(2)}, u32[]{:S(2)}) collective-permute-start(bf16[32,16,768]{2,1,0:T(8,128)(2,1)S(1)} %all-to-all-done.1.refs_0_), channel_id=1, source_target_pairs={{0,32},{32,0},{1,33},{33,1},{2,34},{34,2},{3,35},{35,3},{4,36},{36... | collective-permute-start | bytes 2359304 | tf_op jit(solution)/shard_map/ppermute | solution.py:49
  102.9 6.8 %all-to-all-start.3 = ((bf16[8,64,768]{2,1,0:T(8,128)(2,1)}), bf16[8,64,768]{2,1,0:T(8,128)(2,1)S(1)}, u32[]{:S(2)}, u32[]{:S(2)}) async-start(bf16[8,64,768]{2,1,0:T(8,128)(2,1)} %bitcast.183), calls=%async_computation.3 | async-start | bytes 1572864 | tf_op jit(solution)/shard_map/all_to_all | solution.py:41
  109.6 6.0 %gather_fusion.3 = bf16[512,768]{1,0:T(8,128)(2,1)S(1)} fusion(bf16[4096,768]{1,0:T(8,128)(2,1)} %param.9, s32[1024]{0:T(1024)S(1)} %pad_clamp_fusion.1), kind=kCustom, calls=%fused_computation.3 | custom fusion | bytes 1574912 | tf_op jit(solution)/shard_map/gather | solution.py:232
  116.7 18.0 %collective-permute-start.6 = (bf16[32,16,768]{2,1,0:T(8,128)(2,1)}, bf16[32,16,768]{2,1,0:T(8,128)(2,1)}, u32[]{:S(2)}, u32[]{:S(2)}) collective-permute-start(bf16[32,16,768]{2,1,0:T(8,128)(2,1)} %collective-permute-done.2.refs_1_), channel_id=1, source_target_pairs={{0,32},{32,0},{1,33},{33,1},{2,34},{34,2},{3,35},{35,3},{4,36},{36... | collective-permute-start | bytes 2359304 | tf_op jit(solution)/shard_map/ppermute | solution.py:49
  135.7 2.5 add.184
  138.1 2.2 add.187
  140.4 6.9 %all-to-all-start.4 = ((bf16[8,64,768]{2,1,0:T(8,128)(2,1)}), bf16[8,64,768]{2,1,0:T(8,128)(2,1)S(1)}, u32[]{:S(2)}, u32[]{:S(2)}) async-start(bf16[8,64,768]{2,1,0:T(8,128)(2,1)} %bitcast.184), calls=%async_computation.4 | async-start | bytes 1572864 | tf_op jit(solution)/shard_map/all_to_all | solution.py:41
  147.3 5.6 %shard_map.86 = bf16[4,2,32,16,768]{4,3,2,1,0:T(8,128)(2,1)} custom-call(s32[2]{0:T(128)S(1)} %pad_add_fusion.4.place_ref, bf16[32,16,768]{2,1,0:T(8,128)(2,1)S(1)} %all-to-all-done.1.refs_0_, bf16[32,16,768]{2,1,0:T(8,128)(2,1)} %collective-permute-done.2.refs_1_, bf16[32,16,768]{2,1,0:T(8,128)(2,1)} %collective-permute-done.3.refs_2_, ...), custom_call_target="tpu_custom_call" | custom-call | tf_op jit(solution)/shard_map/pallas_call | solution.py:263
  153.0 2.2 slice_bitcast_fusion.1
  162.4 1.9 slice_bitcast_fusion
  165.2 6.6 %all-to-all-start.5 = ((bf16[8,64,768]{2,1,0:T(8,128)(2,1)}), bf16[8,64,768]{2,1,0:T(8,128)(2,1)S(1)}, u32[]{:S(2)}, u32[]{:S(2)}) async-start(bf16[8,64,768]{2,1,0:T(8,128)(2,1)} %bitcast.41), calls=%async_computation.5 | async-start | bytes 1572864 | tf_op jit(solution)/shard_map/all_to_all | solution.py:41
  171.9 2.3 copy.42
  176.1 1.7 fusion.12
  179.2 2.3 shard_map.87
  183.0 3.8 %all-to-all-done.5 = bf16[8,64,768]{2,1,0:T(8,128)(2,1)S(1)} async-done(((bf16[8,64,768]{2,1,0:T(8,128)(2,1)}), bf16[8,64,768]{2,1,0:T(8,128)(2,1)S(1)}, u32[]{:S(2)}, u32[]{:S(2)}) %all-to-all-start.5) | async-done | bytes 786464 | tf_op jit(solution)/shard_map/all_to_all | solution.py:41
  189.7 4.3 %shard_map.88 = (f32[128,1]{1,0:T(8,128)S(1)}, bf16[128,768]{1,0:T(8,128)(2,1)S(1)}, bf16[4,4,128,384]{3,2,1,0:T(8,128)(2,1)}, bf16[4,4,128,384]{3,2,1,0:T(8,128)(2,1)}) custom-call(s32[2]{0:T(128)S(1)} %pad_add_fusion.4.place_ref, bf16[128,768]{1,0:T(8,128)(2,1)S(1)} %fusion.embedded_ref, bf16[128,768]{1,0:T(8,128)(2,1)S(1)} %copy-done.8, ...), custom_call_target="tpu_custom_call" | custom-call | tf_op jit(solution)/shard_map/pallas_call | solution.py:299
  194.6 11.4 %collective-permute-start.17 = (bf16[4,4,128,384]{3,2,1,0:T(8,128)(2,1)}, bf16[4,4,128,384]{3,2,1,0:T(8,128)(2,1)S(1)}, u32[]{:S(2)}, u32[]{:S(2)}) collective-permute-start(bf16[4,4,128,384]{3,2,1,0:T(8,128)(2,1)} %get-tuple-element.68), channel_id=1, source_target_pairs={{0,32},{32,0},{1,33},{33,1},{2,34},{34,2},{3,35},{35,3},{4,36},{36... | collective-permute-start | bytes 4718600 | tf_op jit(solution)/shard_map/ppermute | solution.py:49
  206.0 5.3 %shard_map.89 = (bf16[4,768,256]{2,1,0:T(8,128)(2,1)S(1)}, bf16[4,768,256]{2,1,0:T(8,128)(2,1)}) custom-call(s32[2]{0:T(128)S(1)} %pad_add_fusion.4.place_ref, bf16[128,768]{1,0:T(8,128)(2,1)S(1)} %copy-done.2, bf16[128,768]{1,0:T(8,128)(2,1)S(1)} %get-tuple-element.64.grad_ref, f32[128,2048]{1,0:T(8,128)S(1)} %get-tuple-element.91.slope_ref, ...), custom_call_target="tpu_custom_call" | custom-call | tf_op jit(solution)/shard_map/pallas_call | solution.py:311
  211.3 1.7 add_convert_fusion
  213.0 3.6 %all-to-all-start.6 = ((bf16[4,4,128,384]{3,2,1,0:T(8,128)(2,1)}), bf16[4,4,128,384]{3,2,1,0:T(8,128)(2,1)S(1)}, u32[]{:S(2)}, u32[]{:S(2)}) async-start(bf16[4,4,128,384]{3,2,1,0:T(8,128)(2,1)} %add_convert_fusion), calls=%async_computation.6 | async-start | bytes 3145728 | tf_op jit(solution)/shard_map/all_to_all | solution.py:41
  216.6 2.8 fusion.18
  219.3 4.0 %collective-permute-start.15 = (bf16[768,256]{1,0:T(8,128)(2,1)}, bf16[768,256]{1,0:T(8,128)(2,1)S(1)}, u32[]{:S(2)}, u32[]{:S(2)}) collective-permute-start(bf16[768,256]{1,0:T(8,128)(2,1)} %get-tuple-element.82), channel_id=1, source_target_pairs={{0,128},{64,192},{128,0},{192,64},{1,129},{65,193},{129,1},{193,65... | collective-permute-start | bytes 1179656 | tf_op jit(solution)/shard_map/ppermute | solution.py:49
  223.5 13.3 %all-to-all-done.6 = bf16[4,4,128,384]{3,2,1,0:T(8,128)(2,1)S(1)} async-done(((bf16[4,4,128,384]{3,2,1,0:T(8,128)(2,1)}), bf16[4,4,128,384]{3,2,1,0:T(8,128)(2,1)S(1)}, u32[]{:S(2)}, u32[]{:S(2)}) %all-to-all-start.6) | async-done | bytes 1572896 | tf_op jit(solution)/shard_map/all_to_all | solution.py:41
  237.8 2.8 collective-permute-done.15
  240.6 2.1 collective-permute-done.16
  242.9 1.3 collective-permute-start.18
  244.2 2.4 collective-permute-start.19
  246.9 3.5 %all-to-all-start.7 = ((bf16[4,128,384]{2,1,0:T(8,128)(2,1)}), bf16[4,128,384]{2,1,0:T(8,128)(2,1)S(1)}, u32[]{:S(2)}, u32[]{:S(2)}) async-start(bf16[4,128,384]{2,1,0:T(8,128)(2,1)} %fusion.19), calls=%async_computation.7 | async-start | bytes 786432 | tf_op jit(solution)/shard_map/all_to_all | solution.py:41
  251.4 5.2 %all-to-all-done.7 = bf16[4,128,384]{2,1,0:T(8,128)(2,1)S(1)} async-done(((bf16[4,128,384]{2,1,0:T(8,128)(2,1)}), bf16[4,128,384]{2,1,0:T(8,128)(2,1)S(1)}, u32[]{:S(2)}, u32[]{:S(2)}) %all-to-all-start.7) | async-done | bytes 393248 | tf_op jit(solution)/shard_map/all_to_all | solution.py:41
  256.7 11.1 %all_to_all.78 = bf16[8,96,128]{2,1,0:T(8,128)(2,1)S(1)} all-to-all(bf16[8,96,128]{2,1,0:T(8,128)(2,1)S(1)} %constant_dynamic-update-slice_fusion.4), channel_id=1, replica_groups=mesh['x'=4,'core'=2,'z'=8,'y'=4] {'z'}, dimensions={0} | all-to-all | bytes 393216 | tf_op jit(solution)/shard_map/all_to_all | solution.py:41
  268.5 8.3 %all-to-all-start.9 = ((bf16[8,96,128]{2,1,0:T(8,128)(2,1)}), bf16[8,96,128]{2,1,0:T(8,128)(2,1)S(1)}, u32[]{:S(2)}, u32[]{:S(2)}) async-start(bf16[8,96,128]{2,1,0:T(8,128)(2,1)} %broadcast_in_dim.126), calls=%async_computation.9 | async-start | bytes 393216 | tf_op jit(solution)/shard_map/all_to_all | solution.py:41
  277.5 5.3 %all-to-all-done.9 = bf16[8,96,128]{2,1,0:T(8,128)(2,1)S(1)} async-done(((bf16[8,96,128]{2,1,0:T(8,128)(2,1)}), bf16[8,96,128]{2,1,0:T(8,128)(2,1)S(1)}, u32[]{:S(2)}, u32[]{:S(2)}) %all-to-all-start.9) | async-done | bytes 196640 | tf_op jit(solution)/shard_map/all_to_all | solution.py:41
  (176 shorter events, 33.4 us)
Async XLA Ops:
  0.6 19.4 %copy-start = (bf16[64,768]{1,0:T(8,128)(2,1)S(1)}, bf16[64,768]{1,0:T(8,128)(2,1)}, u32[]{:S(2)}) copy-start(bf16[64,768]{1,0:T(8,128)(2,1)} %param.11) | copy-start | bytes 294916
  7.9 20.6 %all-to-all-start = ((s32[32,1,128]{2,1,0:T(1,128)}), s32[32,1,128]{2,1,0:T(1,128)S(1)}, u32[]{:S(2)}, u32[]{:S(2)}) async-start(s32[32,1,128]{2,1,0:T(1,128)} %bitcast.2), calls=%async_computation | async-start | bytes 32768 | tf_op jit(solution)/shard_map/all_to_all | solution.py:41
  39.3 32.7 %all-to-all-start.1 = ((bf16[32,16,768]{2,1,0:T(8,128)(2,1)}), bf16[32,16,768]{2,1,0:T(8,128)(2,1)S(1)}, u32[]{:S(2)}, u32[]{:S(2)}) async-start(bf16[32,16,768]{2,1,0:T(8,128)(2,1)} %broadcast_in_dim.107), calls=%async_computation.1 | async-start | bytes 1572864 | tf_op jit(solution)/shard_map/all_to_all | solution.py:41
  43.2 25.5 %collective-permute-start = (bf16[512,768]{1,0:T(8,128)(2,1)}, bf16[512,768]{1,0:T(8,128)(2,1)}, u32[]{:S(2)}, u32[]{:S(2)}) collective-permute-start(bf16[512,768]{1,0:T(8,128)(2,1)} %get-tuple-element.90), channel_id=1, source_target_pairs={{0,1},{1,0},{2,3},{3,2},{4,5},{5,4},{6,7},{7,6},{8,9},{9,8},{10,11... | collective-permute-start | bytes 2359304 | tf_op jit(solution)/shard_map/ppermute | solution.py:49
  44.5 27.5 %collective-permute-start.1 = (bf16[512,768]{1,0:T(8,128)(2,1)}, bf16[512,768]{1,0:T(8,128)(2,1)}, u32[]{:S(2)}, u32[]{:S(2)}) collective-permute-start(bf16[512,768]{1,0:T(8,128)(2,1)} %get-tuple-element.89), channel_id=1, source_target_pairs={{0,3},{1,2},{2,1},{3,0},{4,7},{5,6},{6,5},{7,4},{8,11},{9,10},{10,... | collective-permute-start | bytes 2359304 | tf_op jit(solution)/shard_map/ppermute | solution.py:49
  57.7 34.2 %collective-permute-start.9 = (bf16[512,768]{1,0:T(8,128)(2,1)}, bf16[512,768]{1,0:T(8,128)(2,1)}, u32[]{:S(2)}, u32[]{:S(2)}) collective-permute-start(bf16[512,768]{1,0:T(8,128)(2,1)} %get-tuple-element.86), channel_id=1, source_target_pairs={{0,1},{1,0},{2,3},{3,2},{4,5},{5,4},{6,7},{7,6},{8,9},{9,8},{10,11... | collective-permute-start | bytes 2359304 | tf_op jit(solution)/shard_map/ppermute | solution.py:49
  72.0 30.9 %all-to-all-start.2 = ((bf16[8,64,768]{2,1,0:T(8,128)(2,1)}), bf16[8,64,768]{2,1,0:T(8,128)(2,1)S(1)}, u32[]{:S(2)}, u32[]{:S(2)}) async-start(bf16[8,64,768]{2,1,0:T(8,128)(2,1)} %bitcast.182), calls=%async_computation.2 | async-start | bytes 1572864 | tf_op jit(solution)/shard_map/all_to_all | solution.py:41
  78.5 24.4 %collective-permute-start.10 = (bf16[512,768]{1,0:T(8,128)(2,1)}, bf16[512,768]{1,0:T(8,128)(2,1)}, u32[]{:S(2)}, u32[]{:S(2)}) collective-permute-start(bf16[512,768]{1,0:T(8,128)(2,1)} %get-tuple-element.85), channel_id=1, source_target_pairs={{0,3},{1,2},{2,1},{3,0},{4,7},{5,6},{6,5},{7,4},{8,11},{9,10},{10,... | collective-permute-start | bytes 2359304 | tf_op jit(solution)/shard_map/ppermute | solution.py:49
  80.5 15.9 %collective-permute-start.2 = (bf16[32,16,768]{2,1,0:T(8,128)(2,1)S(1)}, bf16[32,16,768]{2,1,0:T(8,128)(2,1)}, u32[]{:S(2)}, u32[]{:S(2)}) collective-permute-start(bf16[32,16,768]{2,1,0:T(8,128)(2,1)S(1)} %all-to-all-done.1.refs_0_), channel_id=1, source_target_pairs={{0,64},{64,0},{128,192},{192,128},{1,65},{65,1},{129,193},{193,129... | collective-permute-start | bytes 2359304 | tf_op jit(solution)/shard_map/ppermute | solution.py:49
  81.7 21.2 %collective-permute-start.4 = (bf16[32,16,768]{2,1,0:T(8,128)(2,1)S(1)}, bf16[32,16,768]{2,1,0:T(8,128)(2,1)}, u32[]{:S(2)}, u32[]{:S(2)}) collective-permute-start(bf16[32,16,768]{2,1,0:T(8,128)(2,1)S(1)} %all-to-all-done.1.refs_0_), channel_id=1, source_target_pairs={{0,192},{64,128},{128,64},{192,0},{1,193},{65,129},{129,65},{193,1... | collective-permute-start | bytes 2359304 | tf_op jit(solution)/shard_map/ppermute | solution.py:49
  94.4 40.3 %collective-permute-start.11 = (bf16[512,768]{1,0:T(8,128)(2,1)}, bf16[512,768]{1,0:T(8,128)(2,1)}, u32[]{:S(2)}, u32[]{:S(2)}) collective-permute-start(bf16[512,768]{1,0:T(8,128)(2,1)} %get-tuple-element.87), channel_id=1, source_target_pairs={{0,2},{1,3},{2,0},{3,1},{4,6},{5,7},{6,4},{7,5},{8,10},{9,11},{10,... | collective-permute-start | bytes 2359304 | tf_op jit(solution)/shard_map/ppermute | solution.py:49
  95.0 39.7 %collective-permute-start.3 = (bf16[32,16,768]{2,1,0:T(8,128)(2,1)S(1)}, bf16[32,16,768]{2,1,0:T(8,128)(2,1)}, u32[]{:S(2)}, u32[]{:S(2)}) collective-permute-start(bf16[32,16,768]{2,1,0:T(8,128)(2,1)S(1)} %all-to-all-done.1.refs_0_), channel_id=1, source_target_pairs={{0,128},{64,192},{128,0},{192,64},{1,129},{65,193},{129,1},{193,65... | collective-permute-start | bytes 2359304 | tf_op jit(solution)/shard_map/ppermute | solution.py:49
  96.4 50.9 %collective-permute-start.5 = (bf16[32,16,768]{2,1,0:T(8,128)(2,1)S(1)}, bf16[32,16,768]{2,1,0:T(8,128)(2,1)}, u32[]{:S(2)}, u32[]{:S(2)}) collective-permute-start(bf16[32,16,768]{2,1,0:T(8,128)(2,1)S(1)} %all-to-all-done.1.refs_0_), channel_id=1, source_target_pairs={{0,32},{32,0},{1,33},{33,1},{2,34},{34,2},{3,35},{35,3},{4,36},{36... | collective-permute-start | bytes 2359304 | tf_op jit(solution)/shard_map/ppermute | solution.py:49
  102.9 37.5 %all-to-all-start.3 = ((bf16[8,64,768]{2,1,0:T(8,128)(2,1)}), bf16[8,64,768]{2,1,0:T(8,128)(2,1)S(1)}, u32[]{:S(2)}, u32[]{:S(2)}) async-start(bf16[8,64,768]{2,1,0:T(8,128)(2,1)} %bitcast.183), calls=%async_computation.3 | async-start | bytes 1572864 | tf_op jit(solution)/shard_map/all_to_all | solution.py:41
  116.7 21.4 %collective-permute-start.12 = (bf16[512,768]{1,0:T(8,128)(2,1)}, bf16[512,768]{1,0:T(8,128)(2,1)S(1)}, u32[]{:S(2)}, u32[]{:S(2)}) collective-permute-start(bf16[512,768]{1,0:T(8,128)(2,1)} %broadcast_select_fusion), channel_id=1, source_target_pairs={{0,2},{1,3},{2,0},{3,1},{4,6},{5,7},{6,4},{7,5},{8,10},{9,11},{10,... | collective-permute-start | bytes 2359304 | tf_op jit(solution)/shard_map/ppermute | solution.py:49
  116.7 30.6 %collective-permute-start.6 = (bf16[32,16,768]{2,1,0:T(8,128)(2,1)}, bf16[32,16,768]{2,1,0:T(8,128)(2,1)}, u32[]{:S(2)}, u32[]{:S(2)}) collective-permute-start(bf16[32,16,768]{2,1,0:T(8,128)(2,1)} %collective-permute-done.2.refs_1_), channel_id=1, source_target_pairs={{0,32},{32,0},{1,33},{33,1},{2,34},{34,2},{3,35},{35,3},{4,36},{36... | collective-permute-start | bytes 2359304 | tf_op jit(solution)/shard_map/ppermute | solution.py:49
  134.7 12.6 %collective-permute-start.8 = (bf16[32,16,768]{2,1,0:T(8,128)(2,1)}, bf16[32,16,768]{2,1,0:T(8,128)(2,1)}, u32[]{:S(2)}, u32[]{:S(2)}) collective-permute-start(bf16[32,16,768]{2,1,0:T(8,128)(2,1)} %collective-permute-done.4.refs_3_), channel_id=1, source_target_pairs={{0,32},{32,0},{1,33},{33,1},{2,34},{34,2},{3,35},{35,3},{4,36},{36... | collective-permute-start | bytes 2359304 | tf_op jit(solution)/shard_map/ppermute | solution.py:49
  134.7 12.6 %collective-permute-start.7 = (bf16[32,16,768]{2,1,0:T(8,128)(2,1)}, bf16[32,16,768]{2,1,0:T(8,128)(2,1)}, u32[]{:S(2)}, u32[]{:S(2)}) collective-permute-start(bf16[32,16,768]{2,1,0:T(8,128)(2,1)} %collective-permute-done.3.refs_2_), channel_id=1, source_target_pairs={{0,32},{32,0},{1,33},{33,1},{2,34},{34,2},{3,35},{35,3},{4,36},{36... | collective-permute-start | bytes 2359304 | tf_op jit(solution)/shard_map/ppermute | solution.py:49
  140.4 12.6 %copy-start.3 = (bf16[8,64,768]{2,1,0:T(8,128)(2,1)}, bf16[8,64,768]{2,1,0:T(8,128)(2,1)S(1)}, u32[]{:S(2)}) copy-start(bf16[8,64,768]{2,1,0:T(8,128)(2,1)S(1)} %all-to-all-done.3) | copy-start | bytes 2359300
  140.4 23.9 %all-to-all-start.4 = ((bf16[8,64,768]{2,1,0:T(8,128)(2,1)}), bf16[8,64,768]{2,1,0:T(8,128)(2,1)S(1)}, u32[]{:S(2)}, u32[]{:S(2)}) async-start(bf16[8,64,768]{2,1,0:T(8,128)(2,1)} %bitcast.184), calls=%async_computation.4 | async-start | bytes 1572864 | tf_op jit(solution)/shard_map/all_to_all | solution.py:41
  153.0 9.5 %slice-start = ((s8[6291456]{0:T(1024)(128)(4,1)}), s8[4194304]{0:T(1024)(128)(4,1)S(1)}, s32[]{:S(2)}) async-start(s8[6291456]{0:T(1024)(128)(4,1)} %bitcast.180), calls=%async_computation.10 | async-start | bytes 8388608
  156.0 0.9 copy-start.2
  156.0 6.4 %slice-start.1 = ((s8[6291456]{0:T(1024)(128)(4,1)}), s8[2097152]{0:T(1024)(128)(4,1)S(1)}, s32[]{:S(2)}) async-start(s8[6291456]{0:T(1024)(128)(4,1)} %bitcast.180), calls=%async_computation.11 | async-start | bytes 4194304
  164.3 7.5 %copy-start.18 = (bf16[32,8,256]{2,1,0:T(8,128)(2,1)S(1)}, bf16[32,8,256]{2,1,0:T(8,128)(2,1)}, u32[]{:S(2)}) copy-start(bf16[32,8,256]{2,1,0:T(8,128)(2,1)} %get-tuple-element.101) | copy-start | bytes 393220
  164.3 0.9 copy-start.5
  165.2 21.6 %all-to-all-start.5 = ((bf16[8,64,768]{2,1,0:T(8,128)(2,1)}), bf16[8,64,768]{2,1,0:T(8,128)(2,1)S(1)}, u32[]{:S(2)}, u32[]{:S(2)}) async-start(bf16[8,64,768]{2,1,0:T(8,128)(2,1)} %bitcast.41), calls=%async_computation.5 | async-start | bytes 1572864 | tf_op jit(solution)/shard_map/all_to_all | solution.py:41
  174.1 3.7 %copy-start.15 = (bf16[32,4,2,8,768]{4,3,2,1,0:T(8,128)(2,1)}, bf16[32,4,2,8,768]{4,3,2,1,0:T(8,128)(2,1)S(1)}, u32[]{:S(2)}) copy-start(bf16[32,4,2,8,768]{4,3,2,1,0:T(8,128)(2,1)S(1)} %copy.42) | copy-start | bytes 9437188
  177.8 1.1 copy-start.4
  177.8 1.4 copy-start.6
  177.9 1.4 copy-start.7
  186.8 0.9 copy-start.8
  187.8 1.0 copy-start.10
  188.7 0.9 copy-start.12
  194.6 16.7 %collective-permute-start.17 = (bf16[4,4,128,384]{3,2,1,0:T(8,128)(2,1)}, bf16[4,4,128,384]{3,2,1,0:T(8,128)(2,1)S(1)}, u32[]{:S(2)}, u32[]{:S(2)}) collective-permute-start(bf16[4,4,128,384]{3,2,1,0:T(8,128)(2,1)} %get-tuple-element.68), channel_id=1, source_target_pairs={{0,32},{32,0},{1,33},{33,1},{2,34},{34,2},{3,35},{35,3},{4,36},{36... | collective-permute-start | bytes 4718600 | tf_op jit(solution)/shard_map/ppermute | solution.py:49
  206.0 5.3 %copy-start.16 = (bf16[4,4,128,384]{3,2,1,0:T(8,128)(2,1)S(1)}, bf16[4,4,128,384]{3,2,1,0:T(8,128)(2,1)}, u32[]{:S(2)}) copy-start(bf16[4,4,128,384]{3,2,1,0:T(8,128)(2,1)} %get-tuple-element.67) | copy-start | bytes 4718596
  211.3 5.2 %collective-permute-start.13 = (bf16[4,768,256]{2,1,0:T(8,128)(2,1)}, bf16[4,768,256]{2,1,0:T(8,128)(2,1)}, u32[]{:S(2)}, u32[]{:S(2)}) collective-permute-start(bf16[4,768,256]{2,1,0:T(8,128)(2,1)} %get-tuple-element.66), channel_id=1, source_target_pairs={{0,32},{32,0},{1,33},{33,1},{2,34},{34,2},{3,35},{35,3},{4,36},{36... | collective-permute-start | bytes 4718600 | tf_op jit(solution)/shard_map/ppermute | solution.py:49
  213.0 23.8 %all-to-all-start.6 = ((bf16[4,4,128,384]{3,2,1,0:T(8,128)(2,1)}), bf16[4,4,128,384]{3,2,1,0:T(8,128)(2,1)S(1)}, u32[]{:S(2)}, u32[]{:S(2)}) async-start(bf16[4,4,128,384]{3,2,1,0:T(8,128)(2,1)} %add_convert_fusion), calls=%async_computation.6 | async-start | bytes 3145728 | tf_op jit(solution)/shard_map/all_to_all | solution.py:41
  219.3 23.4 %copy-start.17 = (bf16[768,256]{1,0:T(8,128)(2,1)S(1)}, bf16[768,256]{1,0:T(8,128)(2,1)}, u32[]{:S(2)}) copy-start(bf16[768,256]{1,0:T(8,128)(2,1)} %get-tuple-element.69) | copy-start | bytes 1179652
  219.3 18.5 %collective-permute-start.14 = (bf16[768,256]{1,0:T(8,128)(2,1)}, bf16[768,256]{1,0:T(8,128)(2,1)S(1)}, u32[]{:S(2)}, u32[]{:S(2)}) collective-permute-start(bf16[768,256]{1,0:T(8,128)(2,1)} %get-tuple-element.83), channel_id=1, source_target_pairs={{0,64},{64,0},{128,192},{192,128},{1,65},{65,1},{129,193},{193,129... | collective-permute-start | bytes 1179656 | tf_op jit(solution)/shard_map/ppermute | solution.py:49
  219.3 21.3 %collective-permute-start.15 = (bf16[768,256]{1,0:T(8,128)(2,1)}, bf16[768,256]{1,0:T(8,128)(2,1)S(1)}, u32[]{:S(2)}, u32[]{:S(2)}) collective-permute-start(bf16[768,256]{1,0:T(8,128)(2,1)} %get-tuple-element.82), channel_id=1, source_target_pairs={{0,128},{64,192},{128,0},{192,64},{1,129},{65,193},{129,1},{193,65... | collective-permute-start | bytes 1179656 | tf_op jit(solution)/shard_map/ppermute | solution.py:49
  223.3 19.4 %collective-permute-start.16 = (bf16[768,256]{1,0:T(8,128)(2,1)}, bf16[768,256]{1,0:T(8,128)(2,1)S(1)}, u32[]{:S(2)}, u32[]{:S(2)}) collective-permute-start(bf16[768,256]{1,0:T(8,128)(2,1)} %get-tuple-element.81), channel_id=1, source_target_pairs={{0,192},{64,128},{128,64},{192,0},{1,193},{65,129},{129,65},{193,1... | collective-permute-start | bytes 1179656 | tf_op jit(solution)/shard_map/ppermute | solution.py:49
  242.9 7.4 %collective-permute-start.18 = (bf16[8,24,256]{2,1,0:T(8,128)(2,1)S(1)}, bf16[8,24,256]{2,1,0:T(8,128)(2,1)S(1)}, u32[]{:S(2)}, u32[]{:S(2)}) collective-permute-start(bf16[8,24,256]{2,1,0:T(8,128)(2,1)S(1)} %get-tuple-element.93), channel_id=1, source_target_pairs={{0,1},{1,0},{2,3},{3,2},{4,5},{5,4},{6,7},{7,6},{8,9},{9,8},{10,11... | collective-permute-start | bytes 294920 | tf_op jit(solution)/shard_map/ppermute | solution.py:49
  244.2 6.2 %collective-permute-start.19 = (bf16[8,24,256]{2,1,0:T(8,128)(2,1)S(1)}, bf16[8,24,256]{2,1,0:T(8,128)(2,1)S(1)}, u32[]{:S(2)}, u32[]{:S(2)}) collective-permute-start(bf16[8,24,256]{2,1,0:T(8,128)(2,1)S(1)} %get-tuple-element.95), channel_id=1, source_target_pairs={{0,2},{1,3},{2,0},{3,1},{4,6},{5,7},{6,4},{7,5},{8,10},{9,11},{10,... | collective-permute-start | bytes 294920 | tf_op jit(solution)/shard_map/ppermute | solution.py:49
  246.6 30.2 %copy-start.14 = (f32[128,1]{1,0:T(8,128)S(1)}, f32[128,1]{1,0:T(8,128)}, u32[]{:S(2)}) copy-start(f32[128,1]{1,0:T(8,128)} %copy-done.13) | copy-start | bytes 1540
  246.6 4.7 %collective-permute-start.20 = (bf16[8,24,256]{2,1,0:T(8,128)(2,1)S(1)}, bf16[8,24,256]{2,1,0:T(8,128)(2,1)S(1)}, u32[]{:S(2)}, u32[]{:S(2)}) collective-permute-start(bf16[8,24,256]{2,1,0:T(8,128)(2,1)S(1)} %get-tuple-element.94), channel_id=1, source_target_pairs={{0,3},{1,2},{2,1},{3,0},{4,7},{5,6},{6,5},{7,4},{8,11},{9,10},{10,... | collective-permute-start | bytes 294920 | tf_op jit(solution)/shard_map/ppermute | solution.py:49
  246.9 9.7 %all-to-all-start.7 = ((bf16[4,128,384]{2,1,0:T(8,128)(2,1)}), bf16[4,128,384]{2,1,0:T(8,128)(2,1)S(1)}, u32[]{:S(2)}, u32[]{:S(2)}) async-start(bf16[4,128,384]{2,1,0:T(8,128)(2,1)} %fusion.19), calls=%async_computation.7 | async-start | bytes 786432 | tf_op jit(solution)/shard_map/all_to_all | solution.py:41
  268.5 14.2 %all-to-all-start.9 = ((bf16[8,96,128]{2,1,0:T(8,128)(2,1)}), bf16[8,96,128]{2,1,0:T(8,128)(2,1)S(1)}, u32[]{:S(2)}, u32[]{:S(2)}) async-start(bf16[8,96,128]{2,1,0:T(8,128)(2,1)} %broadcast_in_dim.126), calls=%async_computation.9 | async-start | bytes 393216 | tf_op jit(solution)/shard_map/all_to_all | solution.py:41
  282.8 0.9 copy-start.1
  (4 other events, 2.8 us)

commit v5 on v4

--- a/solution.py
+++ b/solution.py
@@ -251,11 +251,11 @@
     rows_0 = exchange(own_0, "z")
     gathered = after(gathered, own_0)
     parts = [gathered] + [swap(gathered, "x", by) for by in range(1, X)]
-    (found_21,) = find([(2, 1)], own_0, parts[1], parts[3])
+    (found_21,) = find([(2, 1)], found_20)
     near_21 = swap(found_21, "y", 2)
     own_1 = found_01 + after(near_11, own_0)
-    rows_1 = exchange(after(own_1, rows_0, near_31), "z")
-    rows_2 = exchange(after(near_20 + near_30, rows_1, parts[2], found_21), "z")
+    rows_1 = exchange(after(own_1, rows_0, near_31, found_21), "z")
+    rows_2 = exchange(after(near_20 + near_30, rows_1, found_21), "z")
     other_1 = near_21 + near_31
     rows_3 = exchange(after(other_1, rows_2), "z")
     chunks = [rows_0, rows_1, rows_2, rows_3]

time: 285 us -> 282 us (0.989)
  starting transfers between devices: 112 us -> 93.1 us
  waiting for transfers between devices: 53.5 us -> 66.6 us
    ppermute x21, starting transfers between devices: 54.1 us -> 38 us  [swap(): lax.ppermute(value, axis, [(i, i ^ by) for i in range(lax.axis_size(axis))])]
    all_to_all x9, waiting for transfers between devices: 35.3 us -> 46.6 us  [exchange(): return lax.all_to_all(value, axes, split_axis=0, concat_axis=0, tiled=True)]
    all_to_all x9, starting transfers between devices: 58.1 us -> 55.1 us  [exchange(): return lax.all_to_all(value, axes, split_axis=0, concat_axis=0, tiled=True)]
    unnamed x52 -> x54, local copies, waits for them, and re-layouts: 8.29 us -> 8.28 us
  transfers between devices with their start and end apart: 30 -> 30, of which waited for: 11 -> 13; matrix products, arithmetic and copies ran while one was open for 21% -> 23% of each run, Pallas kernels for 5% -> 5%
where the time goes in v5:
time: 282 us; the launch traced here: 280 us
  starting transfers between devices  93.1 us (33%)
  waiting for transfers between devices  66.6 us (24%)
  local copies, waits for them, and re-layouts  53.6 us (19%)
  Pallas kernels  23.4 us (8%)
  other arithmetic  23.2 us (8%)
  blocking collectives  11.1 us (4%)
  matrix products  7.98 us (3%)
    all_to_all x9, starting transfers between devices, exchange(): return lax.all_to_all(value, axes, split_axis=0, concat_axis=0, tiled=True)  55.1 us
    all_to_all x9, waiting for transfers between devices, exchange(): return lax.all_to_all(value, axes, split_axis=0, concat_axis=0, tiled=True)  46.6 us
    ppermute x21, starting transfers between devices, swap(): lax.ppermute(value, axis, [(i, i ^ by) for i in range(lax.axis_size(axis))])  38 us
    gather x4, local copies, waits for them, and re-layouts, find(): passage_table.at[ids].get(mode='promise_in_bounds')  33.5 us
    ppermute x21, waiting for transfers between devices, swap(): lax.ppermute(value, axis, [(i, i ^ by) for i in range(lax.axis_size(axis))])  20.1 us
    all_to_all x1, blocking collectives, exchange(): return lax.all_to_all(value, axes, split_axis=0, concat_axis=0, tiled=True)  11.1 us
    unnamed x54, local copies, waits for them, and re-layouts  8.28 us
    dot_general x8, matrix products, shards(): jnp.dot(queries, part, preferred_element_type=jnp.float32)  7.37 us
  transfers between devices with their start and end apart: 30, of which 13 were waited for; matrix products, arithmetic and copies ran while one was open for 23% of the time, Pallas kernels for 5%

profile of v5, /device:TPU:1, one launch (start us, length us, event | category | flops | bytes accessed | tf_op | source)
XLA Modules:
  0.0 280.3 jit_solution(15991346784167419828)
XLA Ops:
  1.5 5.8 %shard_map.85 = (s32[16,128]{1,0:T(8,128)S(1)}, s32[16,128]{1,0:T(8,128)S(1)}) custom-call(s32[128,16]{1,0:T(8,128)S(1)} %copy.33.ids_ref), custom_call_target="tpu_custom_call" | custom-call | tf_op jit(solution)/shard_map/pallas_call | solution.py:216
  7.9 12.0 %all-to-all-start = ((s32[32,1,128]{2,1,0:T(1,128)}), s32[32,1,128]{2,1,0:T(1,128)S(1)}, u32[]{:S(2)}, u32[]{:S(2)}) async-start(s32[32,1,128]{2,1,0:T(1,128)} %bitcast.2), calls=%async_computation | async-start | bytes 32768 | tf_op jit(solution)/shard_map/all_to_all | solution.py:41
  20.8 7.7 %all-to-all-done = s32[32,1,128]{2,1,0:T(1,128)S(1)} async-done(((s32[32,1,128]{2,1,0:T(1,128)}), s32[32,1,128]{2,1,0:T(1,128)S(1)}, u32[]{:S(2)}, u32[]{:S(2)}) %all-to-all-start) | async-done | bytes 16416 | tf_op jit(solution)/shard_map/all_to_all | solution.py:41
  29.0 8.1 %gather_fusion = bf16[1024,768]{1,0:T(8,128)(2,1)S(1)} fusion(bf16[4096,768]{1,0:T(8,128)(2,1)} %param.9, s32[1024]{0:T(1024)S(1)} %fusion.40), kind=kCustom, calls=%fused_computation | custom fusion | bytes 3149824 | tf_op jit(solution)/shard_map/gather | solution.py:232
  39.1 3.9 %all-to-all-start.1 = ((bf16[32,16,768]{2,1,0:T(8,128)(2,1)}), bf16[32,16,768]{2,1,0:T(8,128)(2,1)S(1)}, u32[]{:S(2)}, u32[]{:S(2)}) async-start(bf16[32,16,768]{2,1,0:T(8,128)(2,1)} %broadcast_in_dim.107), calls=%async_computation.1 | async-start | bytes 1572864 | tf_op jit(solution)/shard_map/all_to_all | solution.py:41
  44.3 1.8 collective-permute-start.1
  46.1 10.3 %gather_fusion.1 = bf16[1536,768]{1,0:T(8,128)(2,1)} fusion(bf16[4096,768]{1,0:T(8,128)(2,1)} %param.9, s32[2048]{0:T(1024)S(1)} %pad_clamp_fusion), kind=kCustom, calls=%fused_computation.1 | custom fusion | bytes 4724736 | tf_op jit(solution)/shard_map/gather | solution.py:232
  56.6 2.7 slice_select_fusion.3
  59.7 8.7 %collective-permute-done = bf16[512,768]{1,0:T(8,128)(2,1)S(1)} collective-permute-done((bf16[512,768]{1,0:T(8,128)(2,1)}, bf16[512,768]{1,0:T(8,128)(2,1)S(1)}, u32[]{:S(2)}, u32[]{:S(2)}) %collective-permute-start) | collective-permute-done | bytes 786464 | tf_op jit(solution)/shard_map/ppermute | solution.py:49
  68.4 2.2 fusion.14
  71.3 6.8 %all-to-all-start.2 = ((bf16[8,64,768]{2,1,0:T(8,128)(2,1)}), bf16[8,64,768]{2,1,0:T(8,128)(2,1)S(1)}, u32[]{:S(2)}, u32[]{:S(2)}) async-start(bf16[8,64,768]{2,1,0:T(8,128)(2,1)} %bitcast.8), calls=%async_computation.2 | async-start | bytes 1572864 | tf_op jit(solution)/shard_map/all_to_all | solution.py:41
  78.1 2.0 collective-permute-start.10
  80.5 9.2 %gather_fusion.2 = bf16[1024,768]{1,0:T(8,128)(2,1)} fusion(bf16[4096,768]{1,0:T(8,128)(2,1)} %param.9, s32[1024]{0:T(1024)S(1)} %fusion.41), kind=kCustom, calls=%fused_computation.2 | custom fusion | bytes 3149824 | tf_op jit(solution)/shard_map/gather | solution.py:232
  90.9 2.5 collective-permute-start.3
  93.5 3.0 %slice_select_fusion = (bf16[512,768]{1,0:T(8,128)(2,1)}, bf16[512,768]{1,0:T(8,128)(2,1)}) fusion(bf16[1024,768]{1,0:T(8,128)(2,1)} %gather_fusion.2, pred[512]{0:T(512)(128)(4,1)S(1)} %broadcast_in_dim.122, bf16[512,768]{1,0:T(8,128)(2,1)} %collective-permute-done.9, pred[512]{0:T(512)(128)(4,1)S(1)} %broadcast_in_dim.117), kind=kLoop, calls=%fused_computation.31 | loop fusion | flops 1179648 | bytes 3933184 | tf_op jit(solution)/shard_map/jit(_where)/select_n | solution.py:234
  97.1 6.0 %gather_fusion.3 = bf16[512,768]{1,0:T(8,128)(2,1)S(1)} fusion(bf16[4096,768]{1,0:T(8,128)(2,1)} %param.9, s32[1024]{0:T(1024)S(1)} %pad_clamp_fusion.1), kind=kCustom, calls=%fused_computation.3 | custom fusion | bytes 1574912 | tf_op jit(solution)/shard_map/gather | solution.py:232
  103.3 6.6 %all-to-all-start.3 = ((bf16[8,64,768]{2,1,0:T(8,128)(2,1)}), bf16[8,64,768]{2,1,0:T(8,128)(2,1)S(1)}, u32[]{:S(2)}, u32[]{:S(2)}) async-start(bf16[8,64,768]{2,1,0:T(8,128)(2,1)} %bitcast.10), calls=%async_computation.3 | async-start | bytes 1572864 | tf_op jit(solution)/shard_map/all_to_all | solution.py:41
  109.9 2.5 collective-permute-start.12
  113.3 8.5 %collective-permute-start.5 = (bf16[32,16,768]{2,1,0:T(8,128)(2,1)S(1)}, bf16[32,16,768]{2,1,0:T(8,128)(2,1)}, u32[]{:S(2)}, u32[]{:S(2)}) collective-permute-start(bf16[32,16,768]{2,1,0:T(8,128)(2,1)S(1)} %all-to-all-done.1.refs_0_), channel_id=1, source_target_pairs={{0,32},{32,0},{1,33},{33,1},{2,34},{34,2},{3,35},{35,3},{4,36},{36... | collective-permute-start | bytes 2359304 | tf_op jit(solution)/shard_map/ppermute | solution.py:49
  121.8 2.8 %collective-permute-done.3.refs_2_ = bf16[32,16,768]{2,1,0:T(8,128)(2,1)} collective-permute-done((bf16[32,16,768]{2,1,0:T(8,128)(2,1)S(1)}, bf16[32,16,768]{2,1,0:T(8,128)(2,1)}, u32[]{:S(2)}, u32[]{:S(2)}) %collective-permute-start.3) | collective-permute-done | bytes 786464 | tf_op jit(solution)/shard_map/ppermute | solution.py:49
  124.6 4.2 %collective-permute-start.7 = (bf16[32,16,768]{2,1,0:T(8,128)(2,1)}, bf16[32,16,768]{2,1,0:T(8,128)(2,1)}, u32[]{:S(2)}, u32[]{:S(2)}) collective-permute-start(bf16[32,16,768]{2,1,0:T(8,128)(2,1)} %collective-permute-done.3.refs_2_), channel_id=1, source_target_pairs={{0,32},{32,0},{1,33},{33,1},{2,34},{34,2},{3,35},{35,3},{4,36},{36... | collective-permute-start | bytes 2359304 | tf_op jit(solution)/shard_map/ppermute | solution.py:49
  128.9 2.6 collective-permute-start.8
  131.9 2.4 add.186
  134.4 2.4 add.187
  136.8 6.6 %all-to-all-start.4 = ((bf16[8,64,768]{2,1,0:T(8,128)(2,1)}), bf16[8,64,768]{2,1,0:T(8,128)(2,1)S(1)}, u32[]{:S(2)}, u32[]{:S(2)}) async-start(bf16[8,64,768]{2,1,0:T(8,128)(2,1)} %bitcast.182), calls=%async_computation.4 | async-start | bytes 1572864 | tf_op jit(solution)/shard_map/all_to_all | solution.py:41
  143.5 5.6 %shard_map.86 = bf16[4,2,32,16,768]{4,3,2,1,0:T(8,128)(2,1)} custom-call(s32[2]{0:T(128)S(1)} %pad_add_fusion.4.place_ref, bf16[32,16,768]{2,1,0:T(8,128)(2,1)S(1)} %all-to-all-done.1.refs_0_, bf16[32,16,768]{2,1,0:T(8,128)(2,1)} %collective-permute-done.2.refs_1_, bf16[32,16,768]{2,1,0:T(8,128)(2,1)} %collective-permute-done.3.refs_2_, ...), custom_call_target="tpu_custom_call" | custom-call | tf_op jit(solution)/shard_map/pallas_call | solution.py:263
  149.2 2.2 slice_bitcast_fusion.1
  158.6 1.9 slice_bitcast_fusion
  160.5 6.6 %all-to-all-done.4 = bf16[8,64,768]{2,1,0:T(8,128)(2,1)S(1)} async-done(((bf16[8,64,768]{2,1,0:T(8,128)(2,1)}), bf16[8,64,768]{2,1,0:T(8,128)(2,1)S(1)}, u32[]{:S(2)}, u32[]{:S(2)}) %all-to-all-start.4) | async-done | bytes 786464 | tf_op jit(solution)/shard_map/all_to_all | solution.py:41
  168.0 3.8 %all-to-all-start.5 = ((bf16[8,64,768]{2,1,0:T(8,128)(2,1)}), bf16[8,64,768]{2,1,0:T(8,128)(2,1)S(1)}, u32[]{:S(2)}, u32[]{:S(2)}) async-start(bf16[8,64,768]{2,1,0:T(8,128)(2,1)} %bitcast.41), calls=%async_computation.5 | async-start | bytes 1572864 | tf_op jit(solution)/shard_map/all_to_all | solution.py:41
  171.8 2.3 copy.42
  176.1 1.7 fusion.12
  179.2 2.3 shard_map.87
  183.0 10.2 %all-to-all-done.5 = bf16[8,64,768]{2,1,0:T(8,128)(2,1)S(1)} async-done(((bf16[8,64,768]{2,1,0:T(8,128)(2,1)}), bf16[8,64,768]{2,1,0:T(8,128)(2,1)S(1)}, u32[]{:S(2)}, u32[]{:S(2)}) %all-to-all-start.5) | async-done | bytes 786464 | tf_op jit(solution)/shard_map/all_to_all | solution.py:41
  196.1 4.3 %shard_map.88 = (f32[128,1]{1,0:T(8,128)S(1)}, bf16[128,768]{1,0:T(8,128)(2,1)S(1)}, bf16[4,4,128,384]{3,2,1,0:T(8,128)(2,1)}, bf16[4,4,128,384]{3,2,1,0:T(8,128)(2,1)}) custom-call(s32[2]{0:T(128)S(1)} %pad_add_fusion.4.place_ref, bf16[128,768]{1,0:T(8,128)(2,1)S(1)} %fusion.embedded_ref, bf16[128,768]{1,0:T(8,128)(2,1)S(1)} %copy-done.8, ...), custom_call_target="tpu_custom_call" | custom-call | tf_op jit(solution)/shard_map/pallas_call | solution.py:299
  201.5 5.3 %shard_map.89 = (bf16[4,768,256]{2,1,0:T(8,128)(2,1)S(1)}, bf16[4,768,256]{2,1,0:T(8,128)(2,1)}) custom-call(s32[2]{0:T(128)S(1)} %pad_add_fusion.4.place_ref, bf16[128,768]{1,0:T(8,128)(2,1)S(1)} %copy-done.2, bf16[128,768]{1,0:T(8,128)(2,1)S(1)} %get-tuple-element.64.grad_ref, f32[128,2048]{1,0:T(8,128)S(1)} %get-tuple-element.91.slope_ref, ...), custom_call_target="tpu_custom_call" | custom-call | tf_op jit(solution)/shard_map/pallas_call | solution.py:311
  208.5 3.6 %all-to-all-start.6 = ((bf16[4,4,128,384]{3,2,1,0:T(8,128)(2,1)}), bf16[4,4,128,384]{3,2,1,0:T(8,128)(2,1)S(1)}, u32[]{:S(2)}, u32[]{:S(2)}) async-start(bf16[4,4,128,384]{3,2,1,0:T(8,128)(2,1)} %add_convert_fusion), calls=%async_computation.6 | async-start | bytes 3145728 | tf_op jit(solution)/shard_map/all_to_all | solution.py:41
  212.0 2.7 fusion.18
  214.8 3.5 %collective-permute-start.14 = (bf16[768,256]{1,0:T(8,128)(2,1)}, bf16[768,256]{1,0:T(8,128)(2,1)S(1)}, u32[]{:S(2)}, u32[]{:S(2)}) collective-permute-start(bf16[768,256]{1,0:T(8,128)(2,1)} %get-tuple-element.83), channel_id=1, source_target_pairs={{0,64},{64,0},{128,192},{192,128},{1,65},{65,1},{129,193},{193,129... | collective-permute-start | bytes 1179656 | tf_op jit(solution)/shard_map/ppermute | solution.py:49
  220.7 11.6 %all-to-all-done.6 = bf16[4,4,128,384]{3,2,1,0:T(8,128)(2,1)S(1)} async-done(((bf16[4,4,128,384]{3,2,1,0:T(8,128)(2,1)}), bf16[4,4,128,384]{3,2,1,0:T(8,128)(2,1)S(1)}, u32[]{:S(2)}, u32[]{:S(2)}) %all-to-all-start.6) | async-done | bytes 1572896 | tf_op jit(solution)/shard_map/all_to_all | solution.py:41
  233.3 3.9 %collective-permute-done.15 = bf16[768,256]{1,0:T(8,128)(2,1)S(1)} collective-permute-done((bf16[768,256]{1,0:T(8,128)(2,1)}, bf16[768,256]{1,0:T(8,128)(2,1)S(1)}, u32[]{:S(2)}, u32[]{:S(2)}) %collective-permute-start.15) | collective-permute-done | bytes 393248 | tf_op jit(solution)/shard_map/ppermute | solution.py:49
  237.2 2.1 collective-permute-done.16
  240.8 2.4 collective-permute-start.19
  243.4 3.5 %all-to-all-start.7 = ((bf16[4,128,384]{2,1,0:T(8,128)(2,1)}), bf16[4,128,384]{2,1,0:T(8,128)(2,1)S(1)}, u32[]{:S(2)}, u32[]{:S(2)}) async-start(bf16[4,128,384]{2,1,0:T(8,128)(2,1)} %fusion.19), calls=%async_computation.7 | async-start | bytes 786432 | tf_op jit(solution)/shard_map/all_to_all | solution.py:41
  247.9 5.2 %all-to-all-done.7 = bf16[4,128,384]{2,1,0:T(8,128)(2,1)S(1)} async-done(((bf16[4,128,384]{2,1,0:T(8,128)(2,1)}), bf16[4,128,384]{2,1,0:T(8,128)(2,1)S(1)}, u32[]{:S(2)}, u32[]{:S(2)}) %all-to-all-start.7) | async-done | bytes 393248 | tf_op jit(solution)/shard_map/all_to_all | solution.py:41
  253.2 11.1 %all_to_all.78 = bf16[8,96,128]{2,1,0:T(8,128)(2,1)S(1)} all-to-all(bf16[8,96,128]{2,1,0:T(8,128)(2,1)S(1)} %constant_dynamic-update-slice_fusion.4), channel_id=1, replica_groups=mesh['x'=4,'core'=2,'z'=8,'y'=4] {'z'}, dimensions={0} | all-to-all | bytes 393216 | tf_op jit(solution)/shard_map/all_to_all | solution.py:41
  265.1 8.3 %all-to-all-start.9 = ((bf16[8,96,128]{2,1,0:T(8,128)(2,1)}), bf16[8,96,128]{2,1,0:T(8,128)(2,1)S(1)}, u32[]{:S(2)}, u32[]{:S(2)}) async-start(bf16[8,96,128]{2,1,0:T(8,128)(2,1)} %broadcast_in_dim.126), calls=%async_computation.9 | async-start | bytes 393216 | tf_op jit(solution)/shard_map/all_to_all | solution.py:41
  274.0 5.3 %all-to-all-done.9 = bf16[8,96,128]{2,1,0:T(8,128)(2,1)S(1)} async-done(((bf16[8,96,128]{2,1,0:T(8,128)(2,1)}), bf16[8,96,128]{2,1,0:T(8,128)(2,1)S(1)}, u32[]{:S(2)}, u32[]{:S(2)}) %all-to-all-start.9) | async-done | bytes 196640 | tf_op jit(solution)/shard_map/all_to_all | solution.py:41
  (178 shorter events, 38.3 us)
Async XLA Ops:
  0.6 19.4 %copy-start = (bf16[64,768]{1,0:T(8,128)(2,1)S(1)}, bf16[64,768]{1,0:T(8,128)(2,1)}, u32[]{:S(2)}) copy-start(bf16[64,768]{1,0:T(8,128)(2,1)} %param.11) | copy-start | bytes 294916
  7.9 20.6 %all-to-all-start = ((s32[32,1,128]{2,1,0:T(1,128)}), s32[32,1,128]{2,1,0:T(1,128)S(1)}, u32[]{:S(2)}, u32[]{:S(2)}) async-start(s32[32,1,128]{2,1,0:T(1,128)} %bitcast.2), calls=%async_computation | async-start | bytes 32768 | tf_op jit(solution)/shard_map/all_to_all | solution.py:41
  39.1 32.2 %all-to-all-start.1 = ((bf16[32,16,768]{2,1,0:T(8,128)(2,1)}), bf16[32,16,768]{2,1,0:T(8,128)(2,1)S(1)}, u32[]{:S(2)}, u32[]{:S(2)}) async-start(bf16[32,16,768]{2,1,0:T(8,128)(2,1)} %broadcast_in_dim.107), calls=%async_computation.1 | async-start | bytes 1572864 | tf_op jit(solution)/shard_map/all_to_all | solution.py:41
  43.0 25.4 %collective-permute-start = (bf16[512,768]{1,0:T(8,128)(2,1)}, bf16[512,768]{1,0:T(8,128)(2,1)S(1)}, u32[]{:S(2)}, u32[]{:S(2)}) collective-permute-start(bf16[512,768]{1,0:T(8,128)(2,1)} %get-tuple-element.90), channel_id=1, source_target_pairs={{0,1},{1,0},{2,3},{3,2},{4,5},{5,4},{6,7},{7,6},{8,9},{9,8},{10,11... | collective-permute-start | bytes 2359304 | tf_op jit(solution)/shard_map/ppermute | solution.py:49
  44.3 27.0 %collective-permute-start.1 = (bf16[512,768]{1,0:T(8,128)(2,1)S(1)}, bf16[512,768]{1,0:T(8,128)(2,1)S(1)}, u32[]{:S(2)}, u32[]{:S(2)}) collective-permute-start(bf16[512,768]{1,0:T(8,128)(2,1)S(1)} %get-tuple-element.89), channel_id=1, source_target_pairs={{0,3},{1,2},{2,1},{3,0},{4,7},{5,6},{6,5},{7,4},{8,11},{9,10},{10,... | collective-permute-start | bytes 2359304 | tf_op jit(solution)/shard_map/ppermute | solution.py:49
  59.3 34.2 %collective-permute-start.9 = (bf16[512,768]{1,0:T(8,128)(2,1)}, bf16[512,768]{1,0:T(8,128)(2,1)}, u32[]{:S(2)}, u32[]{:S(2)}) collective-permute-start(bf16[512,768]{1,0:T(8,128)(2,1)} %get-tuple-element.86), channel_id=1, source_target_pairs={{0,1},{1,0},{2,3},{3,2},{4,5},{5,4},{6,7},{7,6},{8,9},{9,8},{10,11... | collective-permute-start | bytes 2359304 | tf_op jit(solution)/shard_map/ppermute | solution.py:49
  71.3 18.4 %copy-start.18 = (bf16[512,768]{1,0:T(8,128)(2,1)}, bf16[512,768]{1,0:T(8,128)(2,1)S(1)}, u32[]{:S(2)}) copy-start(bf16[512,768]{1,0:T(8,128)(2,1)S(1)} %collective-permute-done.1) | copy-start | bytes 2359300
  71.3 31.9 %all-to-all-start.2 = ((bf16[8,64,768]{2,1,0:T(8,128)(2,1)}), bf16[8,64,768]{2,1,0:T(8,128)(2,1)S(1)}, u32[]{:S(2)}, u32[]{:S(2)}) async-start(bf16[8,64,768]{2,1,0:T(8,128)(2,1)} %bitcast.8), calls=%async_computation.2 | async-start | bytes 1572864 | tf_op jit(solution)/shard_map/all_to_all | solution.py:41
  78.1 25.2 %collective-permute-start.10 = (bf16[512,768]{1,0:T(8,128)(2,1)}, bf16[512,768]{1,0:T(8,128)(2,1)}, u32[]{:S(2)}, u32[]{:S(2)}) collective-permute-start(bf16[512,768]{1,0:T(8,128)(2,1)} %get-tuple-element.85), channel_id=1, source_target_pairs={{0,3},{1,2},{2,1},{3,0},{4,7},{5,6},{6,5},{7,4},{8,11},{9,10},{10,... | collective-permute-start | bytes 2359304 | tf_op jit(solution)/shard_map/ppermute | solution.py:49
  89.7 32.2 %collective-permute-start.2 = (bf16[32,16,768]{2,1,0:T(8,128)(2,1)S(1)}, bf16[32,16,768]{2,1,0:T(8,128)(2,1)}, u32[]{:S(2)}, u32[]{:S(2)}) collective-permute-start(bf16[32,16,768]{2,1,0:T(8,128)(2,1)S(1)} %all-to-all-done.1.refs_0_), channel_id=1, source_target_pairs={{0,64},{64,0},{128,192},{192,128},{1,65},{65,1},{129,193},{193,129... | collective-permute-start | bytes 2359304 | tf_op jit(solution)/shard_map/ppermute | solution.py:49
  90.9 33.8 %collective-permute-start.3 = (bf16[32,16,768]{2,1,0:T(8,128)(2,1)S(1)}, bf16[32,16,768]{2,1,0:T(8,128)(2,1)}, u32[]{:S(2)}, u32[]{:S(2)}) collective-permute-start(bf16[32,16,768]{2,1,0:T(8,128)(2,1)S(1)} %all-to-all-done.1.refs_0_), channel_id=1, source_target_pairs={{0,128},{64,192},{128,0},{192,64},{1,129},{65,193},{129,1},{193,65... | collective-permute-start | bytes 2359304 | tf_op jit(solution)/shard_map/ppermute | solution.py:49
  93.3 35.6 %collective-permute-start.4 = (bf16[32,16,768]{2,1,0:T(8,128)(2,1)S(1)}, bf16[32,16,768]{2,1,0:T(8,128)(2,1)}, u32[]{:S(2)}, u32[]{:S(2)}) collective-permute-start(bf16[32,16,768]{2,1,0:T(8,128)(2,1)S(1)} %all-to-all-done.1.refs_0_), channel_id=1, source_target_pairs={{0,192},{64,128},{128,64},{192,0},{1,193},{65,129},{129,65},{193,1... | collective-permute-start | bytes 2359304 | tf_op jit(solution)/shard_map/ppermute | solution.py:49
  96.5 16.8 %collective-permute-start.11 = (bf16[512,768]{1,0:T(8,128)(2,1)}, bf16[512,768]{1,0:T(8,128)(2,1)}, u32[]{:S(2)}, u32[]{:S(2)}) collective-permute-start(bf16[512,768]{1,0:T(8,128)(2,1)} %get-tuple-element.87), channel_id=1, source_target_pairs={{0,2},{1,3},{2,0},{3,1},{4,6},{5,7},{6,4},{7,5},{8,10},{9,11},{10,... | collective-permute-start | bytes 2359304 | tf_op jit(solution)/shard_map/ppermute | solution.py:49
  103.3 33.6 %all-to-all-start.3 = ((bf16[8,64,768]{2,1,0:T(8,128)(2,1)}), bf16[8,64,768]{2,1,0:T(8,128)(2,1)S(1)}, u32[]{:S(2)}, u32[]{:S(2)}) async-start(bf16[8,64,768]{2,1,0:T(8,128)(2,1)} %bitcast.10), calls=%async_computation.3 | async-start | bytes 1572864 | tf_op jit(solution)/shard_map/all_to_all | solution.py:41
  109.9 24.5 %collective-permute-start.12 = (bf16[512,768]{1,0:T(8,128)(2,1)S(1)}, bf16[512,768]{1,0:T(8,128)(2,1)}, u32[]{:S(2)}, u32[]{:S(2)}) collective-permute-start(bf16[512,768]{1,0:T(8,128)(2,1)S(1)} %broadcast_select_fusion), channel_id=1, source_target_pairs={{0,2},{1,3},{2,0},{3,1},{4,6},{5,7},{6,4},{7,5},{8,10},{9,11},{10,... | collective-permute-start | bytes 2359304 | tf_op jit(solution)/shard_map/ppermute | solution.py:49
  113.3 30.2 %collective-permute-start.5 = (bf16[32,16,768]{2,1,0:T(8,128)(2,1)S(1)}, bf16[32,16,768]{2,1,0:T(8,128)(2,1)}, u32[]{:S(2)}, u32[]{:S(2)}) collective-permute-start(bf16[32,16,768]{2,1,0:T(8,128)(2,1)S(1)} %all-to-all-done.1.refs_0_), channel_id=1, source_target_pairs={{0,32},{32,0},{1,33},{33,1},{2,34},{34,2},{3,35},{35,3},{4,36},{36... | collective-permute-start | bytes 2359304 | tf_op jit(solution)/shard_map/ppermute | solution.py:49
  121.8 21.7 %collective-permute-start.6 = (bf16[32,16,768]{2,1,0:T(8,128)(2,1)}, bf16[32,16,768]{2,1,0:T(8,128)(2,1)}, u32[]{:S(2)}, u32[]{:S(2)}) collective-permute-start(bf16[32,16,768]{2,1,0:T(8,128)(2,1)} %collective-permute-done.2.refs_1_), channel_id=1, source_target_pairs={{0,32},{32,0},{1,33},{33,1},{2,34},{34,2},{3,35},{35,3},{4,36},{36... | collective-permute-start | bytes 2359304 | tf_op jit(solution)/shard_map/ppermute | solution.py:49
  124.6 18.9 %collective-permute-start.7 = (bf16[32,16,768]{2,1,0:T(8,128)(2,1)}, bf16[32,16,768]{2,1,0:T(8,128)(2,1)}, u32[]{:S(2)}, u32[]{:S(2)}) collective-permute-start(bf16[32,16,768]{2,1,0:T(8,128)(2,1)} %collective-permute-done.3.refs_2_), channel_id=1, source_target_pairs={{0,32},{32,0},{1,33},{33,1},{2,34},{34,2},{3,35},{35,3},{4,36},{36... | collective-permute-start | bytes 2359304 | tf_op jit(solution)/shard_map/ppermute | solution.py:49
  128.9 14.6 %collective-permute-start.8 = (bf16[32,16,768]{2,1,0:T(8,128)(2,1)}, bf16[32,16,768]{2,1,0:T(8,128)(2,1)}, u32[]{:S(2)}, u32[]{:S(2)}) collective-permute-start(bf16[32,16,768]{2,1,0:T(8,128)(2,1)} %collective-permute-done.4.refs_3_), channel_id=1, source_target_pairs={{0,32},{32,0},{1,33},{33,1},{2,34},{34,2},{3,35},{35,3},{4,36},{36... | collective-permute-start | bytes 2359304 | tf_op jit(solution)/shard_map/ppermute | solution.py:49
  136.8 12.3 %copy-start.3 = (bf16[8,64,768]{2,1,0:T(8,128)(2,1)}, bf16[8,64,768]{2,1,0:T(8,128)(2,1)S(1)}, u32[]{:S(2)}) copy-start(bf16[8,64,768]{2,1,0:T(8,128)(2,1)S(1)} %all-to-all-done.3) | copy-start | bytes 2359300
  136.8 30.2 %all-to-all-start.4 = ((bf16[8,64,768]{2,1,0:T(8,128)(2,1)}), bf16[8,64,768]{2,1,0:T(8,128)(2,1)S(1)}, u32[]{:S(2)}, u32[]{:S(2)}) async-start(bf16[8,64,768]{2,1,0:T(8,128)(2,1)} %bitcast.182), calls=%async_computation.4 | async-start | bytes 1572864 | tf_op jit(solution)/shard_map/all_to_all | solution.py:41
  149.2 9.5 %slice-start = ((s8[6291456]{0:T(1024)(128)(4,1)}), s8[4194304]{0:T(1024)(128)(4,1)S(1)}, s32[]{:S(2)}) async-start(s8[6291456]{0:T(1024)(128)(4,1)} %bitcast.180), calls=%async_computation.10 | async-start | bytes 8388608
  152.2 0.9 copy-start.2
  152.2 6.4 %slice-start.1 = ((s8[6291456]{0:T(1024)(128)(4,1)}), s8[2097152]{0:T(1024)(128)(4,1)S(1)}, s32[]{:S(2)}) async-start(s8[6291456]{0:T(1024)(128)(4,1)} %bitcast.180), calls=%async_computation.11 | async-start | bytes 4194304
  160.5 11.2 %copy-start.19 = (bf16[32,8,256]{2,1,0:T(8,128)(2,1)S(1)}, bf16[32,8,256]{2,1,0:T(8,128)(2,1)}, u32[]{:S(2)}) copy-start(bf16[32,8,256]{2,1,0:T(8,128)(2,1)} %get-tuple-element.101) | copy-start | bytes 393220
  168.0 25.2 %all-to-all-start.5 = ((bf16[8,64,768]{2,1,0:T(8,128)(2,1)}), bf16[8,64,768]{2,1,0:T(8,128)(2,1)S(1)}, u32[]{:S(2)}, u32[]{:S(2)}) async-start(bf16[8,64,768]{2,1,0:T(8,128)(2,1)} %bitcast.41), calls=%async_computation.5 | async-start | bytes 1572864 | tf_op jit(solution)/shard_map/all_to_all | solution.py:41
  174.1 3.7 %copy-start.15 = (bf16[32,4,2,8,768]{4,3,2,1,0:T(8,128)(2,1)}, bf16[32,4,2,8,768]{4,3,2,1,0:T(8,128)(2,1)S(1)}, u32[]{:S(2)}) copy-start(bf16[32,4,2,8,768]{4,3,2,1,0:T(8,128)(2,1)S(1)} %copy.42) | copy-start | bytes 9437188
  177.8 1.1 copy-start.4
  177.8 1.4 copy-start.6
  177.8 1.4 copy-start.7
  193.2 0.9 copy-start.8
  194.1 1.0 copy-start.10
  195.1 0.9 copy-start.12
  201.0 5.8 %collective-permute-start.17 = (bf16[4,4,128,384]{3,2,1,0:T(8,128)(2,1)}, bf16[4,4,128,384]{3,2,1,0:T(8,128)(2,1)S(1)}, u32[]{:S(2)}, u32[]{:S(2)}) collective-permute-start(bf16[4,4,128,384]{3,2,1,0:T(8,128)(2,1)} %get-tuple-element.68), channel_id=1, source_target_pairs={{0,32},{32,0},{1,33},{33,1},{2,34},{34,2},{3,35},{35,3},{4,36},{36... | collective-permute-start | bytes 4718600 | tf_op jit(solution)/shard_map/ppermute | solution.py:49
  201.5 5.3 %copy-start.16 = (bf16[4,4,128,384]{3,2,1,0:T(8,128)(2,1)S(1)}, bf16[4,4,128,384]{3,2,1,0:T(8,128)(2,1)}, u32[]{:S(2)}) copy-start(bf16[4,4,128,384]{3,2,1,0:T(8,128)(2,1)} %get-tuple-element.67) | copy-start | bytes 4718596
  206.8 5.2 %collective-permute-start.13 = (bf16[4,768,256]{2,1,0:T(8,128)(2,1)}, bf16[4,768,256]{2,1,0:T(8,128)(2,1)}, u32[]{:S(2)}, u32[]{:S(2)}) collective-permute-start(bf16[4,768,256]{2,1,0:T(8,128)(2,1)} %get-tuple-element.66), channel_id=1, source_target_pairs={{0,32},{32,0},{1,33},{33,1},{2,34},{34,2},{3,35},{35,3},{4,36},{36... | collective-permute-start | bytes 4718600 | tf_op jit(solution)/shard_map/ppermute | solution.py:49
  208.5 23.8 %all-to-all-start.6 = ((bf16[4,4,128,384]{3,2,1,0:T(8,128)(2,1)}), bf16[4,4,128,384]{3,2,1,0:T(8,128)(2,1)S(1)}, u32[]{:S(2)}, u32[]{:S(2)}) async-start(bf16[4,4,128,384]{3,2,1,0:T(8,128)(2,1)} %add_convert_fusion), calls=%async_computation.6 | async-start | bytes 3145728 | tf_op jit(solution)/shard_map/all_to_all | solution.py:41
  214.8 24.5 %copy-start.17 = (bf16[768,256]{1,0:T(8,128)(2,1)S(1)}, bf16[768,256]{1,0:T(8,128)(2,1)}, u32[]{:S(2)}) copy-start(bf16[768,256]{1,0:T(8,128)(2,1)} %get-tuple-element.69) | copy-start | bytes 1179652
  214.8 18.5 %collective-permute-start.14 = (bf16[768,256]{1,0:T(8,128)(2,1)}, bf16[768,256]{1,0:T(8,128)(2,1)S(1)}, u32[]{:S(2)}, u32[]{:S(2)}) collective-permute-start(bf16[768,256]{1,0:T(8,128)(2,1)} %get-tuple-element.83), channel_id=1, source_target_pairs={{0,64},{64,0},{128,192},{192,128},{1,65},{65,1},{129,193},{193,129... | collective-permute-start | bytes 1179656 | tf_op jit(solution)/shard_map/ppermute | solution.py:49
  218.2 18.9 %collective-permute-start.15 = (bf16[768,256]{1,0:T(8,128)(2,1)}, bf16[768,256]{1,0:T(8,128)(2,1)S(1)}, u32[]{:S(2)}, u32[]{:S(2)}) collective-permute-start(bf16[768,256]{1,0:T(8,128)(2,1)} %get-tuple-element.82), channel_id=1, source_target_pairs={{0,128},{64,192},{128,0},{192,64},{1,129},{65,193},{129,1},{193,65... | collective-permute-start | bytes 1179656 | tf_op jit(solution)/shard_map/ppermute | solution.py:49
  219.9 19.4 %collective-permute-start.16 = (bf16[768,256]{1,0:T(8,128)(2,1)}, bf16[768,256]{1,0:T(8,128)(2,1)S(1)}, u32[]{:S(2)}, u32[]{:S(2)}) collective-permute-start(bf16[768,256]{1,0:T(8,128)(2,1)} %get-tuple-element.81), channel_id=1, source_target_pairs={{0,192},{64,128},{128,64},{192,0},{1,193},{65,129},{129,65},{193,1... | collective-permute-start | bytes 1179656 | tf_op jit(solution)/shard_map/ppermute | solution.py:49
  239.5 7.4 %collective-permute-start.18 = (bf16[8,24,256]{2,1,0:T(8,128)(2,1)S(1)}, bf16[8,24,256]{2,1,0:T(8,128)(2,1)S(1)}, u32[]{:S(2)}, u32[]{:S(2)}) collective-permute-start(bf16[8,24,256]{2,1,0:T(8,128)(2,1)S(1)} %get-tuple-element.93), channel_id=1, source_target_pairs={{0,1},{1,0},{2,3},{3,2},{4,5},{5,4},{6,7},{7,6},{8,9},{9,8},{10,11... | collective-permute-start | bytes 294920 | tf_op jit(solution)/shard_map/ppermute | solution.py:49
  240.8 6.2 %collective-permute-start.19 = (bf16[8,24,256]{2,1,0:T(8,128)(2,1)S(1)}, bf16[8,24,256]{2,1,0:T(8,128)(2,1)S(1)}, u32[]{:S(2)}, u32[]{:S(2)}) collective-permute-start(bf16[8,24,256]{2,1,0:T(8,128)(2,1)S(1)} %get-tuple-element.95), channel_id=1, source_target_pairs={{0,2},{1,3},{2,0},{3,1},{4,6},{5,7},{6,4},{7,5},{8,10},{9,11},{10,... | collective-permute-start | bytes 294920 | tf_op jit(solution)/shard_map/ppermute | solution.py:49
  243.2 30.2 %copy-start.14 = (f32[128,1]{1,0:T(8,128)S(1)}, f32[128,1]{1,0:T(8,128)}, u32[]{:S(2)}) copy-start(f32[128,1]{1,0:T(8,128)} %copy-done.13) | copy-start | bytes 1540
  243.2 4.7 %collective-permute-start.20 = (bf16[8,24,256]{2,1,0:T(8,128)(2,1)S(1)}, bf16[8,24,256]{2,1,0:T(8,128)(2,1)S(1)}, u32[]{:S(2)}, u32[]{:S(2)}) collective-permute-start(bf16[8,24,256]{2,1,0:T(8,128)(2,1)S(1)} %get-tuple-element.94), channel_id=1, source_target_pairs={{0,3},{1,2},{2,1},{3,0},{4,7},{5,6},{6,5},{7,4},{8,11},{9,10},{10,... | collective-permute-start | bytes 294920 | tf_op jit(solution)/shard_map/ppermute | solution.py:49
  243.4 9.7 %all-to-all-start.7 = ((bf16[4,128,384]{2,1,0:T(8,128)(2,1)}), bf16[4,128,384]{2,1,0:T(8,128)(2,1)S(1)}, u32[]{:S(2)}, u32[]{:S(2)}) async-start(bf16[4,128,384]{2,1,0:T(8,128)(2,1)} %fusion.19), calls=%async_computation.7 | async-start | bytes 786432 | tf_op jit(solution)/shard_map/all_to_all | solution.py:41
  265.1 14.2 %all-to-all-start.9 = ((bf16[8,96,128]{2,1,0:T(8,128)(2,1)}), bf16[8,96,128]{2,1,0:T(8,128)(2,1)S(1)}, u32[]{:S(2)}, u32[]{:S(2)}) async-start(bf16[8,96,128]{2,1,0:T(8,128)(2,1)} %broadcast_in_dim.126), calls=%async_computation.9 | async-start | bytes 393216 | tf_op jit(solution)/shard_map/all_to_all | solution.py:41
  279.3 0.9 copy-start.1
  (5 other events, 3.7 us)

commit v6 on v5

--- a/solution.py
+++ b/solution.py
@@ -251,7 +251,7 @@
     rows_0 = exchange(own_0, "z")
     gathered = after(gathered, own_0)
     parts = [gathered] + [swap(gathered, "x", by) for by in range(1, X)]
-    (found_21,) = find([(2, 1)], found_20)
+    (found_21,) = find([(2, 1)], found_20, near_31)
     near_21 = swap(found_21, "y", 2)
     own_1 = found_01 + after(near_11, own_0)
     rows_1 = exchange(after(own_1, rows_0, near_31, found_21), "z")

time: 282 us -> 278 us (0.986)
  starting transfers between devices: 93.1 us -> 89.6 us
    ppermute x21, starting transfers between devices: 38 us -> 33.5 us  [swap(): lax.ppermute(value, axis, [(i, i ^ by) for i in range(lax.axis_size(axis))])]
    ppermute x21, waiting for transfers between devices: 20.1 us -> 16.6 us  [swap(): lax.ppermute(value, axis, [(i, i ^ by) for i in range(lax.axis_size(axis))])]
  transfers between devices with their start and end apart: 30 -> 30, of which waited for: 13 -> 12; matrix products, arithmetic and copies ran while one was open for 23% -> 23% of each run, Pallas kernels for 5% -> 5%
where the time goes in v6:
time: 278 us; the launch traced here: 276 us
  starting transfers between devices  89.6 us (32%)
  waiting for transfers between devices  65.2 us (23%)
  local copies, waits for them, and re-layouts  53.6 us (19%)
  Pallas kernels  23.4 us (8%)
  other arithmetic  23.2 us (8%)
  blocking collectives  12.2 us (4%)
  matrix products  7.98 us (3%)
    all_to_all x9, starting transfers between devices, exchange(): return lax.all_to_all(value, axes, split_axis=0, concat_axis=0, tiled=True)  56.1 us
    all_to_all x9, waiting for transfers between devices, exchange(): return lax.all_to_all(value, axes, split_axis=0, concat_axis=0, tiled=True)  48.6 us
    ppermute x21, starting transfers between devices, swap(): lax.ppermute(value, axis, [(i, i ^ by) for i in range(lax.axis_size(axis))])  33.5 us
    gather x4, local copies, waits for them, and re-layouts, find(): passage_table.at[ids].get(mode='promise_in_bounds')  33.5 us
    ppermute x21, waiting for transfers between devices, swap(): lax.ppermute(value, axis, [(i, i ^ by) for i in range(lax.axis_size(axis))])  16.6 us
    all_to_all x1, blocking collectives, exchange(): return lax.all_to_all(value, axes, split_axis=0, concat_axis=0, tiled=True)  12.2 us
    unnamed x54, local copies, waits for them, and re-layouts  8.28 us
    dot_general x8, matrix products, shards(): jnp.dot(queries, part, preferred_element_type=jnp.float32)  7.37 us
  transfers between devices with their start and end apart: 30, of which 12 were waited for; matrix products, arithmetic and copies ran while one was open for 23% of the time, Pallas kernels for 5%

profile of v6, /device:TPU:1, one launch (start us, length us, event | category | flops | bytes accessed | tf_op | source)
XLA Modules:
  0.0 276.5 jit_solution(8720318070404713017)
XLA Ops:
  1.5 5.8 %shard_map.85 = (s32[16,128]{1,0:T(8,128)S(1)}, s32[16,128]{1,0:T(8,128)S(1)}) custom-call(s32[128,16]{1,0:T(8,128)S(1)} %copy.33.ids_ref), custom_call_target="tpu_custom_call" | custom-call | tf_op jit(solution)/shard_map/pallas_call | solution.py:216
  7.9 12.0 %all-to-all-start = ((s32[32,1,128]{2,1,0:T(1,128)}), s32[32,1,128]{2,1,0:T(1,128)S(1)}, u32[]{:S(2)}, u32[]{:S(2)}) async-start(s32[32,1,128]{2,1,0:T(1,128)} %bitcast.2), calls=%async_computation | async-start | bytes 32768 | tf_op jit(solution)/shard_map/all_to_all | solution.py:41
  20.8 7.7 %all-to-all-done = s32[32,1,128]{2,1,0:T(1,128)S(1)} async-done(((s32[32,1,128]{2,1,0:T(1,128)}), s32[32,1,128]{2,1,0:T(1,128)S(1)}, u32[]{:S(2)}, u32[]{:S(2)}) %all-to-all-start) | async-done | bytes 16416 | tf_op jit(solution)/shard_map/all_to_all | solution.py:41
  29.0 8.1 %gather_fusion = bf16[1024,768]{1,0:T(8,128)(2,1)S(1)} fusion(bf16[4096,768]{1,0:T(8,128)(2,1)} %param.9, s32[1024]{0:T(1024)S(1)} %fusion.40), kind=kCustom, calls=%fused_computation | custom fusion | bytes 3149824 | tf_op jit(solution)/shard_map/gather | solution.py:232
  39.1 3.9 %all-to-all-start.1 = ((bf16[32,16,768]{2,1,0:T(8,128)(2,1)}), bf16[32,16,768]{2,1,0:T(8,128)(2,1)S(1)}, u32[]{:S(2)}, u32[]{:S(2)}) async-start(bf16[32,16,768]{2,1,0:T(8,128)(2,1)} %broadcast_in_dim.107), calls=%async_computation.1 | async-start | bytes 1572864 | tf_op jit(solution)/shard_map/all_to_all | solution.py:41
  44.3 1.8 collective-permute-start.1
  46.1 10.3 %gather_fusion.1 = bf16[1536,768]{1,0:T(8,128)(2,1)} fusion(bf16[4096,768]{1,0:T(8,128)(2,1)} %param.9, s32[2048]{0:T(1024)S(1)} %pad_clamp_fusion), kind=kCustom, calls=%fused_computation.1 | custom fusion | bytes 4724736 | tf_op jit(solution)/shard_map/gather | solution.py:232
  56.6 2.7 slice_select_fusion.3
  60.3 8.1 %collective-permute-done = bf16[512,768]{1,0:T(8,128)(2,1)S(1)} collective-permute-done((bf16[512,768]{1,0:T(8,128)(2,1)}, bf16[512,768]{1,0:T(8,128)(2,1)S(1)}, u32[]{:S(2)}, u32[]{:S(2)}) %collective-permute-start) | collective-permute-done | bytes 786464 | tf_op jit(solution)/shard_map/ppermute | solution.py:49
  68.4 2.2 fusion.14
  71.3 6.8 %all-to-all-start.2 = ((bf16[8,64,768]{2,1,0:T(8,128)(2,1)}), bf16[8,64,768]{2,1,0:T(8,128)(2,1)S(1)}, u32[]{:S(2)}, u32[]{:S(2)}) async-start(bf16[8,64,768]{2,1,0:T(8,128)(2,1)} %bitcast.8), calls=%async_computation.2 | async-start | bytes 1572864 | tf_op jit(solution)/shard_map/all_to_all | solution.py:41
  78.5 9.2 %gather_fusion.2 = bf16[1024,768]{1,0:T(8,128)(2,1)} fusion(bf16[4096,768]{1,0:T(8,128)(2,1)} %param.9, s32[1024]{0:T(1024)S(1)} %fusion.41), kind=kCustom, calls=%fused_computation.2 | custom fusion | bytes 3149824 | tf_op jit(solution)/shard_map/gather | solution.py:232
  88.9 2.5 collective-permute-start.3
  91.5 3.0 %slice_select_fusion = (bf16[512,768]{1,0:T(8,128)(2,1)}, bf16[512,768]{1,0:T(8,128)(2,1)}) fusion(bf16[1024,768]{1,0:T(8,128)(2,1)} %gather_fusion.2, pred[512]{0:T(512)(128)(4,1)S(1)} %broadcast_in_dim.122, bf16[512,768]{1,0:T(8,128)(2,1)} %collective-permute-done.9, pred[512]{0:T(512)(128)(4,1)S(1)} %broadcast_in_dim.117), kind=kLoop, calls=%fused_computation.31 | loop fusion | flops 1179648 | bytes 3933184 | tf_op jit(solution)/shard_map/jit(_where)/select_n | solution.py:234
  94.5 2.5 collective-permute-start.11
  97.1 6.0 %gather_fusion.3 = bf16[512,768]{1,0:T(8,128)(2,1)S(1)} fusion(bf16[4096,768]{1,0:T(8,128)(2,1)} %param.9, s32[1024]{0:T(1024)S(1)} %pad_clamp_fusion.1), kind=kCustom, calls=%fused_computation.3 | custom fusion | bytes 1574912 | tf_op jit(solution)/shard_map/gather | solution.py:232
  103.2 6.7 %all-to-all-start.3 = ((bf16[8,64,768]{2,1,0:T(8,128)(2,1)}), bf16[8,64,768]{2,1,0:T(8,128)(2,1)S(1)}, u32[]{:S(2)}, u32[]{:S(2)}) async-start(bf16[8,64,768]{2,1,0:T(8,128)(2,1)} %bitcast.10), calls=%async_computation.3 | async-start | bytes 1572864 | tf_op jit(solution)/shard_map/all_to_all | solution.py:41
  111.3 7.5 %collective-permute-start.5 = (bf16[32,16,768]{2,1,0:T(8,128)(2,1)S(1)}, bf16[32,16,768]{2,1,0:T(8,128)(2,1)}, u32[]{:S(2)}, u32[]{:S(2)}) collective-permute-start(bf16[32,16,768]{2,1,0:T(8,128)(2,1)S(1)} %all-to-all-done.1.refs_0_), channel_id=1, source_target_pairs={{0,32},{32,0},{1,33},{33,1},{2,34},{34,2},{3,35},{35,3},{4,36},{36... | collective-permute-start | bytes 2359304 | tf_op jit(solution)/shard_map/ppermute | solution.py:49
  118.8 3.8 %collective-permute-done.3.refs_2_ = bf16[32,16,768]{2,1,0:T(8,128)(2,1)} collective-permute-done((bf16[32,16,768]{2,1,0:T(8,128)(2,1)S(1)}, bf16[32,16,768]{2,1,0:T(8,128)(2,1)}, u32[]{:S(2)}, u32[]{:S(2)}) %collective-permute-start.3) | collective-permute-done | bytes 786464 | tf_op jit(solution)/shard_map/ppermute | solution.py:49
  122.6 4.3 %collective-permute-start.7 = (bf16[32,16,768]{2,1,0:T(8,128)(2,1)}, bf16[32,16,768]{2,1,0:T(8,128)(2,1)}, u32[]{:S(2)}, u32[]{:S(2)}) collective-permute-start(bf16[32,16,768]{2,1,0:T(8,128)(2,1)} %collective-permute-done.3.refs_2_), channel_id=1, source_target_pairs={{0,32},{32,0},{1,33},{33,1},{2,34},{34,2},{3,35},{35,3},{4,36},{36... | collective-permute-start | bytes 2359304 | tf_op jit(solution)/shard_map/ppermute | solution.py:49
  126.9 2.6 collective-permute-start.8
  129.9 2.4 add.186
  132.4 2.4 add.187
  134.8 6.6 %all-to-all-start.4 = ((bf16[8,64,768]{2,1,0:T(8,128)(2,1)}), bf16[8,64,768]{2,1,0:T(8,128)(2,1)S(1)}, u32[]{:S(2)}, u32[]{:S(2)}) async-start(bf16[8,64,768]{2,1,0:T(8,128)(2,1)} %bitcast.182), calls=%async_computation.4 | async-start | bytes 1572864 | tf_op jit(solution)/shard_map/all_to_all | solution.py:41
  141.5 5.6 %shard_map.86 = bf16[4,2,32,16,768]{4,3,2,1,0:T(8,128)(2,1)} custom-call(s32[2]{0:T(128)S(1)} %pad_add_fusion.4.place_ref, bf16[32,16,768]{2,1,0:T(8,128)(2,1)S(1)} %all-to-all-done.1.refs_0_, bf16[32,16,768]{2,1,0:T(8,128)(2,1)} %collective-permute-done.2.refs_1_, bf16[32,16,768]{2,1,0:T(8,128)(2,1)} %collective-permute-done.3.refs_2_, ...), custom_call_target="tpu_custom_call" | custom-call | tf_op jit(solution)/shard_map/pallas_call | solution.py:263
  147.2 2.2 slice_bitcast_fusion.1
  156.6 1.9 slice_bitcast_fusion
  158.5 6.6 %all-to-all-done.4 = bf16[8,64,768]{2,1,0:T(8,128)(2,1)S(1)} async-done(((bf16[8,64,768]{2,1,0:T(8,128)(2,1)}), bf16[8,64,768]{2,1,0:T(8,128)(2,1)S(1)}, u32[]{:S(2)}, u32[]{:S(2)}) %all-to-all-start.4) | async-done | bytes 786464 | tf_op jit(solution)/shard_map/all_to_all | solution.py:41
  166.0 3.8 %all-to-all-start.5 = ((bf16[8,64,768]{2,1,0:T(8,128)(2,1)}), bf16[8,64,768]{2,1,0:T(8,128)(2,1)S(1)}, u32[]{:S(2)}, u32[]{:S(2)}) async-start(bf16[8,64,768]{2,1,0:T(8,128)(2,1)} %bitcast.41), calls=%async_computation.5 | async-start | bytes 1572864 | tf_op jit(solution)/shard_map/all_to_all | solution.py:41
  169.8 2.3 copy.42
  174.1 1.7 fusion.12
  177.2 2.3 shard_map.87
  181.0 10.2 %all-to-all-done.5 = bf16[8,64,768]{2,1,0:T(8,128)(2,1)S(1)} async-done(((bf16[8,64,768]{2,1,0:T(8,128)(2,1)}), bf16[8,64,768]{2,1,0:T(8,128)(2,1)S(1)}, u32[]{:S(2)}, u32[]{:S(2)}) %all-to-all-start.5) | async-done | bytes 786464 | tf_op jit(solution)/shard_map/all_to_all | solution.py:41
  194.1 4.3 %shard_map.88 = (f32[128,1]{1,0:T(8,128)S(1)}, bf16[128,768]{1,0:T(8,128)(2,1)S(1)}, bf16[4,4,128,384]{3,2,1,0:T(8,128)(2,1)}, bf16[4,4,128,384]{3,2,1,0:T(8,128)(2,1)}) custom-call(s32[2]{0:T(128)S(1)} %pad_add_fusion.4.place_ref, bf16[128,768]{1,0:T(8,128)(2,1)S(1)} %fusion.embedded_ref, bf16[128,768]{1,0:T(8,128)(2,1)S(1)} %copy-done.8, ...), custom_call_target="tpu_custom_call" | custom-call | tf_op jit(solution)/shard_map/pallas_call | solution.py:299
  199.5 5.3 %shard_map.89 = (bf16[4,768,256]{2,1,0:T(8,128)(2,1)S(1)}, bf16[4,768,256]{2,1,0:T(8,128)(2,1)}) custom-call(s32[2]{0:T(128)S(1)} %pad_add_fusion.4.place_ref, bf16[128,768]{1,0:T(8,128)(2,1)S(1)} %copy-done.2, bf16[128,768]{1,0:T(8,128)(2,1)S(1)} %get-tuple-element.64.grad_ref, f32[128,2048]{1,0:T(8,128)S(1)} %get-tuple-element.91.slope_ref, ...), custom_call_target="tpu_custom_call" | custom-call | tf_op jit(solution)/shard_map/pallas_call | solution.py:311
  204.8 1.7 add_convert_fusion
  206.5 3.8 %all-to-all-start.6 = ((bf16[4,4,128,384]{3,2,1,0:T(8,128)(2,1)}), bf16[4,4,128,384]{3,2,1,0:T(8,128)(2,1)S(1)}, u32[]{:S(2)}, u32[]{:S(2)}) async-start(bf16[4,4,128,384]{3,2,1,0:T(8,128)(2,1)} %add_convert_fusion), calls=%async_computation.6 | async-start | bytes 3145728 | tf_op jit(solution)/shard_map/all_to_all | solution.py:41
  210.3 2.7 fusion.18
  213.1 3.8 %collective-permute-start.16 = (bf16[768,256]{1,0:T(8,128)(2,1)}, bf16[768,256]{1,0:T(8,128)(2,1)S(1)}, u32[]{:S(2)}, u32[]{:S(2)}) collective-permute-start(bf16[768,256]{1,0:T(8,128)(2,1)} %get-tuple-element.81), channel_id=1, source_target_pairs={{0,192},{64,128},{128,64},{192,0},{1,193},{65,129},{129,65},{193,1... | collective-permute-start | bytes 1179656 | tf_op jit(solution)/shard_map/ppermute | solution.py:49
  216.9 13.4 %all-to-all-done.6 = bf16[4,4,128,384]{3,2,1,0:T(8,128)(2,1)S(1)} async-done(((bf16[4,4,128,384]{3,2,1,0:T(8,128)(2,1)}), bf16[4,4,128,384]{3,2,1,0:T(8,128)(2,1)S(1)}, u32[]{:S(2)}, u32[]{:S(2)}) %all-to-all-start.6) | async-done | bytes 1572896 | tf_op jit(solution)/shard_map/all_to_all | solution.py:41
  231.2 2.4 collective-permute-done.16
  233.8 1.3 collective-permute-start.18
  235.1 2.4 collective-permute-start.19
  237.8 3.7 %all-to-all-start.7 = ((bf16[4,128,384]{2,1,0:T(8,128)(2,1)}), bf16[4,128,384]{2,1,0:T(8,128)(2,1)S(1)}, u32[]{:S(2)}, u32[]{:S(2)}) async-start(bf16[4,128,384]{2,1,0:T(8,128)(2,1)} %fusion.19), calls=%async_computation.7 | async-start | bytes 786432 | tf_op jit(solution)/shard_map/all_to_all | solution.py:41
  242.3 5.4 %all-to-all-done.7 = bf16[4,128,384]{2,1,0:T(8,128)(2,1)S(1)} async-done(((bf16[4,128,384]{2,1,0:T(8,128)(2,1)}), bf16[4,128,384]{2,1,0:T(8,128)(2,1)S(1)}, u32[]{:S(2)}, u32[]{:S(2)}) %all-to-all-start.7) | async-done | bytes 393248 | tf_op jit(solution)/shard_map/all_to_all | solution.py:41
  247.8 12.2 %all_to_all.78 = bf16[8,96,128]{2,1,0:T(8,128)(2,1)S(1)} all-to-all(bf16[8,96,128]{2,1,0:T(8,128)(2,1)S(1)} %constant_dynamic-update-slice_fusion.4), channel_id=1, replica_groups=mesh['x'=4,'core'=2,'z'=8,'y'=4] {'z'}, dimensions={0} | all-to-all | bytes 393216 | tf_op jit(solution)/shard_map/all_to_all | solution.py:41
  260.8 8.8 %all-to-all-start.9 = ((bf16[8,96,128]{2,1,0:T(8,128)(2,1)}), bf16[8,96,128]{2,1,0:T(8,128)(2,1)S(1)}, u32[]{:S(2)}, u32[]{:S(2)}) async-start(bf16[8,96,128]{2,1,0:T(8,128)(2,1)} %broadcast_in_dim.126), calls=%async_computation.9 | async-start | bytes 393216 | tf_op jit(solution)/shard_map/all_to_all | solution.py:41
  270.2 5.3 %all-to-all-done.9 = bf16[8,96,128]{2,1,0:T(8,128)(2,1)S(1)} async-done(((bf16[8,96,128]{2,1,0:T(8,128)(2,1)}), bf16[8,96,128]{2,1,0:T(8,128)(2,1)S(1)}, u32[]{:S(2)}, u32[]{:S(2)}) %all-to-all-start.9) | async-done | bytes 196640 | tf_op jit(solution)/shard_map/all_to_all | solution.py:41
  (178 shorter events, 33.4 us)
Async XLA Ops:
  0.6 19.4 %copy-start = (bf16[64,768]{1,0:T(8,128)(2,1)S(1)}, bf16[64,768]{1,0:T(8,128)(2,1)}, u32[]{:S(2)}) copy-start(bf16[64,768]{1,0:T(8,128)(2,1)} %param.11) | copy-start | bytes 294916
  7.9 20.6 %all-to-all-start = ((s32[32,1,128]{2,1,0:T(1,128)}), s32[32,1,128]{2,1,0:T(1,128)S(1)}, u32[]{:S(2)}, u32[]{:S(2)}) async-start(s32[32,1,128]{2,1,0:T(1,128)} %bitcast.2), calls=%async_computation | async-start | bytes 32768 | tf_op jit(solution)/shard_map/all_to_all | solution.py:41
  39.1 32.2 %all-to-all-start.1 = ((bf16[32,16,768]{2,1,0:T(8,128)(2,1)}), bf16[32,16,768]{2,1,0:T(8,128)(2,1)S(1)}, u32[]{:S(2)}, u32[]{:S(2)}) async-start(bf16[32,16,768]{2,1,0:T(8,128)(2,1)} %broadcast_in_dim.107), calls=%async_computation.1 | async-start | bytes 1572864 | tf_op jit(solution)/shard_map/all_to_all | solution.py:41
  43.0 25.4 %collective-permute-start = (bf16[512,768]{1,0:T(8,128)(2,1)}, bf16[512,768]{1,0:T(8,128)(2,1)S(1)}, u32[]{:S(2)}, u32[]{:S(2)}) collective-permute-start(bf16[512,768]{1,0:T(8,128)(2,1)} %get-tuple-element.90), channel_id=1, source_target_pairs={{0,1},{1,0},{2,3},{3,2},{4,5},{5,4},{6,7},{7,6},{8,9},{9,8},{10,11... | collective-permute-start | bytes 2359304 | tf_op jit(solution)/shard_map/ppermute | solution.py:49
  44.3 27.0 %collective-permute-start.1 = (bf16[512,768]{1,0:T(8,128)(2,1)S(1)}, bf16[512,768]{1,0:T(8,128)(2,1)S(1)}, u32[]{:S(2)}, u32[]{:S(2)}) collective-permute-start(bf16[512,768]{1,0:T(8,128)(2,1)S(1)} %get-tuple-element.89), channel_id=1, source_target_pairs={{0,3},{1,2},{2,1},{3,0},{4,7},{5,6},{6,5},{7,4},{8,11},{9,10},{10,... | collective-permute-start | bytes 2359304 | tf_op jit(solution)/shard_map/ppermute | solution.py:49
  59.3 32.2 %collective-permute-start.9 = (bf16[512,768]{1,0:T(8,128)(2,1)}, bf16[512,768]{1,0:T(8,128)(2,1)}, u32[]{:S(2)}, u32[]{:S(2)}) collective-permute-start(bf16[512,768]{1,0:T(8,128)(2,1)} %get-tuple-element.86), channel_id=1, source_target_pairs={{0,1},{1,0},{2,3},{3,2},{4,5},{5,4},{6,7},{7,6},{8,9},{9,8},{10,11... | collective-permute-start | bytes 2359304 | tf_op jit(solution)/shard_map/ppermute | solution.py:49
  59.7 37.4 %collective-permute-start.10 = (bf16[512,768]{1,0:T(8,128)(2,1)}, bf16[512,768]{1,0:T(8,128)(2,1)}, u32[]{:S(2)}, u32[]{:S(2)}) collective-permute-start(bf16[512,768]{1,0:T(8,128)(2,1)} %get-tuple-element.85), channel_id=1, source_target_pairs={{0,3},{1,2},{2,1},{3,0},{4,7},{5,6},{6,5},{7,4},{8,11},{9,10},{10,... | collective-permute-start | bytes 2359304 | tf_op jit(solution)/shard_map/ppermute | solution.py:49
  71.3 16.4 %copy-start.18 = (bf16[512,768]{1,0:T(8,128)(2,1)}, bf16[512,768]{1,0:T(8,128)(2,1)S(1)}, u32[]{:S(2)}) copy-start(bf16[512,768]{1,0:T(8,128)(2,1)S(1)} %collective-permute-done.1) | copy-start | bytes 2359300
  71.3 31.9 %all-to-all-start.2 = ((bf16[8,64,768]{2,1,0:T(8,128)(2,1)}), bf16[8,64,768]{2,1,0:T(8,128)(2,1)S(1)}, u32[]{:S(2)}, u32[]{:S(2)}) async-start(bf16[8,64,768]{2,1,0:T(8,128)(2,1)} %bitcast.8), calls=%async_computation.2 | async-start | bytes 1572864 | tf_op jit(solution)/shard_map/all_to_all | solution.py:41
  87.7 31.1 %collective-permute-start.2 = (bf16[32,16,768]{2,1,0:T(8,128)(2,1)S(1)}, bf16[32,16,768]{2,1,0:T(8,128)(2,1)}, u32[]{:S(2)}, u32[]{:S(2)}) collective-permute-start(bf16[32,16,768]{2,1,0:T(8,128)(2,1)S(1)} %all-to-all-done.1.refs_0_), channel_id=1, source_target_pairs={{0,64},{64,0},{128,192},{192,128},{1,65},{65,1},{129,193},{193,129... | collective-permute-start | bytes 2359304 | tf_op jit(solution)/shard_map/ppermute | solution.py:49
  88.9 33.7 %collective-permute-start.3 = (bf16[32,16,768]{2,1,0:T(8,128)(2,1)S(1)}, bf16[32,16,768]{2,1,0:T(8,128)(2,1)}, u32[]{:S(2)}, u32[]{:S(2)}) collective-permute-start(bf16[32,16,768]{2,1,0:T(8,128)(2,1)S(1)} %all-to-all-done.1.refs_0_), channel_id=1, source_target_pairs={{0,128},{64,192},{128,0},{192,64},{1,129},{65,193},{129,1},{193,65... | collective-permute-start | bytes 2359304 | tf_op jit(solution)/shard_map/ppermute | solution.py:49
  91.3 35.6 %collective-permute-start.4 = (bf16[32,16,768]{2,1,0:T(8,128)(2,1)S(1)}, bf16[32,16,768]{2,1,0:T(8,128)(2,1)}, u32[]{:S(2)}, u32[]{:S(2)}) collective-permute-start(bf16[32,16,768]{2,1,0:T(8,128)(2,1)S(1)} %all-to-all-done.1.refs_0_), channel_id=1, source_target_pairs={{0,192},{64,128},{128,64},{192,0},{1,193},{65,129},{129,65},{193,1... | collective-permute-start | bytes 2359304 | tf_op jit(solution)/shard_map/ppermute | solution.py:49
  94.5 16.7 %collective-permute-start.11 = (bf16[512,768]{1,0:T(8,128)(2,1)}, bf16[512,768]{1,0:T(8,128)(2,1)}, u32[]{:S(2)}, u32[]{:S(2)}) collective-permute-start(bf16[512,768]{1,0:T(8,128)(2,1)} %get-tuple-element.87), channel_id=1, source_target_pairs={{0,2},{1,3},{2,0},{3,1},{4,6},{5,7},{6,4},{7,5},{8,10},{9,11},{10,... | collective-permute-start | bytes 2359304 | tf_op jit(solution)/shard_map/ppermute | solution.py:49
  103.2 31.6 %all-to-all-start.3 = ((bf16[8,64,768]{2,1,0:T(8,128)(2,1)}), bf16[8,64,768]{2,1,0:T(8,128)(2,1)S(1)}, u32[]{:S(2)}, u32[]{:S(2)}) async-start(bf16[8,64,768]{2,1,0:T(8,128)(2,1)} %bitcast.10), calls=%async_computation.3 | async-start | bytes 1572864 | tf_op jit(solution)/shard_map/all_to_all | solution.py:41
  109.9 22.5 %collective-permute-start.12 = (bf16[512,768]{1,0:T(8,128)(2,1)S(1)}, bf16[512,768]{1,0:T(8,128)(2,1)}, u32[]{:S(2)}, u32[]{:S(2)}) collective-permute-start(bf16[512,768]{1,0:T(8,128)(2,1)S(1)} %broadcast_select_fusion), channel_id=1, source_target_pairs={{0,2},{1,3},{2,0},{3,1},{4,6},{5,7},{6,4},{7,5},{8,10},{9,11},{10,... | collective-permute-start | bytes 2359304 | tf_op jit(solution)/shard_map/ppermute | solution.py:49
  111.3 30.2 %collective-permute-start.5 = (bf16[32,16,768]{2,1,0:T(8,128)(2,1)S(1)}, bf16[32,16,768]{2,1,0:T(8,128)(2,1)}, u32[]{:S(2)}, u32[]{:S(2)}) collective-permute-start(bf16[32,16,768]{2,1,0:T(8,128)(2,1)S(1)} %all-to-all-done.1.refs_0_), channel_id=1, source_target_pairs={{0,32},{32,0},{1,33},{33,1},{2,34},{34,2},{3,35},{35,3},{4,36},{36... | collective-permute-start | bytes 2359304 | tf_op jit(solution)/shard_map/ppermute | solution.py:49
  118.8 22.7 %collective-permute-start.6 = (bf16[32,16,768]{2,1,0:T(8,128)(2,1)}, bf16[32,16,768]{2,1,0:T(8,128)(2,1)}, u32[]{:S(2)}, u32[]{:S(2)}) collective-permute-start(bf16[32,16,768]{2,1,0:T(8,128)(2,1)} %collective-permute-done.2.refs_1_), channel_id=1, source_target_pairs={{0,32},{32,0},{1,33},{33,1},{2,34},{34,2},{3,35},{35,3},{4,36},{36... | collective-permute-start | bytes 2359304 | tf_op jit(solution)/shard_map/ppermute | solution.py:49
  122.6 18.9 %collective-permute-start.7 = (bf16[32,16,768]{2,1,0:T(8,128)(2,1)}, bf16[32,16,768]{2,1,0:T(8,128)(2,1)}, u32[]{:S(2)}, u32[]{:S(2)}) collective-permute-start(bf16[32,16,768]{2,1,0:T(8,128)(2,1)} %collective-permute-done.3.refs_2_), channel_id=1, source_target_pairs={{0,32},{32,0},{1,33},{33,1},{2,34},{34,2},{3,35},{35,3},{4,36},{36... | collective-permute-start | bytes 2359304 | tf_op jit(solution)/shard_map/ppermute | solution.py:49
  126.9 14.6 %collective-permute-start.8 = (bf16[32,16,768]{2,1,0:T(8,128)(2,1)}, bf16[32,16,768]{2,1,0:T(8,128)(2,1)}, u32[]{:S(2)}, u32[]{:S(2)}) collective-permute-start(bf16[32,16,768]{2,1,0:T(8,128)(2,1)} %collective-permute-done.4.refs_3_), channel_id=1, source_target_pairs={{0,32},{32,0},{1,33},{33,1},{2,34},{34,2},{3,35},{35,3},{4,36},{36... | collective-permute-start | bytes 2359304 | tf_op jit(solution)/shard_map/ppermute | solution.py:49
  134.8 12.3 %copy-start.3 = (bf16[8,64,768]{2,1,0:T(8,128)(2,1)}, bf16[8,64,768]{2,1,0:T(8,128)(2,1)S(1)}, u32[]{:S(2)}) copy-start(bf16[8,64,768]{2,1,0:T(8,128)(2,1)S(1)} %all-to-all-done.3) | copy-start | bytes 2359300
  134.8 30.2 %all-to-all-start.4 = ((bf16[8,64,768]{2,1,0:T(8,128)(2,1)}), bf16[8,64,768]{2,1,0:T(8,128)(2,1)S(1)}, u32[]{:S(2)}, u32[]{:S(2)}) async-start(bf16[8,64,768]{2,1,0:T(8,128)(2,1)} %bitcast.182), calls=%async_computation.4 | async-start | bytes 1572864 | tf_op jit(solution)/shard_map/all_to_all | solution.py:41
  147.2 9.5 %slice-start = ((s8[6291456]{0:T(1024)(128)(4,1)}), s8[4194304]{0:T(1024)(128)(4,1)S(1)}, s32[]{:S(2)}) async-start(s8[6291456]{0:T(1024)(128)(4,1)} %bitcast.180), calls=%async_computation.10 | async-start | bytes 8388608
  150.2 0.9 copy-start.2
  150.2 6.4 %slice-start.1 = ((s8[6291456]{0:T(1024)(128)(4,1)}), s8[2097152]{0:T(1024)(128)(4,1)S(1)}, s32[]{:S(2)}) async-start(s8[6291456]{0:T(1024)(128)(4,1)} %bitcast.180), calls=%async_computation.11 | async-start | bytes 4194304
  158.5 11.2 %copy-start.19 = (bf16[32,8,256]{2,1,0:T(8,128)(2,1)S(1)}, bf16[32,8,256]{2,1,0:T(8,128)(2,1)}, u32[]{:S(2)}) copy-start(bf16[32,8,256]{2,1,0:T(8,128)(2,1)} %get-tuple-element.101) | copy-start | bytes 393220
  166.0 25.2 %all-to-all-start.5 = ((bf16[8,64,768]{2,1,0:T(8,128)(2,1)}), bf16[8,64,768]{2,1,0:T(8,128)(2,1)S(1)}, u32[]{:S(2)}, u32[]{:S(2)}) async-start(bf16[8,64,768]{2,1,0:T(8,128)(2,1)} %bitcast.41), calls=%async_computation.5 | async-start | bytes 1572864 | tf_op jit(solution)/shard_map/all_to_all | solution.py:41
  172.1 3.7 %copy-start.15 = (bf16[32,4,2,8,768]{4,3,2,1,0:T(8,128)(2,1)}, bf16[32,4,2,8,768]{4,3,2,1,0:T(8,128)(2,1)S(1)}, u32[]{:S(2)}) copy-start(bf16[32,4,2,8,768]{4,3,2,1,0:T(8,128)(2,1)S(1)} %copy.42) | copy-start | bytes 9437188
  175.8 1.1 copy-start.4
  175.8 1.4 copy-start.6
  175.8 1.4 copy-start.7
  191.2 0.9 copy-start.8
  192.1 1.0 copy-start.10
  193.1 0.9 copy-start.12
  199.0 5.8 %collective-permute-start.17 = (bf16[4,4,128,384]{3,2,1,0:T(8,128)(2,1)}, bf16[4,4,128,384]{3,2,1,0:T(8,128)(2,1)S(1)}, u32[]{:S(2)}, u32[]{:S(2)}) collective-permute-start(bf16[4,4,128,384]{3,2,1,0:T(8,128)(2,1)} %get-tuple-element.68), channel_id=1, source_target_pairs={{0,32},{32,0},{1,33},{33,1},{2,34},{34,2},{3,35},{35,3},{4,36},{36... | collective-permute-start | bytes 4718600 | tf_op jit(solution)/shard_map/ppermute | solution.py:49
  199.5 5.3 %copy-start.16 = (bf16[4,4,128,384]{3,2,1,0:T(8,128)(2,1)S(1)}, bf16[4,4,128,384]{3,2,1,0:T(8,128)(2,1)}, u32[]{:S(2)}) copy-start(bf16[4,4,128,384]{3,2,1,0:T(8,128)(2,1)} %get-tuple-element.67) | copy-start | bytes 4718596
  204.8 5.5 %collective-permute-start.13 = (bf16[4,768,256]{2,1,0:T(8,128)(2,1)}, bf16[4,768,256]{2,1,0:T(8,128)(2,1)}, u32[]{:S(2)}, u32[]{:S(2)}) collective-permute-start(bf16[4,768,256]{2,1,0:T(8,128)(2,1)} %get-tuple-element.66), channel_id=1, source_target_pairs={{0,32},{32,0},{1,33},{33,1},{2,34},{34,2},{3,35},{35,3},{4,36},{36... | collective-permute-start | bytes 4718600 | tf_op jit(solution)/shard_map/ppermute | solution.py:49
  206.5 23.8 %all-to-all-start.6 = ((bf16[4,4,128,384]{3,2,1,0:T(8,128)(2,1)}), bf16[4,4,128,384]{3,2,1,0:T(8,128)(2,1)S(1)}, u32[]{:S(2)}, u32[]{:S(2)}) async-start(bf16[4,4,128,384]{3,2,1,0:T(8,128)(2,1)} %add_convert_fusion), calls=%async_computation.6 | async-start | bytes 3145728 | tf_op jit(solution)/shard_map/all_to_all | solution.py:41
  213.0 20.6 %copy-start.17 = (bf16[768,256]{1,0:T(8,128)(2,1)S(1)}, bf16[768,256]{1,0:T(8,128)(2,1)}, u32[]{:S(2)}) copy-start(bf16[768,256]{1,0:T(8,128)(2,1)} %get-tuple-element.69) | copy-start | bytes 1179652
  213.0 18.2 %collective-permute-start.14 = (bf16[768,256]{1,0:T(8,128)(2,1)}, bf16[768,256]{1,0:T(8,128)(2,1)S(1)}, u32[]{:S(2)}, u32[]{:S(2)}) collective-permute-start(bf16[768,256]{1,0:T(8,128)(2,1)} %get-tuple-element.83), channel_id=1, source_target_pairs={{0,64},{64,0},{128,192},{192,128},{1,65},{65,1},{129,193},{193,129... | collective-permute-start | bytes 1179656 | tf_op jit(solution)/shard_map/ppermute | solution.py:49
  213.0 18.2 %collective-permute-start.15 = (bf16[768,256]{1,0:T(8,128)(2,1)}, bf16[768,256]{1,0:T(8,128)(2,1)S(1)}, u32[]{:S(2)}, u32[]{:S(2)}) collective-permute-start(bf16[768,256]{1,0:T(8,128)(2,1)} %get-tuple-element.82), channel_id=1, source_target_pairs={{0,128},{64,192},{128,0},{192,64},{1,129},{65,193},{129,1},{193,65... | collective-permute-start | bytes 1179656 | tf_op jit(solution)/shard_map/ppermute | solution.py:49
  213.1 20.5 %collective-permute-start.16 = (bf16[768,256]{1,0:T(8,128)(2,1)}, bf16[768,256]{1,0:T(8,128)(2,1)S(1)}, u32[]{:S(2)}, u32[]{:S(2)}) collective-permute-start(bf16[768,256]{1,0:T(8,128)(2,1)} %get-tuple-element.81), channel_id=1, source_target_pairs={{0,192},{64,128},{128,64},{192,0},{1,193},{65,129},{129,65},{193,1... | collective-permute-start | bytes 1179656 | tf_op jit(solution)/shard_map/ppermute | solution.py:49
  233.8 7.6 %collective-permute-start.18 = (bf16[8,24,256]{2,1,0:T(8,128)(2,1)S(1)}, bf16[8,24,256]{2,1,0:T(8,128)(2,1)S(1)}, u32[]{:S(2)}, u32[]{:S(2)}) collective-permute-start(bf16[8,24,256]{2,1,0:T(8,128)(2,1)S(1)} %get-tuple-element.93), channel_id=1, source_target_pairs={{0,1},{1,0},{2,3},{3,2},{4,5},{5,4},{6,7},{7,6},{8,9},{9,8},{10,11... | collective-permute-start | bytes 294920 | tf_op jit(solution)/shard_map/ppermute | solution.py:49
  235.1 6.3 %collective-permute-start.19 = (bf16[8,24,256]{2,1,0:T(8,128)(2,1)S(1)}, bf16[8,24,256]{2,1,0:T(8,128)(2,1)S(1)}, u32[]{:S(2)}, u32[]{:S(2)}) collective-permute-start(bf16[8,24,256]{2,1,0:T(8,128)(2,1)S(1)} %get-tuple-element.95), channel_id=1, source_target_pairs={{0,2},{1,3},{2,0},{3,1},{4,6},{5,7},{6,4},{7,5},{8,10},{9,11},{10,... | collective-permute-start | bytes 294920 | tf_op jit(solution)/shard_map/ppermute | solution.py:49
  237.5 32.1 %copy-start.14 = (f32[128,1]{1,0:T(8,128)S(1)}, f32[128,1]{1,0:T(8,128)}, u32[]{:S(2)}) copy-start(f32[128,1]{1,0:T(8,128)} %copy-done.13) | copy-start | bytes 1540
  237.5 4.7 %collective-permute-start.20 = (bf16[8,24,256]{2,1,0:T(8,128)(2,1)S(1)}, bf16[8,24,256]{2,1,0:T(8,128)(2,1)S(1)}, u32[]{:S(2)}, u32[]{:S(2)}) collective-permute-start(bf16[8,24,256]{2,1,0:T(8,128)(2,1)S(1)} %get-tuple-element.94), channel_id=1, source_target_pairs={{0,3},{1,2},{2,1},{3,0},{4,7},{5,6},{6,5},{7,4},{8,11},{9,10},{10,... | collective-permute-start | bytes 294920 | tf_op jit(solution)/shard_map/ppermute | solution.py:49
  237.8 9.9 %all-to-all-start.7 = ((bf16[4,128,384]{2,1,0:T(8,128)(2,1)}), bf16[4,128,384]{2,1,0:T(8,128)(2,1)S(1)}, u32[]{:S(2)}, u32[]{:S(2)}) async-start(bf16[4,128,384]{2,1,0:T(8,128)(2,1)} %fusion.19), calls=%async_computation.7 | async-start | bytes 786432 | tf_op jit(solution)/shard_map/all_to_all | solution.py:41
  260.8 14.7 %all-to-all-start.9 = ((bf16[8,96,128]{2,1,0:T(8,128)(2,1)}), bf16[8,96,128]{2,1,0:T(8,128)(2,1)S(1)}, u32[]{:S(2)}, u32[]{:S(2)}) async-start(bf16[8,96,128]{2,1,0:T(8,128)(2,1)} %broadcast_in_dim.126), calls=%async_computation.9 | async-start | bytes 393216 | tf_op jit(solution)/shard_map/all_to_all | solution.py:41
  275.5 0.9 copy-start.1
  (5 other events, 3.7 us)

commit v7 on v6

--- a/solution.py
+++ b/solution.py
@@ -54,33 +54,36 @@
 
 
 def request_kernel(shift, ids_ref, code_ref, query_ref):
-    ids = ids_ref[...]
-    q_dev, neg = ids.shape
-    lane = lax.broadcasted_iota(jnp.int32, (q_dev, q_dev), 1)
-    query = lax.broadcasted_iota(jnp.int32, (q_dev, q_dev), 0)
-    before = (lane < query).astype(jnp.float32).astype(jnp.bfloat16)
-    kind, pair_lane = lane // PAIRS, lane % PAIRS
-    seen = jnp.zeros((1, q_dev), jnp.float32)
-    placed = jnp.zeros((q_dev, q_dev), jnp.float32)
+    neg, q_dev = ids_ref.shape
+    owner_row = lax.broadcasted_iota(jnp.int32, (SHARD, q_dev), 0)
+    first = lax.broadcasted_iota(jnp.int32, (q_dev, q_dev), 0)
+    before = (first < lax.broadcasted_iota(jnp.int32, (q_dev, q_dev), 1)).astype(jnp.float32)
+    before = before.astype(jnp.bfloat16)
+    rows = 2 * SHARD + PAIRS
+    row = lax.broadcasted_iota(jnp.int32, (rows, q_dev), 0)
+    query = lax.broadcasted_iota(jnp.int32, (1, q_dev), 1)
+    pair_row = jnp.where(row < 2 * SHARD, (row & (SHARD - 1)) >> 1, row - 2 * SHARD)
+    seen = jnp.zeros((SHARD, 1), jnp.float32)
+    placed = jnp.zeros((rows, q_dev), jnp.float32)
     for k in range(neg):
-        id_k = ids[:, k : k + 1]
-        owner = id_k >> shift
+        ids = ids_ref[k : k + 1, :]
+        owner = ids >> shift
         odd = owner & 1
-        member = owner == lane
+        member = owner == owner_row
         ones = member.astype(jnp.float32)
-        counts = seen + jnp.dot(before, ones.astype(jnp.bfloat16), preferred_element_type=jnp.float32)
-        rank = jnp.sum(jnp.where(member, counts, 0.0), axis=1, keepdims=True).astype(jnp.int32)
-        seen = seen + jnp.sum(ones, axis=0, keepdims=True)
+        counts = seen + jnp.dot(ones.astype(jnp.bfloat16), before, preferred_element_type=jnp.float32)
+        rank = jnp.sum(jnp.where(member, counts, 0.0), axis=0, keepdims=True).astype(jnp.int32)
+        seen = seen + jnp.sum(ones, axis=1, keepdims=True)
         slot = jnp.where(odd == 1, q_dev - 1 - rank, rank)
-        at_slot = (slot == lane).astype(jnp.float32).astype(jnp.bfloat16)
-        code = (odd << shift) + (id_k - (owner << shift))
+        at_slot = (slot == first).astype(jnp.float32).astype(jnp.bfloat16)
+        code = (odd << shift) + (ids - (owner << shift))
         item = jnp.where(
-            kind == 0, code >> 6, jnp.where(kind == 1, code & 63, jnp.where(kind == 2, query, 0))
+            row < SHARD, code >> 6, jnp.where(row < 2 * SHARD, code & 63, query)
         )
-        item = jnp.where((owner >> 1) == pair_lane, item, 0)
-        placed = placed + contract_first(item.astype(jnp.float32).astype(jnp.bfloat16), at_slot)
-    code_ref[...] = (placed[:PAIRS] * 64.0 + placed[PAIRS : 2 * PAIRS]).astype(jnp.int32)
-    query_ref[...] = placed[2 * PAIRS : 3 * PAIRS].astype(jnp.int32)
+        item = jnp.where((owner >> 1) == pair_row, item, 0)
+        placed = placed + contract_last(item.astype(jnp.float32).astype(jnp.bfloat16), at_slot)
+    code_ref[...] = (placed[:SHARD] * 64.0 + placed[SHARD : 2 * SHARD]).astype(jnp.int32)
+    query_ref[...] = placed[2 * SHARD :].astype(jnp.int32)
 
 
 def arrange_kernel(place_ref, *refs):
@@ -212,13 +215,15 @@
     in_smem = pl.BlockSpec(memory_space=pltpu.SMEM)
     in_vmem = pl.BlockSpec(memory_space=pltpu.VMEM)
 
-    slots = jax.ShapeDtypeStruct((PAIRS, q_dev), jnp.int32)
     code, slot_query = pl.pallas_call(
-        functools.partial(request_kernel, shift), out_shape=[slots] * 2, **limits
-    )(negative_ids)
-    code = exchange(
-        jnp.broadcast_to(code[:, None], (PAIRS, 2, q_dev)).reshape(SHARD, q_dev), ("z", "y")
-    ).reshape(Z, Y, q_dev)
+        functools.partial(request_kernel, shift),
+        out_shape=[
+            jax.ShapeDtypeStruct((SHARD, q_dev), jnp.int32),
+            jax.ShapeDtypeStruct((PAIRS, q_dev), jnp.int32),
+        ],
+        **limits,
+    )(negative_ids.T)
+    code = exchange(code, ("z", "y")).reshape(Z, Y, q_dev)
     code = jnp.stack([lax.dynamic_index_in_dim(code, my_y ^ by, 1, False) for by in range(Y)])
     own = (code >> shift) == my_y % 2
     wanted = code & (rows_dev - 1)

time: 278 us -> 273 us (0.982)
  Pallas kernels: 23.4 us -> 19.5 us
    pallas_call x1, Pallas kernels: 5.85 us -> 1.92 us  [shards(): pl.pallas_call(functools.partial(request_kernel, shift), out_shape=[jax.S...]
    unnamed x54 -> x55, local copies, waits for them, and re-layouts: 8.28 us -> 8.17 us
where the time goes in v7:
time: 273 us; the launch traced here: 272 us
  starting transfers between devices  89.6 us (33%)
  waiting for transfers between devices  65.2 us (24%)
  local copies, waits for them, and re-layouts  52.9 us (19%)
  other arithmetic  23.2 us (8%)
  Pallas kernels  19.5 us (7%)
  blocking collectives  12.3 us (5%)
  matrix products  7.92 us (3%)
    all_to_all x9, starting transfers between devices, exchange(): return lax.all_to_all(value, axes, split_axis=0, concat_axis=0, tiled=True)  56.1 us
    all_to_all x9, waiting for transfers between devices, exchange(): return lax.all_to_all(value, axes, split_axis=0, concat_axis=0, tiled=True)  48.6 us
    gather x4, local copies, waits for them, and re-layouts, find(): passage_table.at[ids].get(mode='promise_in_bounds')  33.6 us
    ppermute x21, starting transfers between devices, swap(): lax.ppermute(value, axis, [(i, i ^ by) for i in range(lax.axis_size(axis))])  33.5 us
    ppermute x21, waiting for transfers between devices, swap(): lax.ppermute(value, axis, [(i, i ^ by) for i in range(lax.axis_size(axis))])  16.6 us
    all_to_all x1, blocking collectives, exchange(): return lax.all_to_all(value, axes, split_axis=0, concat_axis=0, tiled=True)  12.3 us
    unnamed x55, local copies, waits for them, and re-layouts  8.17 us
    dot_general x8, matrix products, shards(): jnp.dot(queries, part, preferred_element_type=jnp.float32)  7.31 us
  transfers between devices with their start and end apart: 30, of which 12 were waited for; matrix products, arithmetic and copies ran while one was open for 23% of the time, Pallas kernels for 5%

profile of v7, /device:TPU:1, one launch (start us, length us, event | category | flops | bytes accessed | tf_op | source)
XLA Modules:
  0.0 271.9 jit_solution(585969883158699393)
XLA Ops:
  1.4 1.9 shard_map.85
  3.3 12.0 %all-to-all-start = ((s32[32,1,128]{2,1,0:T(1,128)}), s32[32,1,128]{2,1,0:T(1,128)S(1)}, u32[]{:S(2)}, u32[]{:S(2)}) async-start(s32[32,1,128]{2,1,0:T(1,128)} %bitcast.4), calls=%async_computation | async-start | bytes 32768 | tf_op jit(solution)/shard_map/all_to_all | solution.py:41
  16.1 7.7 %all-to-all-done = s32[32,1,128]{2,1,0:T(1,128)S(1)} async-done(((s32[32,1,128]{2,1,0:T(1,128)}), s32[32,1,128]{2,1,0:T(1,128)S(1)}, u32[]{:S(2)}, u32[]{:S(2)}) %all-to-all-start) | async-done | bytes 16416 | tf_op jit(solution)/shard_map/all_to_all | solution.py:41
  24.3 8.1 %gather_fusion = bf16[1024,768]{1,0:T(8,128)(2,1)S(1)} fusion(bf16[4096,768]{1,0:T(8,128)(2,1)} %param.9, s32[1024]{0:T(1024)S(1)} %fusion.40), kind=kCustom, calls=%fused_computation | custom fusion | bytes 3149824 | tf_op jit(solution)/shard_map/gather | solution.py:237
  34.4 3.9 %all-to-all-start.1 = ((bf16[32,16,768]{2,1,0:T(8,128)(2,1)}), bf16[32,16,768]{2,1,0:T(8,128)(2,1)S(1)}, u32[]{:S(2)}, u32[]{:S(2)}) async-start(bf16[32,16,768]{2,1,0:T(8,128)(2,1)} %broadcast_in_dim.100), calls=%async_computation.1 | async-start | bytes 1572864 | tf_op jit(solution)/shard_map/all_to_all | solution.py:41
  39.6 1.8 collective-permute-start.1
  41.5 10.3 %gather_fusion.1 = bf16[1536,768]{1,0:T(8,128)(2,1)} fusion(bf16[4096,768]{1,0:T(8,128)(2,1)} %param.9, s32[2048]{0:T(1024)S(1)} %pad_clamp_fusion), kind=kCustom, calls=%fused_computation.1 | custom fusion | bytes 4724736 | tf_op jit(solution)/shard_map/gather | solution.py:237
  51.9 2.7 %slice_select_fusion.3 = (bf16[512,768]{1,0:T(8,128)(2,1)}, bf16[512,768]{1,0:T(8,128)(2,1)}) fusion(bf16[1536,768]{1,0:T(8,128)(2,1)} %gather_fusion.1, pred[512]{0:T(512)(128)(4,1)S(1)} %broadcast_in_dim.106, pred[512]{0:T(512)(128)(4,1)S(1)} %broadcast_in_dim.104), kind=kLoop, calls=%fused_computation.35 | loop fusion | flops 786432 | bytes 3146752 | tf_op jit(solution)/shard_map/jit(_where)/select_n | solution.py:239
  55.7 8.1 %collective-permute-done = bf16[512,768]{1,0:T(8,128)(2,1)S(1)} collective-permute-done((bf16[512,768]{1,0:T(8,128)(2,1)}, bf16[512,768]{1,0:T(8,128)(2,1)S(1)}, u32[]{:S(2)}, u32[]{:S(2)}) %collective-permute-start) | collective-permute-done | bytes 786464 | tf_op jit(solution)/shard_map/ppermute | solution.py:49
  63.8 2.2 fusion.14
  66.7 6.8 %all-to-all-start.2 = ((bf16[8,64,768]{2,1,0:T(8,128)(2,1)}), bf16[8,64,768]{2,1,0:T(8,128)(2,1)S(1)}, u32[]{:S(2)}, u32[]{:S(2)}) async-start(bf16[8,64,768]{2,1,0:T(8,128)(2,1)} %bitcast.10), calls=%async_computation.2 | async-start | bytes 1572864 | tf_op jit(solution)/shard_map/all_to_all | solution.py:41
  73.8 9.2 %gather_fusion.2 = bf16[1024,768]{1,0:T(8,128)(2,1)} fusion(bf16[4096,768]{1,0:T(8,128)(2,1)} %param.9, s32[1024]{0:T(1024)S(1)} %fusion.41), kind=kCustom, calls=%fused_computation.2 | custom fusion | bytes 3149824 | tf_op jit(solution)/shard_map/gather | solution.py:237
  84.2 2.4 collective-permute-start.3
  86.9 3.0 %slice_select_fusion = (bf16[512,768]{1,0:T(8,128)(2,1)}, bf16[512,768]{1,0:T(8,128)(2,1)}) fusion(bf16[1024,768]{1,0:T(8,128)(2,1)} %gather_fusion.2, pred[512]{0:T(512)(128)(4,1)S(1)} %broadcast_in_dim.115, bf16[512,768]{1,0:T(8,128)(2,1)} %collective-permute-done.9, pred[512]{0:T(512)(128)(4,1)S(1)} %broadcast_in_dim.110), kind=kLoop, calls=%fused_computation.31 | loop fusion | flops 1179648 | bytes 3933184 | tf_op jit(solution)/shard_map/jit(_where)/select_n | solution.py:239
  89.9 2.5 collective-permute-start.11
  92.5 6.0 %gather_fusion.3 = bf16[512,768]{1,0:T(8,128)(2,1)S(1)} fusion(bf16[4096,768]{1,0:T(8,128)(2,1)} %param.9, s32[1024]{0:T(1024)S(1)} %pad_clamp_fusion.1), kind=kCustom, calls=%fused_computation.3 | custom fusion | bytes 1574912 | tf_op jit(solution)/shard_map/gather | solution.py:237
  98.6 6.7 %all-to-all-start.3 = ((bf16[8,64,768]{2,1,0:T(8,128)(2,1)}), bf16[8,64,768]{2,1,0:T(8,128)(2,1)S(1)}, u32[]{:S(2)}, u32[]{:S(2)}) async-start(bf16[8,64,768]{2,1,0:T(8,128)(2,1)} %bitcast.12), calls=%async_computation.3 | async-start | bytes 1572864 | tf_op jit(solution)/shard_map/all_to_all | solution.py:41
  106.6 7.5 %collective-permute-start.5 = (bf16[32,16,768]{2,1,0:T(8,128)(2,1)S(1)}, bf16[32,16,768]{2,1,0:T(8,128)(2,1)}, u32[]{:S(2)}, u32[]{:S(2)}) collective-permute-start(bf16[32,16,768]{2,1,0:T(8,128)(2,1)S(1)} %all-to-all-done.1.refs_0_), channel_id=1, source_target_pairs={{0,32},{32,0},{1,33},{33,1},{2,34},{34,2},{3,35},{35,3},{4,36},{36... | collective-permute-start | bytes 2359304 | tf_op jit(solution)/shard_map/ppermute | solution.py:49
  114.2 3.8 %collective-permute-done.3.refs_2_ = bf16[32,16,768]{2,1,0:T(8,128)(2,1)} collective-permute-done((bf16[32,16,768]{2,1,0:T(8,128)(2,1)S(1)}, bf16[32,16,768]{2,1,0:T(8,128)(2,1)}, u32[]{:S(2)}, u32[]{:S(2)}) %collective-permute-start.3) | collective-permute-done | bytes 786464 | tf_op jit(solution)/shard_map/ppermute | solution.py:49
  118.0 4.3 %collective-permute-start.7 = (bf16[32,16,768]{2,1,0:T(8,128)(2,1)}, bf16[32,16,768]{2,1,0:T(8,128)(2,1)}, u32[]{:S(2)}, u32[]{:S(2)}) collective-permute-start(bf16[32,16,768]{2,1,0:T(8,128)(2,1)} %collective-permute-done.3.refs_2_), channel_id=1, source_target_pairs={{0,32},{32,0},{1,33},{33,1},{2,34},{34,2},{3,35},{35,3},{4,36},{36... | collective-permute-start | bytes 2359304 | tf_op jit(solution)/shard_map/ppermute | solution.py:49
  122.3 2.6 collective-permute-start.8
  125.3 2.4 add.186
  127.8 2.4 add.187
  130.2 6.6 %all-to-all-start.4 = ((bf16[8,64,768]{2,1,0:T(8,128)(2,1)}), bf16[8,64,768]{2,1,0:T(8,128)(2,1)S(1)}, u32[]{:S(2)}, u32[]{:S(2)}) async-start(bf16[8,64,768]{2,1,0:T(8,128)(2,1)} %bitcast.186), calls=%async_computation.4 | async-start | bytes 1572864 | tf_op jit(solution)/shard_map/all_to_all | solution.py:41
  136.9 5.6 %shard_map.86 = bf16[4,2,32,16,768]{4,3,2,1,0:T(8,128)(2,1)} custom-call(s32[2]{0:T(128)S(1)} %pad_add_fusion.4.place_ref, bf16[32,16,768]{2,1,0:T(8,128)(2,1)S(1)} %all-to-all-done.1.refs_0_, bf16[32,16,768]{2,1,0:T(8,128)(2,1)} %collective-permute-done.2.refs_1_, bf16[32,16,768]{2,1,0:T(8,128)(2,1)} %collective-permute-done.3.refs_2_, ...), custom_call_target="tpu_custom_call" | custom-call | tf_op jit(solution)/shard_map/pallas_call | solution.py:268
  142.5 2.2 slice_bitcast_fusion.1
  152.0 1.9 slice_bitcast_fusion
  153.8 6.6 %all-to-all-done.4 = bf16[8,64,768]{2,1,0:T(8,128)(2,1)S(1)} async-done(((bf16[8,64,768]{2,1,0:T(8,128)(2,1)}), bf16[8,64,768]{2,1,0:T(8,128)(2,1)S(1)}, u32[]{:S(2)}, u32[]{:S(2)}) %all-to-all-start.4) | async-done | bytes 786464 | tf_op jit(solution)/shard_map/all_to_all | solution.py:41
  161.3 3.8 %all-to-all-start.5 = ((bf16[8,64,768]{2,1,0:T(8,128)(2,1)}), bf16[8,64,768]{2,1,0:T(8,128)(2,1)S(1)}, u32[]{:S(2)}, u32[]{:S(2)}) async-start(bf16[8,64,768]{2,1,0:T(8,128)(2,1)} %bitcast.43), calls=%async_computation.5 | async-start | bytes 1572864 | tf_op jit(solution)/shard_map/all_to_all | solution.py:41
  165.1 2.3 copy.40
  169.4 1.7 fusion.12
  172.5 2.3 shard_map.87
  176.3 10.3 %all-to-all-done.5 = bf16[8,64,768]{2,1,0:T(8,128)(2,1)S(1)} async-done(((bf16[8,64,768]{2,1,0:T(8,128)(2,1)}), bf16[8,64,768]{2,1,0:T(8,128)(2,1)S(1)}, u32[]{:S(2)}, u32[]{:S(2)}) %all-to-all-start.5) | async-done | bytes 786464 | tf_op jit(solution)/shard_map/all_to_all | solution.py:41
  189.4 4.3 %shard_map.88 = (f32[128,1]{1,0:T(8,128)S(1)}, bf16[128,768]{1,0:T(8,128)(2,1)S(1)}, bf16[4,4,128,384]{3,2,1,0:T(8,128)(2,1)}, bf16[4,4,128,384]{3,2,1,0:T(8,128)(2,1)}) custom-call(s32[2]{0:T(128)S(1)} %pad_add_fusion.4.place_ref, bf16[128,768]{1,0:T(8,128)(2,1)S(1)} %fusion.embedded_ref, bf16[128,768]{1,0:T(8,128)(2,1)S(1)} %copy-done.8, ...), custom_call_target="tpu_custom_call" | custom-call | tf_op jit(solution)/shard_map/pallas_call | solution.py:304
  194.9 5.3 %shard_map.89 = (bf16[4,768,256]{2,1,0:T(8,128)(2,1)S(1)}, bf16[4,768,256]{2,1,0:T(8,128)(2,1)}) custom-call(s32[2]{0:T(128)S(1)} %pad_add_fusion.4.place_ref, bf16[128,768]{1,0:T(8,128)(2,1)S(1)} %copy-done.2, bf16[128,768]{1,0:T(8,128)(2,1)S(1)} %get-tuple-element.64.grad_ref, f32[128,2048]{1,0:T(8,128)S(1)} %get-tuple-element.91.slope_ref, ...), custom_call_target="tpu_custom_call" | custom-call | tf_op jit(solution)/shard_map/pallas_call | solution.py:316
  200.2 1.6 add_convert_fusion
  201.8 3.8 %all-to-all-start.6 = ((bf16[4,4,128,384]{3,2,1,0:T(8,128)(2,1)}), bf16[4,4,128,384]{3,2,1,0:T(8,128)(2,1)S(1)}, u32[]{:S(2)}, u32[]{:S(2)}) async-start(bf16[4,4,128,384]{3,2,1,0:T(8,128)(2,1)} %add_convert_fusion), calls=%async_computation.6 | async-start | bytes 3145728 | tf_op jit(solution)/shard_map/all_to_all | solution.py:41
  205.6 2.8 %fusion.18 = (bf16[768,256]{1,0:T(8,128)(2,1)}, bf16[768,256]{1,0:T(8,128)(2,1)}, bf16[768,256]{1,0:T(8,128)(2,1)}, bf16[768,256]{1,0:T(8,128)(2,1)}) fusion(bf16[4,768,256]{2,1,0:T(8,128)(2,1)} %collective-permute-done.13, bf16[4,768,256]{2,1,0:T(8,128)(2,1)S(1)} %get-tuple-element.65), kind=kLoop, calls=%fused_computation.64 | loop fusion | flops 3145728 | bytes 4718592 | tf_op jit(solution)/shard_map/convert_element_type | solution.py:324
  208.5 3.8 %collective-permute-start.16 = (bf16[768,256]{1,0:T(8,128)(2,1)}, bf16[768,256]{1,0:T(8,128)(2,1)S(1)}, u32[]{:S(2)}, u32[]{:S(2)}) collective-permute-start(bf16[768,256]{1,0:T(8,128)(2,1)} %get-tuple-element.81), channel_id=1, source_target_pairs={{0,192},{64,128},{128,64},{192,0},{1,193},{65,129},{129,65},{193,1... | collective-permute-start | bytes 1179656 | tf_op jit(solution)/shard_map/ppermute | solution.py:49
  212.2 13.4 %all-to-all-done.6 = bf16[4,4,128,384]{3,2,1,0:T(8,128)(2,1)S(1)} async-done(((bf16[4,4,128,384]{3,2,1,0:T(8,128)(2,1)}), bf16[4,4,128,384]{3,2,1,0:T(8,128)(2,1)S(1)}, u32[]{:S(2)}, u32[]{:S(2)}) %all-to-all-start.6) | async-done | bytes 1572896 | tf_op jit(solution)/shard_map/all_to_all | solution.py:41
  226.6 2.4 collective-permute-done.16
  229.2 1.3 collective-permute-start.18
  230.5 2.4 collective-permute-start.19
  233.1 3.7 %all-to-all-start.7 = ((bf16[4,128,384]{2,1,0:T(8,128)(2,1)}), bf16[4,128,384]{2,1,0:T(8,128)(2,1)S(1)}, u32[]{:S(2)}, u32[]{:S(2)}) async-start(bf16[4,128,384]{2,1,0:T(8,128)(2,1)} %fusion.19), calls=%async_computation.7 | async-start | bytes 786432 | tf_op jit(solution)/shard_map/all_to_all | solution.py:41
  237.6 5.4 %all-to-all-done.7 = bf16[4,128,384]{2,1,0:T(8,128)(2,1)S(1)} async-done(((bf16[4,128,384]{2,1,0:T(8,128)(2,1)}), bf16[4,128,384]{2,1,0:T(8,128)(2,1)S(1)}, u32[]{:S(2)}, u32[]{:S(2)}) %all-to-all-start.7) | async-done | bytes 393248 | tf_op jit(solution)/shard_map/all_to_all | solution.py:41
  243.2 12.3 %all_to_all.78 = bf16[8,96,128]{2,1,0:T(8,128)(2,1)S(1)} all-to-all(bf16[8,96,128]{2,1,0:T(8,128)(2,1)S(1)} %constant_dynamic-update-slice_fusion.4), channel_id=1, replica_groups=mesh['x'=4,'core'=2,'z'=8,'y'=4] {'z'}, dimensions={0} | all-to-all | bytes 393216 | tf_op jit(solution)/shard_map/all_to_all | solution.py:41
  256.1 8.8 %all-to-all-start.9 = ((bf16[8,96,128]{2,1,0:T(8,128)(2,1)}), bf16[8,96,128]{2,1,0:T(8,128)(2,1)S(1)}, u32[]{:S(2)}, u32[]{:S(2)}) async-start(bf16[8,96,128]{2,1,0:T(8,128)(2,1)} %broadcast_in_dim.119), calls=%async_computation.9 | async-start | bytes 393216 | tf_op jit(solution)/shard_map/all_to_all | solution.py:41
  265.6 5.3 %all-to-all-done.9 = bf16[8,96,128]{2,1,0:T(8,128)(2,1)S(1)} async-done(((bf16[8,96,128]{2,1,0:T(8,128)(2,1)}), bf16[8,96,128]{2,1,0:T(8,128)(2,1)S(1)}, u32[]{:S(2)}, u32[]{:S(2)}) %all-to-all-start.9) | async-done | bytes 196640 | tf_op jit(solution)/shard_map/all_to_all | solution.py:41
  (178 shorter events, 32.6 us)
Async XLA Ops:
  0.6 14.7 %copy-start = (bf16[64,768]{1,0:T(8,128)(2,1)S(1)}, bf16[64,768]{1,0:T(8,128)(2,1)}, u32[]{:S(2)}) copy-start(bf16[64,768]{1,0:T(8,128)(2,1)} %param.11) | copy-start | bytes 294916
  3.3 20.6 %all-to-all-start = ((s32[32,1,128]{2,1,0:T(1,128)}), s32[32,1,128]{2,1,0:T(1,128)S(1)}, u32[]{:S(2)}, u32[]{:S(2)}) async-start(s32[32,1,128]{2,1,0:T(1,128)} %bitcast.4), calls=%async_computation | async-start | bytes 32768 | tf_op jit(solution)/shard_map/all_to_all | solution.py:41
  34.4 32.2 %all-to-all-start.1 = ((bf16[32,16,768]{2,1,0:T(8,128)(2,1)}), bf16[32,16,768]{2,1,0:T(8,128)(2,1)S(1)}, u32[]{:S(2)}, u32[]{:S(2)}) async-start(bf16[32,16,768]{2,1,0:T(8,128)(2,1)} %broadcast_in_dim.100), calls=%async_computation.1 | async-start | bytes 1572864 | tf_op jit(solution)/shard_map/all_to_all | solution.py:41
  38.3 25.4 %collective-permute-start = (bf16[512,768]{1,0:T(8,128)(2,1)}, bf16[512,768]{1,0:T(8,128)(2,1)S(1)}, u32[]{:S(2)}, u32[]{:S(2)}) collective-permute-start(bf16[512,768]{1,0:T(8,128)(2,1)} %get-tuple-element.90), channel_id=1, source_target_pairs={{0,1},{1,0},{2,3},{3,2},{4,5},{5,4},{6,7},{7,6},{8,9},{9,8},{10,11... | collective-permute-start | bytes 2359304 | tf_op jit(solution)/shard_map/ppermute | solution.py:49
  39.6 27.0 %collective-permute-start.1 = (bf16[512,768]{1,0:T(8,128)(2,1)S(1)}, bf16[512,768]{1,0:T(8,128)(2,1)S(1)}, u32[]{:S(2)}, u32[]{:S(2)}) collective-permute-start(bf16[512,768]{1,0:T(8,128)(2,1)S(1)} %get-tuple-element.89), channel_id=1, source_target_pairs={{0,3},{1,2},{2,1},{3,0},{4,7},{5,6},{6,5},{7,4},{8,11},{9,10},{10,... | collective-permute-start | bytes 2359304 | tf_op jit(solution)/shard_map/ppermute | solution.py:49
  54.7 32.2 %collective-permute-start.9 = (bf16[512,768]{1,0:T(8,128)(2,1)}, bf16[512,768]{1,0:T(8,128)(2,1)}, u32[]{:S(2)}, u32[]{:S(2)}) collective-permute-start(bf16[512,768]{1,0:T(8,128)(2,1)} %get-tuple-element.86), channel_id=1, source_target_pairs={{0,1},{1,0},{2,3},{3,2},{4,5},{5,4},{6,7},{7,6},{8,9},{9,8},{10,11... | collective-permute-start | bytes 2359304 | tf_op jit(solution)/shard_map/ppermute | solution.py:49
  55.0 37.4 %collective-permute-start.10 = (bf16[512,768]{1,0:T(8,128)(2,1)}, bf16[512,768]{1,0:T(8,128)(2,1)}, u32[]{:S(2)}, u32[]{:S(2)}) collective-permute-start(bf16[512,768]{1,0:T(8,128)(2,1)} %get-tuple-element.85), channel_id=1, source_target_pairs={{0,3},{1,2},{2,1},{3,0},{4,7},{5,6},{6,5},{7,4},{8,11},{9,10},{10,... | collective-permute-start | bytes 2359304 | tf_op jit(solution)/shard_map/ppermute | solution.py:49
  66.6 16.4 %copy-start.19 = (bf16[512,768]{1,0:T(8,128)(2,1)}, bf16[512,768]{1,0:T(8,128)(2,1)S(1)}, u32[]{:S(2)}) copy-start(bf16[512,768]{1,0:T(8,128)(2,1)S(1)} %collective-permute-done.1) | copy-start | bytes 2359300
  66.7 31.9 %all-to-all-start.2 = ((bf16[8,64,768]{2,1,0:T(8,128)(2,1)}), bf16[8,64,768]{2,1,0:T(8,128)(2,1)S(1)}, u32[]{:S(2)}, u32[]{:S(2)}) async-start(bf16[8,64,768]{2,1,0:T(8,128)(2,1)} %bitcast.10), calls=%async_computation.2 | async-start | bytes 1572864 | tf_op jit(solution)/shard_map/all_to_all | solution.py:41
  83.0 31.1 %collective-permute-start.2 = (bf16[32,16,768]{2,1,0:T(8,128)(2,1)S(1)}, bf16[32,16,768]{2,1,0:T(8,128)(2,1)}, u32[]{:S(2)}, u32[]{:S(2)}) collective-permute-start(bf16[32,16,768]{2,1,0:T(8,128)(2,1)S(1)} %all-to-all-done.1.refs_0_), channel_id=1, source_target_pairs={{0,64},{64,0},{128,192},{192,128},{1,65},{65,1},{129,193},{193,129... | collective-permute-start | bytes 2359304 | tf_op jit(solution)/shard_map/ppermute | solution.py:49
  84.2 33.7 %collective-permute-start.3 = (bf16[32,16,768]{2,1,0:T(8,128)(2,1)S(1)}, bf16[32,16,768]{2,1,0:T(8,128)(2,1)}, u32[]{:S(2)}, u32[]{:S(2)}) collective-permute-start(bf16[32,16,768]{2,1,0:T(8,128)(2,1)S(1)} %all-to-all-done.1.refs_0_), channel_id=1, source_target_pairs={{0,128},{64,192},{128,0},{192,64},{1,129},{65,193},{129,1},{193,65... | collective-permute-start | bytes 2359304 | tf_op jit(solution)/shard_map/ppermute | solution.py:49
  86.7 35.6 %collective-permute-start.4 = (bf16[32,16,768]{2,1,0:T(8,128)(2,1)S(1)}, bf16[32,16,768]{2,1,0:T(8,128)(2,1)}, u32[]{:S(2)}, u32[]{:S(2)}) collective-permute-start(bf16[32,16,768]{2,1,0:T(8,128)(2,1)S(1)} %all-to-all-done.1.refs_0_), channel_id=1, source_target_pairs={{0,192},{64,128},{128,64},{192,0},{1,193},{65,129},{129,65},{193,1... | collective-permute-start | bytes 2359304 | tf_op jit(solution)/shard_map/ppermute | solution.py:49
  89.9 16.7 %collective-permute-start.11 = (bf16[512,768]{1,0:T(8,128)(2,1)}, bf16[512,768]{1,0:T(8,128)(2,1)}, u32[]{:S(2)}, u32[]{:S(2)}) collective-permute-start(bf16[512,768]{1,0:T(8,128)(2,1)} %get-tuple-element.87), channel_id=1, source_target_pairs={{0,2},{1,3},{2,0},{3,1},{4,6},{5,7},{6,4},{7,5},{8,10},{9,11},{10,... | collective-permute-start | bytes 2359304 | tf_op jit(solution)/shard_map/ppermute | solution.py:49
  98.6 31.6 %all-to-all-start.3 = ((bf16[8,64,768]{2,1,0:T(8,128)(2,1)}), bf16[8,64,768]{2,1,0:T(8,128)(2,1)S(1)}, u32[]{:S(2)}, u32[]{:S(2)}) async-start(bf16[8,64,768]{2,1,0:T(8,128)(2,1)} %bitcast.12), calls=%async_computation.3 | async-start | bytes 1572864 | tf_op jit(solution)/shard_map/all_to_all | solution.py:41
  105.3 22.5 %collective-permute-start.12 = (bf16[512,768]{1,0:T(8,128)(2,1)S(1)}, bf16[512,768]{1,0:T(8,128)(2,1)}, u32[]{:S(2)}, u32[]{:S(2)}) collective-permute-start(bf16[512,768]{1,0:T(8,128)(2,1)S(1)} %broadcast_select_fusion), channel_id=1, source_target_pairs={{0,2},{1,3},{2,0},{3,1},{4,6},{5,7},{6,4},{7,5},{8,10},{9,11},{10,... | collective-permute-start | bytes 2359304 | tf_op jit(solution)/shard_map/ppermute | solution.py:49
  106.6 30.2 %collective-permute-start.5 = (bf16[32,16,768]{2,1,0:T(8,128)(2,1)S(1)}, bf16[32,16,768]{2,1,0:T(8,128)(2,1)}, u32[]{:S(2)}, u32[]{:S(2)}) collective-permute-start(bf16[32,16,768]{2,1,0:T(8,128)(2,1)S(1)} %all-to-all-done.1.refs_0_), channel_id=1, source_target_pairs={{0,32},{32,0},{1,33},{33,1},{2,34},{34,2},{3,35},{35,3},{4,36},{36... | collective-permute-start | bytes 2359304 | tf_op jit(solution)/shard_map/ppermute | solution.py:49
  114.2 22.7 %collective-permute-start.6 = (bf16[32,16,768]{2,1,0:T(8,128)(2,1)}, bf16[32,16,768]{2,1,0:T(8,128)(2,1)}, u32[]{:S(2)}, u32[]{:S(2)}) collective-permute-start(bf16[32,16,768]{2,1,0:T(8,128)(2,1)} %collective-permute-done.2.refs_1_), channel_id=1, source_target_pairs={{0,32},{32,0},{1,33},{33,1},{2,34},{34,2},{3,35},{35,3},{4,36},{36... | collective-permute-start | bytes 2359304 | tf_op jit(solution)/shard_map/ppermute | solution.py:49
  118.0 18.9 %collective-permute-start.7 = (bf16[32,16,768]{2,1,0:T(8,128)(2,1)}, bf16[32,16,768]{2,1,0:T(8,128)(2,1)}, u32[]{:S(2)}, u32[]{:S(2)}) collective-permute-start(bf16[32,16,768]{2,1,0:T(8,128)(2,1)} %collective-permute-done.3.refs_2_), channel_id=1, source_target_pairs={{0,32},{32,0},{1,33},{33,1},{2,34},{34,2},{3,35},{35,3},{4,36},{36... | collective-permute-start | bytes 2359304 | tf_op jit(solution)/shard_map/ppermute | solution.py:49
  122.3 14.6 %collective-permute-start.8 = (bf16[32,16,768]{2,1,0:T(8,128)(2,1)}, bf16[32,16,768]{2,1,0:T(8,128)(2,1)}, u32[]{:S(2)}, u32[]{:S(2)}) collective-permute-start(bf16[32,16,768]{2,1,0:T(8,128)(2,1)} %collective-permute-done.4.refs_3_), channel_id=1, source_target_pairs={{0,32},{32,0},{1,33},{33,1},{2,34},{34,2},{3,35},{35,3},{4,36},{36... | collective-permute-start | bytes 2359304 | tf_op jit(solution)/shard_map/ppermute | solution.py:49
  130.2 12.3 %copy-start.3 = (bf16[8,64,768]{2,1,0:T(8,128)(2,1)}, bf16[8,64,768]{2,1,0:T(8,128)(2,1)S(1)}, u32[]{:S(2)}) copy-start(bf16[8,64,768]{2,1,0:T(8,128)(2,1)S(1)} %all-to-all-done.3) | copy-start | bytes 2359300
  130.2 30.2 %all-to-all-start.4 = ((bf16[8,64,768]{2,1,0:T(8,128)(2,1)}), bf16[8,64,768]{2,1,0:T(8,128)(2,1)S(1)}, u32[]{:S(2)}, u32[]{:S(2)}) async-start(bf16[8,64,768]{2,1,0:T(8,128)(2,1)} %bitcast.186), calls=%async_computation.4 | async-start | bytes 1572864 | tf_op jit(solution)/shard_map/all_to_all | solution.py:41
  142.5 9.4 %slice-start = ((s8[6291456]{0:T(1024)(128)(4,1)}), s8[4194304]{0:T(1024)(128)(4,1)S(1)}, s32[]{:S(2)}) async-start(s8[6291456]{0:T(1024)(128)(4,1)} %bitcast.184), calls=%async_computation.10 | async-start | bytes 8388608
  145.5 0.9 copy-start.2
  145.6 6.4 %slice-start.1 = ((s8[6291456]{0:T(1024)(128)(4,1)}), s8[2097152]{0:T(1024)(128)(4,1)S(1)}, s32[]{:S(2)}) async-start(s8[6291456]{0:T(1024)(128)(4,1)} %bitcast.184), calls=%async_computation.11 | async-start | bytes 4194304
  153.8 11.3 %copy-start.20 = (bf16[32,8,256]{2,1,0:T(8,128)(2,1)S(1)}, bf16[32,8,256]{2,1,0:T(8,128)(2,1)}, u32[]{:S(2)}) copy-start(bf16[32,8,256]{2,1,0:T(8,128)(2,1)} %get-tuple-element.101) | copy-start | bytes 393220
  161.3 25.2 %all-to-all-start.5 = ((bf16[8,64,768]{2,1,0:T(8,128)(2,1)}), bf16[8,64,768]{2,1,0:T(8,128)(2,1)S(1)}, u32[]{:S(2)}, u32[]{:S(2)}) async-start(bf16[8,64,768]{2,1,0:T(8,128)(2,1)} %bitcast.43), calls=%async_computation.5 | async-start | bytes 1572864 | tf_op jit(solution)/shard_map/all_to_all | solution.py:41
  167.4 3.7 %copy-start.16 = (bf16[32,4,2,8,768]{4,3,2,1,0:T(8,128)(2,1)}, bf16[32,4,2,8,768]{4,3,2,1,0:T(8,128)(2,1)S(1)}, u32[]{:S(2)}) copy-start(bf16[32,4,2,8,768]{4,3,2,1,0:T(8,128)(2,1)S(1)} %copy.40) | copy-start | bytes 9437188
  171.1 1.1 copy-start.4
  171.1 1.4 copy-start.6
  171.2 1.4 copy-start.7
  186.6 0.9 copy-start.8
  187.5 1.0 copy-start.10
  188.5 0.9 copy-start.12
  194.3 5.8 %collective-permute-start.17 = (bf16[4,4,128,384]{3,2,1,0:T(8,128)(2,1)}, bf16[4,4,128,384]{3,2,1,0:T(8,128)(2,1)S(1)}, u32[]{:S(2)}, u32[]{:S(2)}) collective-permute-start(bf16[4,4,128,384]{3,2,1,0:T(8,128)(2,1)} %get-tuple-element.68), channel_id=1, source_target_pairs={{0,32},{32,0},{1,33},{33,1},{2,34},{34,2},{3,35},{35,3},{4,36},{36... | collective-permute-start | bytes 4718600 | tf_op jit(solution)/shard_map/ppermute | solution.py:49
  194.9 5.3 %copy-start.17 = (bf16[4,4,128,384]{3,2,1,0:T(8,128)(2,1)S(1)}, bf16[4,4,128,384]{3,2,1,0:T(8,128)(2,1)}, u32[]{:S(2)}) copy-start(bf16[4,4,128,384]{3,2,1,0:T(8,128)(2,1)} %get-tuple-element.67) | copy-start | bytes 4718596
  200.2 5.5 %collective-permute-start.13 = (bf16[4,768,256]{2,1,0:T(8,128)(2,1)}, bf16[4,768,256]{2,1,0:T(8,128)(2,1)}, u32[]{:S(2)}, u32[]{:S(2)}) collective-permute-start(bf16[4,768,256]{2,1,0:T(8,128)(2,1)} %get-tuple-element.66), channel_id=1, source_target_pairs={{0,32},{32,0},{1,33},{33,1},{2,34},{34,2},{3,35},{35,3},{4,36},{36... | collective-permute-start | bytes 4718600 | tf_op jit(solution)/shard_map/ppermute | solution.py:49
  201.8 23.8 %all-to-all-start.6 = ((bf16[4,4,128,384]{3,2,1,0:T(8,128)(2,1)}), bf16[4,4,128,384]{3,2,1,0:T(8,128)(2,1)S(1)}, u32[]{:S(2)}, u32[]{:S(2)}) async-start(bf16[4,4,128,384]{3,2,1,0:T(8,128)(2,1)} %add_convert_fusion), calls=%async_computation.6 | async-start | bytes 3145728 | tf_op jit(solution)/shard_map/all_to_all | solution.py:41
  208.4 20.6 %copy-start.18 = (bf16[768,256]{1,0:T(8,128)(2,1)S(1)}, bf16[768,256]{1,0:T(8,128)(2,1)}, u32[]{:S(2)}) copy-start(bf16[768,256]{1,0:T(8,128)(2,1)} %get-tuple-element.69) | copy-start | bytes 1179652
  208.4 18.2 %collective-permute-start.14 = (bf16[768,256]{1,0:T(8,128)(2,1)}, bf16[768,256]{1,0:T(8,128)(2,1)S(1)}, u32[]{:S(2)}, u32[]{:S(2)}) collective-permute-start(bf16[768,256]{1,0:T(8,128)(2,1)} %get-tuple-element.83), channel_id=1, source_target_pairs={{0,64},{64,0},{128,192},{192,128},{1,65},{65,1},{129,193},{193,129... | collective-permute-start | bytes 1179656 | tf_op jit(solution)/shard_map/ppermute | solution.py:49
  208.4 18.2 %collective-permute-start.15 = (bf16[768,256]{1,0:T(8,128)(2,1)}, bf16[768,256]{1,0:T(8,128)(2,1)S(1)}, u32[]{:S(2)}, u32[]{:S(2)}) collective-permute-start(bf16[768,256]{1,0:T(8,128)(2,1)} %get-tuple-element.82), channel_id=1, source_target_pairs={{0,128},{64,192},{128,0},{192,64},{1,129},{65,193},{129,1},{193,65... | collective-permute-start | bytes 1179656 | tf_op jit(solution)/shard_map/ppermute | solution.py:49
  208.5 20.5 %collective-permute-start.16 = (bf16[768,256]{1,0:T(8,128)(2,1)}, bf16[768,256]{1,0:T(8,128)(2,1)S(1)}, u32[]{:S(2)}, u32[]{:S(2)}) collective-permute-start(bf16[768,256]{1,0:T(8,128)(2,1)} %get-tuple-element.81), channel_id=1, source_target_pairs={{0,192},{64,128},{128,64},{192,0},{1,193},{65,129},{129,65},{193,1... | collective-permute-start | bytes 1179656 | tf_op jit(solution)/shard_map/ppermute | solution.py:49
  229.2 7.6 %collective-permute-start.18 = (bf16[8,24,256]{2,1,0:T(8,128)(2,1)S(1)}, bf16[8,24,256]{2,1,0:T(8,128)(2,1)S(1)}, u32[]{:S(2)}, u32[]{:S(2)}) collective-permute-start(bf16[8,24,256]{2,1,0:T(8,128)(2,1)S(1)} %get-tuple-element.93), channel_id=1, source_target_pairs={{0,1},{1,0},{2,3},{3,2},{4,5},{5,4},{6,7},{7,6},{8,9},{9,8},{10,11... | collective-permute-start | bytes 294920 | tf_op jit(solution)/shard_map/ppermute | solution.py:49
  230.5 6.3 %collective-permute-start.19 = (bf16[8,24,256]{2,1,0:T(8,128)(2,1)S(1)}, bf16[8,24,256]{2,1,0:T(8,128)(2,1)S(1)}, u32[]{:S(2)}, u32[]{:S(2)}) collective-permute-start(bf16[8,24,256]{2,1,0:T(8,128)(2,1)S(1)} %get-tuple-element.95), channel_id=1, source_target_pairs={{0,2},{1,3},{2,0},{3,1},{4,6},{5,7},{6,4},{7,5},{8,10},{9,11},{10,... | collective-permute-start | bytes 294920 | tf_op jit(solution)/shard_map/ppermute | solution.py:49
  232.9 32.1 %copy-start.14 = (f32[128,1]{1,0:T(8,128)S(1)}, f32[128,1]{1,0:T(8,128)}, u32[]{:S(2)}) copy-start(f32[128,1]{1,0:T(8,128)} %copy-done.13) | copy-start | bytes 1540
  232.9 4.7 %collective-permute-start.20 = (bf16[8,24,256]{2,1,0:T(8,128)(2,1)S(1)}, bf16[8,24,256]{2,1,0:T(8,128)(2,1)S(1)}, u32[]{:S(2)}, u32[]{:S(2)}) collective-permute-start(bf16[8,24,256]{2,1,0:T(8,128)(2,1)S(1)} %get-tuple-element.94), channel_id=1, source_target_pairs={{0,3},{1,2},{2,1},{3,0},{4,7},{5,6},{6,5},{7,4},{8,11},{9,10},{10,... | collective-permute-start | bytes 294920 | tf_op jit(solution)/shard_map/ppermute | solution.py:49
  233.1 9.9 %all-to-all-start.7 = ((bf16[4,128,384]{2,1,0:T(8,128)(2,1)}), bf16[4,128,384]{2,1,0:T(8,128)(2,1)S(1)}, u32[]{:S(2)}, u32[]{:S(2)}) async-start(bf16[4,128,384]{2,1,0:T(8,128)(2,1)} %fusion.19), calls=%async_computation.7 | async-start | bytes 786432 | tf_op jit(solution)/shard_map/all_to_all | solution.py:41
  256.1 14.7 %all-to-all-start.9 = ((bf16[8,96,128]{2,1,0:T(8,128)(2,1)}), bf16[8,96,128]{2,1,0:T(8,128)(2,1)S(1)}, u32[]{:S(2)}, u32[]{:S(2)}) async-start(bf16[8,96,128]{2,1,0:T(8,128)(2,1)} %broadcast_in_dim.119), calls=%async_computation.9 | async-start | bytes 393216 | tf_op jit(solution)/shard_map/all_to_all | solution.py:41
  270.9 0.9 copy-start.1
  (6 other events, 4.4 us)

commit v8 on v7

--- a/solution.py
+++ b/solution.py
@@ -11,6 +11,7 @@
 GRP, SHARD = X * CORE, Z * Y
 PAIRS = SHARD // 2
 CHUNKS = 4
+LANES = 128
 VMEM = 50 * 1024 * 1024
 
 
@@ -103,10 +104,10 @@
 
 
 def early_kernel(scale, embedded_ref, positives_ref, query_ref, *refs):
-    row_refs, (stats_ref, sum_ref) = refs[: CHUNKS - 1], refs[CHUNKS - 1 :]
+    row_refs, out_ref = refs[: CHUNKS - 1], refs[CHUNKS - 1]
     embedded = embedded_ref[...]
     positives = positives_ref[...].astype(jnp.float32)
-    q_dev = embedded.shape[0]
+    q_dev, width = embedded.shape
     pos_scores = (
         jnp.sum(embedded.astype(jnp.float32) * positives, axis=1, keepdims=True) * scale
     )
@@ -121,25 +122,24 @@
         scores.append(score)
         members.append(member)
     total = jnp.exp(pos_scores - largest)
-    grad = jnp.zeros(sum_ref.shape, jnp.float32)
+    grad = jnp.zeros((q_dev, width), jnp.float32)
     for c in range(CHUNKS - 1):
         weight = jnp.where(members[c], jnp.exp(scores[c] - largest), 0.0)
         total = total + jnp.sum(weight, axis=1, keepdims=True)
         grad = grad + weighted_rows(weight, row_refs[c][...])
-    stats_ref[0] = pos_scores
-    stats_ref[1] = largest
-    stats_ref[2] = total
-    sum_ref[...] = grad
+    lane = lax.broadcasted_iota(jnp.int32, (q_dev, LANES), 1)
+    out_ref[:, :width] = grad
+    out_ref[:, width:] = jnp.where(lane == 0, pos_scores, jnp.where(lane == 1, largest, total))
 
 
 def score_kernel(
-    scale, place_ref, embedded_ref, positives_ref, hidden_ref, query_ref, stats_ref, sum_ref,
+    scale, place_ref, embedded_ref, positives_ref, hidden_ref, query_ref, early_ref,
     rows_ref, loss_ref, grad_ref, keep_ref, send_ref,
 ):
     embedded = embedded_ref[...]
     positives = positives_ref[...].astype(jnp.float32)
     q_dev, width = embedded.shape
-    pos_scores, early, total = stats_ref[0], stats_ref[1], stats_ref[2]
+    pos_scores, early, total = (early_ref[:, width + i : width + i + 1] for i in range(3))
     rows = rows_ref[...]
     per = rows.shape[0]
     score = contract_last(embedded, rows) * scale
@@ -154,7 +154,7 @@
     log_total = largest + jnp.log(total)
     loss_ref[...] = log_total - pos_scores
     grad = (jnp.exp(pos_scores - log_total) - 1.0) * positives
-    grad = grad + jnp.exp(early - log_total) * sum_ref[...]
+    grad = grad + jnp.exp(early - log_total) * early_ref[:, :width]
     grad = grad + weighted_rows(late * (1.0 / total), rows)
     query_grad = (grad * scale).astype(jnp.bfloat16)
     grad_ref[...] = query_grad
@@ -293,12 +293,9 @@
 
     half = width // CORE
     outer_cut = jax.ShapeDtypeStruct((Y, X, hid // Y // X, half), jnp.bfloat16)
-    stats, early_sum = pl.pallas_call(
+    early = pl.pallas_call(
         functools.partial(early_kernel, scale),
-        out_shape=[
-            jax.ShapeDtypeStruct((3, q_dev, 1), jnp.float32),
-            jax.ShapeDtypeStruct((q_dev, width), jnp.float32),
-        ],
+        out_shape=jax.ShapeDtypeStruct((q_dev, width + LANES), jnp.float32),
         **limits,
     )(embedded, positives, slot_query, *chunks[:-1])
     losses, query_grad, outer, outer_sent = pl.pallas_call(
@@ -309,9 +306,9 @@
             outer_cut,
             outer_cut,
         ],
-        in_specs=[in_smem] + [in_vmem] * 7,
-        **limits,
-    )(place, embedded, positives, hidden, slot_query, stats, early_sum, chunks[-1])
+        in_specs=[in_smem] + [in_vmem] * 6,
+        **limits,
+    )(place, embedded, positives, hidden, slot_query, early, chunks[-1])
     outer_sent = swap(outer_sent, "core", 1)
     inner, inner_sent = pl.pallas_call(
         inner_kernel,

time: 273 us -> 272 us (level)
    unnamed x55 -> x49, local copies, waits for them, and re-layouts: 8.17 us -> 6.6 us
  transfers between devices with their start and end apart: 30 -> 30, of which waited for: 12 -> 12; matrix products, arithmetic and copies ran while one was open for 23% -> 24% of each run, Pallas kernels for 5% -> 5%
where the time goes in v8:
time: 272 us; the launch traced here: 270 us
  starting transfers between devices  89.6 us (33%)
  waiting for transfers between devices  65.9 us (24%)
  local copies, waits for them, and re-layouts  51.4 us (19%)
  other arithmetic  23.3 us (9%)
  Pallas kernels  18.8 us (7%)
  blocking collectives  12.3 us (5%)
  matrix products  7.91 us (3%)
    all_to_all x9, starting transfers between devices, exchange(): return lax.all_to_all(value, axes, split_axis=0, concat_axis=0, tiled=True)  56.1 us
    all_to_all x9, waiting for transfers between devices, exchange(): return lax.all_to_all(value, axes, split_axis=0, concat_axis=0, tiled=True)  49.3 us
    gather x4, local copies, waits for them, and re-layouts, find(): passage_table.at[ids].get(mode='promise_in_bounds')  33.6 us
    ppermute x21, starting transfers between devices, swap(): lax.ppermute(value, axis, [(i, i ^ by) for i in range(lax.axis_size(axis))])  33.5 us
    ppermute x21, waiting for transfers between devices, swap(): lax.ppermute(value, axis, [(i, i ^ by) for i in range(lax.axis_size(axis))])  16.5 us
    all_to_all x1, blocking collectives, exchange(): return lax.all_to_all(value, axes, split_axis=0, concat_axis=0, tiled=True)  12.3 us
    dot_general x8, matrix products, shards(): jnp.dot(queries, part, preferred_element_type=jnp.float32)  7.3 us
    select_n x4, other arithmetic, find(): jnp.where(own[by, :, cuts[part]].reshape(-1, 1), found[i], jnp.zeros((),...  7.04 us
  transfers between devices with their start and end apart: 30, of which 12 were waited for; matrix products, arithmetic and copies ran while one was open for 24% of the time, Pallas kernels for 5%

profile of v8, /device:TPU:1, one launch (start us, length us, event | category | flops | bytes accessed | tf_op | source)
XLA Modules:
  0.0 270.4 jit_solution(2385902551915731822)
XLA Ops:
  1.4 1.9 shard_map.85
  3.3 12.0 %all-to-all-start = ((s32[32,1,128]{2,1,0:T(1,128)}), s32[32,1,128]{2,1,0:T(1,128)S(1)}, u32[]{:S(2)}, u32[]{:S(2)}) async-start(s32[32,1,128]{2,1,0:T(1,128)} %bitcast.4), calls=%async_computation | async-start | bytes 32768 | tf_op jit(solution)/shard_map/all_to_all | solution.py:42
  16.1 7.7 %all-to-all-done = s32[32,1,128]{2,1,0:T(1,128)S(1)} async-done(((s32[32,1,128]{2,1,0:T(1,128)}), s32[32,1,128]{2,1,0:T(1,128)S(1)}, u32[]{:S(2)}, u32[]{:S(2)}) %all-to-all-start) | async-done | bytes 16416 | tf_op jit(solution)/shard_map/all_to_all | solution.py:42
  24.3 8.1 %gather_fusion = bf16[1024,768]{1,0:T(8,128)(2,1)S(1)} fusion(bf16[4096,768]{1,0:T(8,128)(2,1)} %param.9, s32[1024]{0:T(1024)S(1)} %fusion.40), kind=kCustom, calls=%fused_computation | custom fusion | bytes 3149824 | tf_op jit(solution)/shard_map/gather | solution.py:237
  34.5 3.9 %all-to-all-start.1 = ((bf16[32,16,768]{2,1,0:T(8,128)(2,1)}), bf16[32,16,768]{2,1,0:T(8,128)(2,1)S(1)}, u32[]{:S(2)}, u32[]{:S(2)}) async-start(bf16[32,16,768]{2,1,0:T(8,128)(2,1)} %broadcast_in_dim.100), calls=%async_computation.1 | async-start | bytes 1572864 | tf_op jit(solution)/shard_map/all_to_all | solution.py:42
  39.7 1.8 collective-permute-start.1
  41.5 10.3 %gather_fusion.1 = bf16[1536,768]{1,0:T(8,128)(2,1)} fusion(bf16[4096,768]{1,0:T(8,128)(2,1)} %param.9, s32[2048]{0:T(1024)S(1)} %pad_clamp_fusion), kind=kCustom, calls=%fused_computation.1 | custom fusion | bytes 4724736 | tf_op jit(solution)/shard_map/gather | solution.py:237
  52.0 2.7 %slice_select_fusion.3 = (bf16[512,768]{1,0:T(8,128)(2,1)}, bf16[512,768]{1,0:T(8,128)(2,1)}) fusion(bf16[1536,768]{1,0:T(8,128)(2,1)} %gather_fusion.1, pred[512]{0:T(512)(128)(4,1)S(1)} %broadcast_in_dim.106, pred[512]{0:T(512)(128)(4,1)S(1)} %broadcast_in_dim.104), kind=kLoop, calls=%fused_computation.35 | loop fusion | flops 786432 | bytes 3146752 | tf_op jit(solution)/shard_map/jit(_where)/select_n | solution.py:239
  55.7 8.0 %collective-permute-done = bf16[512,768]{1,0:T(8,128)(2,1)S(1)} collective-permute-done((bf16[512,768]{1,0:T(8,128)(2,1)}, bf16[512,768]{1,0:T(8,128)(2,1)S(1)}, u32[]{:S(2)}, u32[]{:S(2)}) %collective-permute-start) | collective-permute-done | bytes 786464 | tf_op jit(solution)/shard_map/ppermute | solution.py:50
  63.8 2.2 fusion.14
  66.7 6.8 %all-to-all-start.2 = ((bf16[8,64,768]{2,1,0:T(8,128)(2,1)}), bf16[8,64,768]{2,1,0:T(8,128)(2,1)S(1)}, u32[]{:S(2)}, u32[]{:S(2)}) async-start(bf16[8,64,768]{2,1,0:T(8,128)(2,1)} %bitcast.10), calls=%async_computation.2 | async-start | bytes 1572864 | tf_op jit(solution)/shard_map/all_to_all | solution.py:42
  73.9 9.2 %gather_fusion.2 = bf16[1024,768]{1,0:T(8,128)(2,1)} fusion(bf16[4096,768]{1,0:T(8,128)(2,1)} %param.9, s32[1024]{0:T(1024)S(1)} %fusion.41), kind=kCustom, calls=%fused_computation.2 | custom fusion | bytes 3149824 | tf_op jit(solution)/shard_map/gather | solution.py:237
  84.3 2.4 collective-permute-start.3
  86.9 3.0 %slice_select_fusion = (bf16[512,768]{1,0:T(8,128)(2,1)}, bf16[512,768]{1,0:T(8,128)(2,1)}) fusion(bf16[1024,768]{1,0:T(8,128)(2,1)} %gather_fusion.2, pred[512]{0:T(512)(128)(4,1)S(1)} %broadcast_in_dim.115, bf16[512,768]{1,0:T(8,128)(2,1)} %collective-permute-done.9, pred[512]{0:T(512)(128)(4,1)S(1)} %broadcast_in_dim.110), kind=kLoop, calls=%fused_computation.31 | loop fusion | flops 1179648 | bytes 3933184 | tf_op jit(solution)/shard_map/jit(_where)/select_n | solution.py:239
  90.0 2.5 collective-permute-start.11
  92.5 6.0 %gather_fusion.3 = bf16[512,768]{1,0:T(8,128)(2,1)S(1)} fusion(bf16[4096,768]{1,0:T(8,128)(2,1)} %param.9, s32[1024]{0:T(1024)S(1)} %pad_clamp_fusion.1), kind=kCustom, calls=%fused_computation.3 | custom fusion | bytes 1574912 | tf_op jit(solution)/shard_map/gather | solution.py:237
  98.7 6.7 %all-to-all-start.3 = ((bf16[8,64,768]{2,1,0:T(8,128)(2,1)}), bf16[8,64,768]{2,1,0:T(8,128)(2,1)S(1)}, u32[]{:S(2)}, u32[]{:S(2)}) async-start(bf16[8,64,768]{2,1,0:T(8,128)(2,1)} %bitcast.12), calls=%async_computation.3 | async-start | bytes 1572864 | tf_op jit(solution)/shard_map/all_to_all | solution.py:42
  106.7 7.5 %collective-permute-start.5 = (bf16[32,16,768]{2,1,0:T(8,128)(2,1)S(1)}, bf16[32,16,768]{2,1,0:T(8,128)(2,1)}, u32[]{:S(2)}, u32[]{:S(2)}) collective-permute-start(bf16[32,16,768]{2,1,0:T(8,128)(2,1)S(1)} %all-to-all-done.1.refs_0_), channel_id=1, source_target_pairs={{0,32},{32,0},{1,33},{33,1},{2,34},{34,2},{3,35},{35,3},{4,36},{36... | collective-permute-start | bytes 2359304 | tf_op jit(solution)/shard_map/ppermute | solution.py:50
  114.2 3.8 %collective-permute-done.3.refs_2_ = bf16[32,16,768]{2,1,0:T(8,128)(2,1)} collective-permute-done((bf16[32,16,768]{2,1,0:T(8,128)(2,1)S(1)}, bf16[32,16,768]{2,1,0:T(8,128)(2,1)}, u32[]{:S(2)}, u32[]{:S(2)}) %collective-permute-start.3) | collective-permute-done | bytes 786464 | tf_op jit(solution)/shard_map/ppermute | solution.py:50
  118.0 4.3 %collective-permute-start.7 = (bf16[32,16,768]{2,1,0:T(8,128)(2,1)}, bf16[32,16,768]{2,1,0:T(8,128)(2,1)}, u32[]{:S(2)}, u32[]{:S(2)}) collective-permute-start(bf16[32,16,768]{2,1,0:T(8,128)(2,1)} %collective-permute-done.3.refs_2_), channel_id=1, source_target_pairs={{0,32},{32,0},{1,33},{33,1},{2,34},{34,2},{3,35},{35,3},{4,36},{36... | collective-permute-start | bytes 2359304 | tf_op jit(solution)/shard_map/ppermute | solution.py:50
  122.3 2.6 collective-permute-start.8
  125.4 2.4 add.186
  127.8 2.5 add.187
  130.3 6.6 %all-to-all-start.4 = ((bf16[8,64,768]{2,1,0:T(8,128)(2,1)}), bf16[8,64,768]{2,1,0:T(8,128)(2,1)S(1)}, u32[]{:S(2)}, u32[]{:S(2)}) async-start(bf16[8,64,768]{2,1,0:T(8,128)(2,1)} %bitcast.186), calls=%async_computation.4 | async-start | bytes 1572864 | tf_op jit(solution)/shard_map/all_to_all | solution.py:42
  137.0 5.6 %shard_map.86 = bf16[4,2,32,16,768]{4,3,2,1,0:T(8,128)(2,1)} custom-call(s32[2]{0:T(128)S(1)} %pad_add_fusion.4.place_ref, bf16[32,16,768]{2,1,0:T(8,128)(2,1)S(1)} %all-to-all-done.1.refs_0_, bf16[32,16,768]{2,1,0:T(8,128)(2,1)} %collective-permute-done.2.refs_1_, bf16[32,16,768]{2,1,0:T(8,128)(2,1)} %collective-permute-done.3.refs_2_, ...), custom_call_target="tpu_custom_call" | custom-call | tf_op jit(solution)/shard_map/pallas_call | solution.py:268
  142.6 2.2 slice_bitcast_fusion.1
  152.0 1.9 slice_bitcast_fusion
  153.9 6.6 %all-to-all-done.4 = bf16[8,64,768]{2,1,0:T(8,128)(2,1)S(1)} async-done(((bf16[8,64,768]{2,1,0:T(8,128)(2,1)}), bf16[8,64,768]{2,1,0:T(8,128)(2,1)S(1)}, u32[]{:S(2)}, u32[]{:S(2)}) %all-to-all-start.4) | async-done | bytes 786464 | tf_op jit(solution)/shard_map/all_to_all | solution.py:42
  161.4 3.8 %all-to-all-start.5 = ((bf16[8,64,768]{2,1,0:T(8,128)(2,1)}), bf16[8,64,768]{2,1,0:T(8,128)(2,1)S(1)}, u32[]{:S(2)}, u32[]{:S(2)}) async-start(bf16[8,64,768]{2,1,0:T(8,128)(2,1)} %bitcast.43), calls=%async_computation.5 | async-start | bytes 1572864 | tf_op jit(solution)/shard_map/all_to_all | solution.py:42
  165.2 2.3 copy.40
  169.5 1.7 fusion.12
  172.6 2.3 shard_map.87.early_ref
  175.7 10.9 %all-to-all-done.5 = bf16[8,64,768]{2,1,0:T(8,128)(2,1)S(1)} async-done(((bf16[8,64,768]{2,1,0:T(8,128)(2,1)}), bf16[8,64,768]{2,1,0:T(8,128)(2,1)S(1)}, u32[]{:S(2)}, u32[]{:S(2)}) %all-to-all-start.5) | async-done | bytes 786464 | tf_op jit(solution)/shard_map/all_to_all | solution.py:42
  188.6 3.8 %shard_map.88 = (f32[128,1]{1,0:T(8,128)S(1)}, bf16[128,768]{1,0:T(8,128)(2,1)S(1)}, bf16[4,4,128,384]{3,2,1,0:T(8,128)(2,1)S(1)}, bf16[4,4,128,384]{3,2,1,0:T(8,128)(2,1)}) custom-call(s32[2]{0:T(128)S(1)} %pad_add_fusion.4.place_ref, bf16[128,768]{1,0:T(8,128)(2,1)S(1)} %fusion.embedded_ref, bf16[128,768]{1,0:T(8,128)(2,1)S(1)} %copy-done.10, ...), custom_call_target="tpu_custom_call" | custom-call | tf_op jit(solution)/shard_map/pallas_call | solution.py:301
  193.5 5.2 %shard_map.89 = (bf16[4,768,256]{2,1,0:T(8,128)(2,1)S(1)}, bf16[4,768,256]{2,1,0:T(8,128)(2,1)}) custom-call(s32[2]{0:T(128)S(1)} %pad_add_fusion.4.place_ref, bf16[128,768]{1,0:T(8,128)(2,1)S(1)} %copy-done.2, bf16[128,768]{1,0:T(8,128)(2,1)S(1)} %get-tuple-element.60.grad_ref, f32[128,2048]{1,0:T(8,128)S(1)} %get-tuple-element.87.slope_ref, ...), custom_call_target="tpu_custom_call" | custom-call | tf_op jit(solution)/shard_map/pallas_call | solution.py:313
  198.7 1.6 add_convert_fusion
  200.4 3.8 %all-to-all-start.6 = ((bf16[4,4,128,384]{3,2,1,0:T(8,128)(2,1)}), bf16[4,4,128,384]{3,2,1,0:T(8,128)(2,1)S(1)}, u32[]{:S(2)}, u32[]{:S(2)}) async-start(bf16[4,4,128,384]{3,2,1,0:T(8,128)(2,1)} %add_convert_fusion), calls=%async_computation.6 | async-start | bytes 3145728 | tf_op jit(solution)/shard_map/all_to_all | solution.py:42
  204.2 2.7 %fusion.18 = (bf16[768,256]{1,0:T(8,128)(2,1)}, bf16[768,256]{1,0:T(8,128)(2,1)}, bf16[768,256]{1,0:T(8,128)(2,1)}, bf16[768,256]{1,0:T(8,128)(2,1)}) fusion(bf16[4,768,256]{2,1,0:T(8,128)(2,1)} %collective-permute-done.13, bf16[4,768,256]{2,1,0:T(8,128)(2,1)S(1)} %get-tuple-element.61), kind=kLoop, calls=%fused_computation.64 | loop fusion | flops 3145728 | bytes 4718592 | tf_op jit(solution)/shard_map/convert_element_type | solution.py:321
  207.0 3.8 %collective-permute-start.16 = (bf16[768,256]{1,0:T(8,128)(2,1)}, bf16[768,256]{1,0:T(8,128)(2,1)S(1)}, u32[]{:S(2)}, u32[]{:S(2)}) collective-permute-start(bf16[768,256]{1,0:T(8,128)(2,1)} %get-tuple-element.77), channel_id=1, source_target_pairs={{0,192},{64,128},{128,64},{192,0},{1,193},{65,129},{129,65},{193,1... | collective-permute-start | bytes 1179656 | tf_op jit(solution)/shard_map/ppermute | solution.py:50
  210.8 13.4 %all-to-all-done.6 = bf16[4,4,128,384]{3,2,1,0:T(8,128)(2,1)S(1)} async-done(((bf16[4,4,128,384]{3,2,1,0:T(8,128)(2,1)}), bf16[4,4,128,384]{3,2,1,0:T(8,128)(2,1)S(1)}, u32[]{:S(2)}, u32[]{:S(2)}) %all-to-all-start.6) | async-done | bytes 1572896 | tf_op jit(solution)/shard_map/all_to_all | solution.py:42
  225.1 2.4 collective-permute-done.16
  227.7 1.3 collective-permute-start.18
  229.0 2.4 collective-permute-start.19
  231.7 3.7 %all-to-all-start.7 = ((bf16[4,128,384]{2,1,0:T(8,128)(2,1)}), bf16[4,128,384]{2,1,0:T(8,128)(2,1)S(1)}, u32[]{:S(2)}, u32[]{:S(2)}) async-start(bf16[4,128,384]{2,1,0:T(8,128)(2,1)} %fusion.19), calls=%async_computation.7 | async-start | bytes 786432 | tf_op jit(solution)/shard_map/all_to_all | solution.py:42
  236.2 5.4 %all-to-all-done.7 = bf16[4,128,384]{2,1,0:T(8,128)(2,1)S(1)} async-done(((bf16[4,128,384]{2,1,0:T(8,128)(2,1)}), bf16[4,128,384]{2,1,0:T(8,128)(2,1)S(1)}, u32[]{:S(2)}, u32[]{:S(2)}) %all-to-all-start.7) | async-done | bytes 393248 | tf_op jit(solution)/shard_map/all_to_all | solution.py:42
  241.7 12.3 %all_to_all.78 = bf16[8,96,128]{2,1,0:T(8,128)(2,1)S(1)} all-to-all(bf16[8,96,128]{2,1,0:T(8,128)(2,1)S(1)} %constant_dynamic-update-slice_fusion.4), channel_id=1, replica_groups=mesh['x'=4,'core'=2,'z'=8,'y'=4] {'z'}, dimensions={0} | all-to-all | bytes 393216 | tf_op jit(solution)/shard_map/all_to_all | solution.py:42
  254.7 8.8 %all-to-all-start.9 = ((bf16[8,96,128]{2,1,0:T(8,128)(2,1)}), bf16[8,96,128]{2,1,0:T(8,128)(2,1)S(1)}, u32[]{:S(2)}, u32[]{:S(2)}) async-start(bf16[8,96,128]{2,1,0:T(8,128)(2,1)} %broadcast_in_dim.119), calls=%async_computation.9 | async-start | bytes 393216 | tf_op jit(solution)/shard_map/all_to_all | solution.py:42
  264.1 5.3 %all-to-all-done.9 = bf16[8,96,128]{2,1,0:T(8,128)(2,1)S(1)} async-done(((bf16[8,96,128]{2,1,0:T(8,128)(2,1)}), bf16[8,96,128]{2,1,0:T(8,128)(2,1)S(1)}, u32[]{:S(2)}, u32[]{:S(2)}) %all-to-all-start.9) | async-done | bytes 196640 | tf_op jit(solution)/shard_map/all_to_all | solution.py:42
  (172 shorter events, 31.1 us)
Async XLA Ops:
  0.6 14.7 %copy-start = (bf16[64,768]{1,0:T(8,128)(2,1)S(1)}, bf16[64,768]{1,0:T(8,128)(2,1)}, u32[]{:S(2)}) copy-start(bf16[64,768]{1,0:T(8,128)(2,1)} %param.11) | copy-start | bytes 294916
  3.3 20.6 %all-to-all-start = ((s32[32,1,128]{2,1,0:T(1,128)}), s32[32,1,128]{2,1,0:T(1,128)S(1)}, u32[]{:S(2)}, u32[]{:S(2)}) async-start(s32[32,1,128]{2,1,0:T(1,128)} %bitcast.4), calls=%async_computation | async-start | bytes 32768 | tf_op jit(solution)/shard_map/all_to_all | solution.py:42
  34.5 32.2 %all-to-all-start.1 = ((bf16[32,16,768]{2,1,0:T(8,128)(2,1)}), bf16[32,16,768]{2,1,0:T(8,128)(2,1)S(1)}, u32[]{:S(2)}, u32[]{:S(2)}) async-start(bf16[32,16,768]{2,1,0:T(8,128)(2,1)} %broadcast_in_dim.100), calls=%async_computation.1 | async-start | bytes 1572864 | tf_op jit(solution)/shard_map/all_to_all | solution.py:42
  38.4 25.4 %collective-permute-start = (bf16[512,768]{1,0:T(8,128)(2,1)}, bf16[512,768]{1,0:T(8,128)(2,1)S(1)}, u32[]{:S(2)}, u32[]{:S(2)}) collective-permute-start(bf16[512,768]{1,0:T(8,128)(2,1)} %get-tuple-element.86), channel_id=1, source_target_pairs={{0,1},{1,0},{2,3},{3,2},{4,5},{5,4},{6,7},{7,6},{8,9},{9,8},{10,11... | collective-permute-start | bytes 2359304 | tf_op jit(solution)/shard_map/ppermute | solution.py:50
  39.7 27.0 %collective-permute-start.1 = (bf16[512,768]{1,0:T(8,128)(2,1)S(1)}, bf16[512,768]{1,0:T(8,128)(2,1)S(1)}, u32[]{:S(2)}, u32[]{:S(2)}) collective-permute-start(bf16[512,768]{1,0:T(8,128)(2,1)S(1)} %get-tuple-element.85), channel_id=1, source_target_pairs={{0,3},{1,2},{2,1},{3,0},{4,7},{5,6},{6,5},{7,4},{8,11},{9,10},{10,... | collective-permute-start | bytes 2359304 | tf_op jit(solution)/shard_map/ppermute | solution.py:50
  54.7 32.2 %collective-permute-start.9 = (bf16[512,768]{1,0:T(8,128)(2,1)}, bf16[512,768]{1,0:T(8,128)(2,1)}, u32[]{:S(2)}, u32[]{:S(2)}) collective-permute-start(bf16[512,768]{1,0:T(8,128)(2,1)} %get-tuple-element.82), channel_id=1, source_target_pairs={{0,1},{1,0},{2,3},{3,2},{4,5},{5,4},{6,7},{7,6},{8,9},{9,8},{10,11... | collective-permute-start | bytes 2359304 | tf_op jit(solution)/shard_map/ppermute | solution.py:50
  55.1 37.4 %collective-permute-start.10 = (bf16[512,768]{1,0:T(8,128)(2,1)}, bf16[512,768]{1,0:T(8,128)(2,1)}, u32[]{:S(2)}, u32[]{:S(2)}) collective-permute-start(bf16[512,768]{1,0:T(8,128)(2,1)} %get-tuple-element.81), channel_id=1, source_target_pairs={{0,3},{1,2},{2,1},{3,0},{4,7},{5,6},{6,5},{7,4},{8,11},{9,10},{10,... | collective-permute-start | bytes 2359304 | tf_op jit(solution)/shard_map/ppermute | solution.py:50
  66.7 16.4 %copy-start.16 = (bf16[512,768]{1,0:T(8,128)(2,1)}, bf16[512,768]{1,0:T(8,128)(2,1)S(1)}, u32[]{:S(2)}) copy-start(bf16[512,768]{1,0:T(8,128)(2,1)S(1)} %collective-permute-done.1) | copy-start | bytes 2359300
  66.7 32.0 %all-to-all-start.2 = ((bf16[8,64,768]{2,1,0:T(8,128)(2,1)}), bf16[8,64,768]{2,1,0:T(8,128)(2,1)S(1)}, u32[]{:S(2)}, u32[]{:S(2)}) async-start(bf16[8,64,768]{2,1,0:T(8,128)(2,1)} %bitcast.10), calls=%async_computation.2 | async-start | bytes 1572864 | tf_op jit(solution)/shard_map/all_to_all | solution.py:42
  83.1 31.1 %collective-permute-start.2 = (bf16[32,16,768]{2,1,0:T(8,128)(2,1)S(1)}, bf16[32,16,768]{2,1,0:T(8,128)(2,1)}, u32[]{:S(2)}, u32[]{:S(2)}) collective-permute-start(bf16[32,16,768]{2,1,0:T(8,128)(2,1)S(1)} %all-to-all-done.1.refs_0_), channel_id=1, source_target_pairs={{0,64},{64,0},{128,192},{192,128},{1,65},{65,1},{129,193},{193,129... | collective-permute-start | bytes 2359304 | tf_op jit(solution)/shard_map/ppermute | solution.py:50
  84.3 33.7 %collective-permute-start.3 = (bf16[32,16,768]{2,1,0:T(8,128)(2,1)S(1)}, bf16[32,16,768]{2,1,0:T(8,128)(2,1)}, u32[]{:S(2)}, u32[]{:S(2)}) collective-permute-start(bf16[32,16,768]{2,1,0:T(8,128)(2,1)S(1)} %all-to-all-done.1.refs_0_), channel_id=1, source_target_pairs={{0,128},{64,192},{128,0},{192,64},{1,129},{65,193},{129,1},{193,65... | collective-permute-start | bytes 2359304 | tf_op jit(solution)/shard_map/ppermute | solution.py:50
  86.7 35.6 %collective-permute-start.4 = (bf16[32,16,768]{2,1,0:T(8,128)(2,1)S(1)}, bf16[32,16,768]{2,1,0:T(8,128)(2,1)}, u32[]{:S(2)}, u32[]{:S(2)}) collective-permute-start(bf16[32,16,768]{2,1,0:T(8,128)(2,1)S(1)} %all-to-all-done.1.refs_0_), channel_id=1, source_target_pairs={{0,192},{64,128},{128,64},{192,0},{1,193},{65,129},{129,65},{193,1... | collective-permute-start | bytes 2359304 | tf_op jit(solution)/shard_map/ppermute | solution.py:50
  90.0 16.7 %collective-permute-start.11 = (bf16[512,768]{1,0:T(8,128)(2,1)}, bf16[512,768]{1,0:T(8,128)(2,1)}, u32[]{:S(2)}, u32[]{:S(2)}) collective-permute-start(bf16[512,768]{1,0:T(8,128)(2,1)} %get-tuple-element.83), channel_id=1, source_target_pairs={{0,2},{1,3},{2,0},{3,1},{4,6},{5,7},{6,4},{7,5},{8,10},{9,11},{10,... | collective-permute-start | bytes 2359304 | tf_op jit(solution)/shard_map/ppermute | solution.py:50
  98.7 31.6 %all-to-all-start.3 = ((bf16[8,64,768]{2,1,0:T(8,128)(2,1)}), bf16[8,64,768]{2,1,0:T(8,128)(2,1)S(1)}, u32[]{:S(2)}, u32[]{:S(2)}) async-start(bf16[8,64,768]{2,1,0:T(8,128)(2,1)} %bitcast.12), calls=%async_computation.3 | async-start | bytes 1572864 | tf_op jit(solution)/shard_map/all_to_all | solution.py:42
  105.3 22.5 %collective-permute-start.12 = (bf16[512,768]{1,0:T(8,128)(2,1)S(1)}, bf16[512,768]{1,0:T(8,128)(2,1)}, u32[]{:S(2)}, u32[]{:S(2)}) collective-permute-start(bf16[512,768]{1,0:T(8,128)(2,1)S(1)} %broadcast_select_fusion), channel_id=1, source_target_pairs={{0,2},{1,3},{2,0},{3,1},{4,6},{5,7},{6,4},{7,5},{8,10},{9,11},{10,... | collective-permute-start | bytes 2359304 | tf_op jit(solution)/shard_map/ppermute | solution.py:50
  106.7 30.2 %collective-permute-start.5 = (bf16[32,16,768]{2,1,0:T(8,128)(2,1)S(1)}, bf16[32,16,768]{2,1,0:T(8,128)(2,1)}, u32[]{:S(2)}, u32[]{:S(2)}) collective-permute-start(bf16[32,16,768]{2,1,0:T(8,128)(2,1)S(1)} %all-to-all-done.1.refs_0_), channel_id=1, source_target_pairs={{0,32},{32,0},{1,33},{33,1},{2,34},{34,2},{3,35},{35,3},{4,36},{36... | collective-permute-start | bytes 2359304 | tf_op jit(solution)/shard_map/ppermute | solution.py:50
  114.2 22.7 %collective-permute-start.6 = (bf16[32,16,768]{2,1,0:T(8,128)(2,1)}, bf16[32,16,768]{2,1,0:T(8,128)(2,1)}, u32[]{:S(2)}, u32[]{:S(2)}) collective-permute-start(bf16[32,16,768]{2,1,0:T(8,128)(2,1)} %collective-permute-done.2.refs_1_), channel_id=1, source_target_pairs={{0,32},{32,0},{1,33},{33,1},{2,34},{34,2},{3,35},{35,3},{4,36},{36... | collective-permute-start | bytes 2359304 | tf_op jit(solution)/shard_map/ppermute | solution.py:50
  118.0 18.9 %collective-permute-start.7 = (bf16[32,16,768]{2,1,0:T(8,128)(2,1)}, bf16[32,16,768]{2,1,0:T(8,128)(2,1)}, u32[]{:S(2)}, u32[]{:S(2)}) collective-permute-start(bf16[32,16,768]{2,1,0:T(8,128)(2,1)} %collective-permute-done.3.refs_2_), channel_id=1, source_target_pairs={{0,32},{32,0},{1,33},{33,1},{2,34},{34,2},{3,35},{35,3},{4,36},{36... | collective-permute-start | bytes 2359304 | tf_op jit(solution)/shard_map/ppermute | solution.py:50
  122.3 14.7 %collective-permute-start.8 = (bf16[32,16,768]{2,1,0:T(8,128)(2,1)}, bf16[32,16,768]{2,1,0:T(8,128)(2,1)}, u32[]{:S(2)}, u32[]{:S(2)}) collective-permute-start(bf16[32,16,768]{2,1,0:T(8,128)(2,1)} %collective-permute-done.4.refs_3_), channel_id=1, source_target_pairs={{0,32},{32,0},{1,33},{33,1},{2,34},{34,2},{3,35},{35,3},{4,36},{36... | collective-permute-start | bytes 2359304 | tf_op jit(solution)/shard_map/ppermute | solution.py:50
  130.3 12.3 %copy-start.3 = (bf16[8,64,768]{2,1,0:T(8,128)(2,1)}, bf16[8,64,768]{2,1,0:T(8,128)(2,1)S(1)}, u32[]{:S(2)}) copy-start(bf16[8,64,768]{2,1,0:T(8,128)(2,1)S(1)} %all-to-all-done.3) | copy-start | bytes 2359300
  130.3 30.2 %all-to-all-start.4 = ((bf16[8,64,768]{2,1,0:T(8,128)(2,1)}), bf16[8,64,768]{2,1,0:T(8,128)(2,1)S(1)}, u32[]{:S(2)}, u32[]{:S(2)}) async-start(bf16[8,64,768]{2,1,0:T(8,128)(2,1)} %bitcast.186), calls=%async_computation.4 | async-start | bytes 1572864 | tf_op jit(solution)/shard_map/all_to_all | solution.py:42
  142.6 9.4 %slice-start = ((s8[6291456]{0:T(1024)(128)(4,1)}), s8[4194304]{0:T(1024)(128)(4,1)S(1)}, s32[]{:S(2)}) async-start(s8[6291456]{0:T(1024)(128)(4,1)} %bitcast.184), calls=%async_computation.10 | async-start | bytes 8388608
  145.6 0.9 copy-start.2
  145.6 6.4 %slice-start.1 = ((s8[6291456]{0:T(1024)(128)(4,1)}), s8[2097152]{0:T(1024)(128)(4,1)S(1)}, s32[]{:S(2)}) async-start(s8[6291456]{0:T(1024)(128)(4,1)} %bitcast.184), calls=%async_computation.11 | async-start | bytes 4194304
  153.9 11.3 %copy-start.17 = (bf16[32,8,256]{2,1,0:T(8,128)(2,1)S(1)}, bf16[32,8,256]{2,1,0:T(8,128)(2,1)}, u32[]{:S(2)}) copy-start(bf16[32,8,256]{2,1,0:T(8,128)(2,1)} %get-tuple-element.97) | copy-start | bytes 393220
  160.5 0.9 copy-start.5
  161.4 25.2 %all-to-all-start.5 = ((bf16[8,64,768]{2,1,0:T(8,128)(2,1)}), bf16[8,64,768]{2,1,0:T(8,128)(2,1)S(1)}, u32[]{:S(2)}, u32[]{:S(2)}) async-start(bf16[8,64,768]{2,1,0:T(8,128)(2,1)} %bitcast.43), calls=%async_computation.5 | async-start | bytes 1572864 | tf_op jit(solution)/shard_map/all_to_all | solution.py:42
  167.5 3.7 %copy-start.14 = (bf16[32,4,2,8,768]{4,3,2,1,0:T(8,128)(2,1)}, bf16[32,4,2,8,768]{4,3,2,1,0:T(8,128)(2,1)S(1)}, u32[]{:S(2)}) copy-start(bf16[32,4,2,8,768]{4,3,2,1,0:T(8,128)(2,1)S(1)} %copy.40) | copy-start | bytes 9437188
  171.2 1.1 copy-start.4
  171.2 1.4 copy-start.6
  171.2 1.4 copy-start.9
  174.9 0.8 copy-start.7
  186.6 1.0 copy-start.8
  187.6 0.9 copy-start.10
  193.0 5.7 %collective-permute-start.17 = (bf16[4,4,128,384]{3,2,1,0:T(8,128)(2,1)}, bf16[4,4,128,384]{3,2,1,0:T(8,128)(2,1)S(1)}, u32[]{:S(2)}, u32[]{:S(2)}) collective-permute-start(bf16[4,4,128,384]{3,2,1,0:T(8,128)(2,1)} %get-tuple-element.64), channel_id=1, source_target_pairs={{0,32},{32,0},{1,33},{33,1},{2,34},{34,2},{3,35},{35,3},{4,36},{36... | collective-permute-start | bytes 4718600 | tf_op jit(solution)/shard_map/ppermute | solution.py:50
  198.7 5.5 %collective-permute-start.13 = (bf16[4,768,256]{2,1,0:T(8,128)(2,1)}, bf16[4,768,256]{2,1,0:T(8,128)(2,1)}, u32[]{:S(2)}, u32[]{:S(2)}) collective-permute-start(bf16[4,768,256]{2,1,0:T(8,128)(2,1)} %get-tuple-element.62), channel_id=1, source_target_pairs={{0,32},{32,0},{1,33},{33,1},{2,34},{34,2},{3,35},{35,3},{4,36},{36... | collective-permute-start | bytes 4718600 | tf_op jit(solution)/shard_map/ppermute | solution.py:50
  200.4 23.8 %all-to-all-start.6 = ((bf16[4,4,128,384]{3,2,1,0:T(8,128)(2,1)}), bf16[4,4,128,384]{3,2,1,0:T(8,128)(2,1)S(1)}, u32[]{:S(2)}, u32[]{:S(2)}) async-start(bf16[4,4,128,384]{3,2,1,0:T(8,128)(2,1)} %add_convert_fusion), calls=%async_computation.6 | async-start | bytes 3145728 | tf_op jit(solution)/shard_map/all_to_all | solution.py:42
  206.9 20.6 %copy-start.15 = (bf16[768,256]{1,0:T(8,128)(2,1)S(1)}, bf16[768,256]{1,0:T(8,128)(2,1)}, u32[]{:S(2)}) copy-start(bf16[768,256]{1,0:T(8,128)(2,1)} %get-tuple-element.65) | copy-start | bytes 1179652
  206.9 18.2 %collective-permute-start.14 = (bf16[768,256]{1,0:T(8,128)(2,1)}, bf16[768,256]{1,0:T(8,128)(2,1)S(1)}, u32[]{:S(2)}, u32[]{:S(2)}) collective-permute-start(bf16[768,256]{1,0:T(8,128)(2,1)} %get-tuple-element.79), channel_id=1, source_target_pairs={{0,64},{64,0},{128,192},{192,128},{1,65},{65,1},{129,193},{193,129... | collective-permute-start | bytes 1179656 | tf_op jit(solution)/shard_map/ppermute | solution.py:50
  206.9 18.2 %collective-permute-start.15 = (bf16[768,256]{1,0:T(8,128)(2,1)}, bf16[768,256]{1,0:T(8,128)(2,1)S(1)}, u32[]{:S(2)}, u32[]{:S(2)}) collective-permute-start(bf16[768,256]{1,0:T(8,128)(2,1)} %get-tuple-element.78), channel_id=1, source_target_pairs={{0,128},{64,192},{128,0},{192,64},{1,129},{65,193},{129,1},{193,65... | collective-permute-start | bytes 1179656 | tf_op jit(solution)/shard_map/ppermute | solution.py:50
  207.0 20.5 %collective-permute-start.16 = (bf16[768,256]{1,0:T(8,128)(2,1)}, bf16[768,256]{1,0:T(8,128)(2,1)S(1)}, u32[]{:S(2)}, u32[]{:S(2)}) collective-permute-start(bf16[768,256]{1,0:T(8,128)(2,1)} %get-tuple-element.77), channel_id=1, source_target_pairs={{0,192},{64,128},{128,64},{192,0},{1,193},{65,129},{129,65},{193,1... | collective-permute-start | bytes 1179656 | tf_op jit(solution)/shard_map/ppermute | solution.py:50
  227.7 7.6 %collective-permute-start.18 = (bf16[8,24,256]{2,1,0:T(8,128)(2,1)S(1)}, bf16[8,24,256]{2,1,0:T(8,128)(2,1)S(1)}, u32[]{:S(2)}, u32[]{:S(2)}) collective-permute-start(bf16[8,24,256]{2,1,0:T(8,128)(2,1)S(1)} %get-tuple-element.89), channel_id=1, source_target_pairs={{0,1},{1,0},{2,3},{3,2},{4,5},{5,4},{6,7},{7,6},{8,9},{9,8},{10,11... | collective-permute-start | bytes 294920 | tf_op jit(solution)/shard_map/ppermute | solution.py:50
  229.0 6.3 %collective-permute-start.19 = (bf16[8,24,256]{2,1,0:T(8,128)(2,1)S(1)}, bf16[8,24,256]{2,1,0:T(8,128)(2,1)S(1)}, u32[]{:S(2)}, u32[]{:S(2)}) collective-permute-start(bf16[8,24,256]{2,1,0:T(8,128)(2,1)S(1)} %get-tuple-element.91), channel_id=1, source_target_pairs={{0,2},{1,3},{2,0},{3,1},{4,6},{5,7},{6,4},{7,5},{8,10},{9,11},{10,... | collective-permute-start | bytes 294920 | tf_op jit(solution)/shard_map/ppermute | solution.py:50
  231.4 32.1 %copy-start.12 = (f32[128,1]{1,0:T(8,128)S(1)}, f32[128,1]{1,0:T(8,128)}, u32[]{:S(2)}) copy-start(f32[128,1]{1,0:T(8,128)} %copy-done.11) | copy-start | bytes 1540
  231.4 4.7 %collective-permute-start.20 = (bf16[8,24,256]{2,1,0:T(8,128)(2,1)S(1)}, bf16[8,24,256]{2,1,0:T(8,128)(2,1)S(1)}, u32[]{:S(2)}, u32[]{:S(2)}) collective-permute-start(bf16[8,24,256]{2,1,0:T(8,128)(2,1)S(1)} %get-tuple-element.90), channel_id=1, source_target_pairs={{0,3},{1,2},{2,1},{3,0},{4,7},{5,6},{6,5},{7,4},{8,11},{9,10},{10,... | collective-permute-start | bytes 294920 | tf_op jit(solution)/shard_map/ppermute | solution.py:50
  231.7 9.9 %all-to-all-start.7 = ((bf16[4,128,384]{2,1,0:T(8,128)(2,1)}), bf16[4,128,384]{2,1,0:T(8,128)(2,1)S(1)}, u32[]{:S(2)}, u32[]{:S(2)}) async-start(bf16[4,128,384]{2,1,0:T(8,128)(2,1)} %fusion.19), calls=%async_computation.7 | async-start | bytes 786432 | tf_op jit(solution)/shard_map/all_to_all | solution.py:42
  254.7 14.7 %all-to-all-start.9 = ((bf16[8,96,128]{2,1,0:T(8,128)(2,1)}), bf16[8,96,128]{2,1,0:T(8,128)(2,1)S(1)}, u32[]{:S(2)}, u32[]{:S(2)}) async-start(bf16[8,96,128]{2,1,0:T(8,128)(2,1)} %broadcast_in_dim.119), calls=%async_computation.9 | async-start | bytes 393216 | tf_op jit(solution)/shard_map/all_to_all | solution.py:42
  269.4 0.9 copy-start.1
  (3 other events, 2.1 us)
